TPU v7x, 32 devices: a whole 2x2x4 slice. The times are simulated.
32 devices in a mesh: wide: 16 (over z, y, x), narrow: 2 (over core).
Axes of the slice: x: 2, y: 2, z: 4, core: 2. Of those that a mesh axis runs over, the one named last changes fastest.
Arguments:
- panel: float32 [8, 1048576], P(None, ('wide', 'narrow')), may hold values from -0.25 to 0.25
- signs: int32 [1048576], P(('wide', 'narrow')), may hold values from -1 to 1, as said below
- samples: int32 [4096], P(('wide', 'narrow')), may hold values from 0 to 1048575, as said below
Outputs:
- sketch: float32 [8, 4096], P(None, ('wide', 'narrow'))
Inputs may be any that keep to these rules, and one draw needn't show every extreme that they name: `signs`: every entry is +1 or -1. `samples`: for every k, entries 128 * k to 128 * (k + 1) - 1 are distinct, increasing, and lie among rows 32768 * k to 32768 * (k + 1) - 1.
All inputs are finite; a program needn't handle non-finite values.
Results may differ from a plain program's by a relative error of at most 0.000071.
Values sent between devices are 32-bit elements; how exact they have to be, the bound alone decides.
No kernel may reach another device: no remote copies, remote signals or barrier semaphores. Data moves between devices by JAX's collectives and lax.ppermute only.
A program may use at most 64 MiB of HBM per device.

v0:
```python
import math

import jax
import jax.numpy as jnp
from jax import lax
from jax.sharding import PartitionSpec as P


def from_partner(block, axis, bit):
    count = lax.axis_size(axis)
    route = []
    for low in range(count):
        high = low | 1 << bit
        if high != low and high < count:
            route += [(low, high), (high, low)]
    return lax.ppermute(block, axis, route)


def parity_sign(left, right, nbits):
    count = (left & 0) + (right & 0)
    for level in range(nbits):
        count = count + (left >> level & 1) * (right >> level & 1)
    return (1 - 2 * (count % 2)).astype(jnp.float32)


def sylvester(order):
    nbits = max(order.bit_length() - 1, 0)
    index = jnp.arange(order, dtype=jnp.int32)
    return parity_sign(index[:, None], index[None, :], nbits)


def local_transform(values):
    cols, rows = values.shape
    inner = min(128, rows)
    outer = rows // inner
    blocks = values.reshape(cols, outer, inner)
    blocks = jnp.einsum("cab,bj->caj", blocks, sylvester(inner), precision=lax.Precision.HIGHEST)
    blocks = jnp.einsum("cab,ai->cib", blocks, sylvester(outer), precision=lax.Precision.HIGHEST)
    return blocks.reshape(cols, rows)


def narrow_section(values):
    n_narrow = lax.axis_size("narrow")
    narrow_bits = n_narrow.bit_length() - 1
    narrow_me = lax.axis_index("narrow")
    for level in range(narrow_bits):
        partner = from_partner(values, "narrow", level)
        upper = narrow_me >> level & 1 == 1
        values = jnp.where(upper, partner - values, values + partner)
    return values


def wide_section(values):
    cols, rows = values.shape
    n_wide = lax.axis_size("wide")
    arranged = values.reshape(cols, n_wide, rows // n_wide)
    received = lax.all_to_all(arranged, "wide", split_axis=1, concat_axis=1, tiled=True)
    return jnp.einsum("ij,cjp->cip", sylvester(n_wide), received, precision=lax.Precision.HIGHEST)


def per_device(panel, signs, samples):
    cols, rows = panel.shape
    samp = samples.shape[0]
    n_wide = lax.axis_size("wide")
    n_narrow = lax.axis_size("narrow")
    total_samples = samp * n_wide * n_narrow
    values = local_transform(panel * signs.astype(jnp.float32)[None, :])
    offsets = samples % rows
    mixed = wide_section(narrow_section(values))
    returned = lax.all_to_all(mixed, "wide", split_axis=1, concat_axis=1, tiled=True).reshape(
        cols, rows
    )
    chosen = jnp.take(returned, offsets, axis=1)
    return chosen * jnp.float32(1.0 / math.sqrt(total_samples))


def solution(mesh):
    in_specs = (P(None, ("wide", "narrow")), P(("wide", "narrow")), P(("wide", "narrow")))
    out_specs = P(None, ("wide", "narrow"))
    return jax.shard_map(
        per_device, mesh=mesh, in_specs=in_specs, out_specs=out_specs, check_vma=False
    )
```

profile of v0, /device:TPU:0, one launch (start us, length us, event | category | flops | bytes accessed | tf_op | source)
XLA Modules:
  0.0 91.0 jit_solution(12529319167097877301)
XLA Ops:
  0.0 0.0 copy-start
  0.1 0.9 %convert_element_type.13 = f32[32768]{0:T(1024)S(1)} convert(s32[32768]{0:T(1024)} %param.4) | non-fusion elementwise | flops 32768 | bytes 262144 | tf_op jit(solution)/shard_map/convert_element_type | solution.py:67
  1.0 1.3 %multiply_bitcast_fusion = f32[8,256,128]{2,0,1:T(8,128)S(1)} fusion(f32[8,32768]{1,0:T(8,128)} %param.3, f32[32768]{0:T(1024)S(1)} %convert_element_type.13), kind=kLoop, calls=%fused_computation.8 | loop fusion | flops 262144 | bytes 2228224 | tf_op jit(solution)/shard_map/reshape | solution.py:36
  2.3 1.1 %fusion = f32[8,256,128]{2,1,0:T(8,128)S(1)} fusion(f32[8,256,128]{2,0,1:T(8,128)S(1)} %multiply_bitcast_fusion, s32[128]{0:T(128)S(1)} %get-tuple-element.7, s32[128]{0:T(128)S(1)} %get-tuple-element.8, s32[128]{0:T(128)S(1)} %get-tuple-element.9, s32[128]{0:T(128)S(1)} %get-tuple-element.10, s32[128]{0:T(128)S(1)} %get-tuple-element.11, ...), kind=kOutput, calls=%fused_computation.4 | convolution fusion | flops 403095552 | bytes 2100736 | tf_op jit(solution)/shard_map/cab,bj->caj/dot_general | solution.py:37
  3.5 1.3 %convolution_bitcast_fusion.1 = f32[1,8,256,128]{3,2,1,0:T(8,128)S(1)} fusion(f32[8,256,128]{2,1,0:T(8,128)S(1)} %fusion, s32[256]{0:T(256)S(1)} %get-tuple-element.13, s32[256]{0:T(256)S(1)} %get-tuple-element.14, s32[256]{0:T(256)S(1)} %get-tuple-element.15, s32[256]{0:T(256)S(1)} %get-tuple-element.16, s32[256]{0:T(256)S(1)} %get-tuple-element.17, ...), kind=kOutput, calls=%fused_computation.2 | convolution fusion | flops 807206912 | bytes 2105344 | tf_op jit(solution)/shard_map/cab,ai->cib/dot_general | solution.py:38
  4.8 0.6 copy.19
  5.4 0.5 collective-permute-start
  5.9 2.3 %collective-permute-done = f32[8,32768]{1,0:T(8,128)S(1)} collective-permute-done((f32[8,32768]{1,0:T(8,128)S(1)}, f32[8,32768]{1,0:T(8,128)S(1)}, u32[]{:S(2)}, u32[]{:S(2)}) %collective-permute-start) | collective-permute-done | bytes 1048608 | tf_op jit(solution)/shard_map/ppermute | solution.py:16
  8.2 1.6 %add_select_fusion = f32[8,32768]{1,0:T(8,128)} fusion(f32[8,32768]{1,0:T(8,128)S(1)} %collective-permute-done, pred[]{:T(512)S(6)} %eq.11, f32[1,8,256,128]{3,2,1,0:T(8,128)S(1)} %convolution_bitcast_fusion.1), kind=kLoop, calls=%fused_computation.7 | loop fusion | flops 786432 | bytes 3145729 | tf_op jit(solution)/shard_map/jit(_where)/select_n | solution.py:49
  9.8 8.2 %all-to-all-start = ((f32[8,16,2048]{2,0,1:T(8,128)}), f32[8,16,2048]{2,0,1:T(8,128)S(1)}, u32[]{:S(2)}, u32[]{:S(2)}) async-start(f32[8,16,2048]{2,0,1:T(8,128)} %bitcast.4), calls=%async_computation | async-start | bytes 2097152 | tf_op jit(solution)/shard_map/all_to_all | solution.py:57
  18.1 24.6 %all-to-all-done = f32[8,16,2048]{2,0,1:T(8,128)S(1)} async-done(((f32[8,16,2048]{2,0,1:T(8,128)}), f32[8,16,2048]{2,0,1:T(8,128)S(1)}, u32[]{:S(2)}, u32[]{:S(2)}) %all-to-all-start) | async-done | bytes 1048608 | tf_op jit(solution)/shard_map/all_to_all | solution.py:57
  42.7 1.6 %convolution_bitcast_fusion = f32[8,16,2048]{2,1,0:T(8,128)S(1)} fusion(f32[8,16,2048]{2,0,1:T(8,128)S(1)} %all-to-all-done, s32[16]{0:T(128)S(1)} %get-tuple-element.21, s32[16]{0:T(128)S(1)} %get-tuple-element.22, s32[16]{0:T(128)S(1)} %get-tuple-element.23, s32[16]{0:T(128)S(1)} %get-tuple-element.24), kind=kOutput, calls=%fused_computation.1 | convolution fusion | flops 50337024 | bytes 2097408 | tf_op jit(solution)/shard_map/ij,cjp->cip/dot_general | solution.py:58
  44.3 1.6 %copy.7 = f32[8,16,2048]{2,0,1:T(8,128)} copy(f32[8,16,2048]{2,1,0:T(8,128)S(1)} %convolution_bitcast_fusion) | data formatting | bytes 2097152 | tf_op jit(solution)/shard_map/ij,cjp->cip/transpose | solution.py:58
  45.9 6.1 %all-to-all-start.1 = ((f32[8,16,2048]{2,0,1:T(8,128)}), f32[8,16,2048]{2,0,1:T(8,128)S(1)}, u32[]{:S(2)}, u32[]{:S(2)}) async-start(f32[8,16,2048]{2,0,1:T(8,128)} %copy.7), calls=%async_computation.1 | async-start | bytes 2097152 | tf_op jit(solution)/shard_map/all_to_all | solution.py:70
  52.0 0.0 copy-done
  52.1 23.3 %all-to-all-done.1 = f32[8,16,2048]{2,0,1:T(8,128)S(1)} async-done(((f32[8,16,2048]{2,0,1:T(8,128)}), f32[8,16,2048]{2,0,1:T(8,128)S(1)}, u32[]{:S(2)}, u32[]{:S(2)}) %all-to-all-start.1) | async-done | bytes 1048608 | tf_op jit(solution)/shard_map/all_to_all | solution.py:70
  75.3 8.5 %copy.8 = f32[8,16,2048]{0,2,1:T(8,128)} copy(f32[8,16,2048]{2,0,1:T(8,128)S(1)} %all-to-all-done.1) | data formatting | bytes 2097152 | tf_op jit(solution)/shard_map/all_to_all | solution.py:70
  83.8 6.4 %gather_fusion = f32[128,8]{1,0:T(8,128)S(1)} fusion(f32[8,32768]{0,1:T(8,128)} %bitcast.26, s32[1024]{0:T(1024)S(1)} %pad_clamp_fusion), kind=kCustom, calls=%fused_computation | custom fusion | bytes 8704 | tf_op jit(solution)/shard_map/jit(_take)/gather | solution.py:73
  90.2 0.1 multiply_bitcast_fusion.1
  90.3 0.7 copy.9
  (12 shorter events, 0.1 us)
Async XLA Ops:
  0.0 52.0 %copy-start = (s32[128]{0:T(128)S(1)}, s32[128]{0:T(128)}, u32[]{:S(2)}) copy-start(s32[128]{0:T(128)} %param.5) | copy-start | bytes 1540
  5.4 2.8 %collective-permute-start = (f32[8,32768]{1,0:T(8,128)S(1)}, f32[8,32768]{1,0:T(8,128)S(1)}, u32[]{:S(2)}, u32[]{:S(2)}) collective-permute-start(f32[8,32768]{1,0:T(8,128)S(1)} %bitcast.27), channel_id=1, source_target_pairs={{0,1},{1,0},{2,3},{3,2},{4,5},{5,4},{6,7},{7,6},{8,9},{9,8},{10,11... | collective-permute-start | bytes 3145736 | tf_op jit(solution)/shard_map/ppermute | solution.py:16
  9.8 32.8 %all-to-all-start = ((f32[8,16,2048]{2,0,1:T(8,128)}), f32[8,16,2048]{2,0,1:T(8,128)S(1)}, u32[]{:S(2)}, u32[]{:S(2)}) async-start(f32[8,16,2048]{2,0,1:T(8,128)} %bitcast.4), calls=%async_computation | async-start | bytes 2097152 | tf_op jit(solution)/shard_map/all_to_all | solution.py:57
  45.9 29.4 %all-to-all-start.1 = ((f32[8,16,2048]{2,0,1:T(8,128)}), f32[8,16,2048]{2,0,1:T(8,128)S(1)}, u32[]{:S(2)}, u32[]{:S(2)}) async-start(f32[8,16,2048]{2,0,1:T(8,128)} %copy.7), calls=%async_computation.1 | async-start | bytes 2097152 | tf_op jit(solution)/shard_map/all_to_all | solution.py:70
where the time goes:
time: 91.3 us; the launch traced here: 91 us
  waiting for transfers between devices  50.2 us (55%)
  local copies, waits for them, and re-layouts  17.7 us (19%)
  starting transfers between devices  14.9 us (16%)
  matrix products  4.08 us (4%)
  other arithmetic  4.01 us (4%)
    all_to_all x1, waiting for transfers between devices, wide_section(): lax.all_to_all(arranged, 'wide', split_axis=1, concat_axis=1, tiled=True)  24.6 us
    all_to_all x1, waiting for transfers between devices, per_device(): lax.all_to_all(mixed, 'wide', split_axis=1, concat_axis=1, tiled=True)  23.3 us
    all_to_all x1, local copies, waits for them, and re-layouts, per_device(): lax.all_to_all(mixed, 'wide', split_axis=1, concat_axis=1, tiled=True)  8.47 us
    all_to_all x1, starting transfers between devices, wide_section(): lax.all_to_all(arranged, 'wide', split_axis=1, concat_axis=1, tiled=True)  8.23 us
    gather x1, local copies, waits for them, and re-layouts, per_device(): chosen = jnp.take(returned, offsets, axis=1)  6.41 us
    all_to_all x1, starting transfers between devices, per_device(): lax.all_to_all(mixed, 'wide', split_axis=1, concat_axis=1, tiled=True)  6.1 us
    ppermute x1, waiting for transfers between devices, from_partner(): return lax.ppermute(block, axis, route)  2.29 us
  transfers between devices with their start and end apart: 3, of which 3 were waited for; matrix products, arithmetic and copies ran while one was open for 0% of the time, Pallas kernels for 0%

commit v1 on v0

v1 whole, which is shorter than its diff:
```python
import functools
import math

import jax
import jax.numpy as jnp
from jax import lax
from jax.experimental import pallas as pl
from jax.experimental.pallas import tpu as pltpu
from jax.sharding import PartitionSpec as P

LANES = 128
LOW = 256
AXES = ("wide", "narrow")
VMEM_LIMIT = 40 << 20


def vmem():
    return pl.BlockSpec(memory_space=pltpu.VMEM)


def parity(value):
    return bin(value).count("1") & 1


def hadamard_rows(order):
    row = lax.broadcasted_iota(jnp.int32, (order, order), 0)
    col = lax.broadcasted_iota(jnp.int32, (order, order), 1)
    bits = row & col
    shift = order.bit_length() // 2
    while shift:
        bits = bits ^ (bits >> shift)
        shift //= 2
    sign = (1 - 2 * (bits & 1)).astype(jnp.float32).astype(jnp.bfloat16)
    return jnp.concatenate([sign, sign], axis=0)


def two_parts(values):
    high = values.astype(jnp.bfloat16)
    low = (values - high.astype(jnp.float32)).astype(jnp.bfloat16)
    return jnp.concatenate([high, low], axis=1)


def butterfly(values):
    values = list(values)
    step = 1
    while step < len(values):
        for at in range(len(values)):
            if not at & step:
                first, second = values[at], values[at | step]
                values[at], values[at | step] = first + second, first - second
        step *= 2
    return values


def transform_kernel(outer, inner, mine_ref, other_ref, mine_signs_ref, other_signs_ref, even_ref, odd_ref, even_mid, odd_mid):
    core = lax.axis_index("narrow") & 1
    flip = (1 - 2 * core).astype(jnp.float32)
    cols = mine_ref.shape[0]
    tiles = LOW // LANES

    def load(group, tile):
        at = group * tiles + tile
        lanes = pl.ds(pl.multiple_of(at * LANES, LANES), LANES)
        mine_sign = mine_signs_ref[pl.ds(at, 1), :].astype(jnp.float32)
        other_sign = other_signs_ref[pl.ds(at, 1), :].astype(jnp.float32)
        mine = mine_ref[:, lanes] * mine_sign
        other = other_ref[:, lanes] * other_sign
        return other + flip * mine, mine - flip * other

    def first_pass(b, carry):
        for tile in range(tiles):
            pairs = [load(a * inner + b, tile) for a in range(outer)]
            for mid, values in ((even_mid, [p[0] for p in pairs]), (odd_mid, [p[1] for p in pairs])):
                for a, value in enumerate(butterfly(values)):
                    rows = pl.ds(pl.multiple_of((a * inner + b) * cols, cols), cols)
                    mid[rows, tile * LANES : (tile + 1) * LANES] = value
        return carry

    lax.fori_loop(0, inner, first_pass, 0)
    matrix = hadamard_rows(LOW)

    def second_pass(a, carry):
        rows = pl.ds(pl.multiple_of(a * inner * cols, inner * cols), inner * cols)
        for mid, out_ref in ((even_mid, even_ref), (odd_mid, odd_ref)):
            block = mid[rows, :]
            values = butterfly([block[b * cols : (b + 1) * cols] for b in range(inner)])
            block = two_parts(jnp.concatenate(values, axis=0))
            block = jnp.dot(block, matrix, preferred_element_type=jnp.float32)
            out_ref[rows, :] = two_parts(block)
        return carry

    lax.fori_loop(0, outer, second_pass, 0)


def transform(mine, other, mine_signs, other_signs):
    cols, rows = mine.shape
    groups = rows // LOW
    outer = 1 << (groups.bit_length() - 1) // 2
    inner = groups // outer
    shape = (groups * cols, 2 * LOW)
    return pl.pallas_call(
        functools.partial(transform_kernel, outer, inner),
        out_shape=[jax.ShapeDtypeStruct(shape, jnp.bfloat16)] * 2,
        in_specs=[vmem()] * 4,
        out_specs=[vmem()] * 2,
        scratch_shapes=[pltpu.VMEM((groups * cols, LOW), jnp.float32)] * 2,
        compiler_params=pltpu.CompilerParams(vmem_limit_bytes=VMEM_LIMIT),
        cost_estimate=pl.CostEstimate(flops=8 * cols * rows * LOW, bytes_accessed=20 * cols * rows, transcendentals=0),
        name="transform",
    )(mine, other, mine_signs.reshape(rows // LANES, LANES), other_signs.reshape(rows // LANES, LANES))


def gather_kernel(first, groups, cols, even_ref, odd_ref, offsets_ref, out_ref):
    count = offsets_ref.shape[0]
    offsets = offsets_ref[...]
    samp = offsets.shape[1]
    by_parity = [[t for t in range(count) if parity(first + t) == p] for p in range(2)]
    for table_ref, targets in zip((even_ref, odd_ref), by_parity):
        for at in range(0, len(targets), 2):
            pair = targets[at : at + 2]
            offset = jnp.concatenate([offsets[t : t + 1] for t in pair], axis=1)
            width = offset.shape[1]
            low = offset & (LOW - 1)
            high = jnp.broadcast_to(offset // LOW & (groups - 1), (cols, width))
            rows = lax.broadcasted_iota(jnp.int32, (LOW, width), 0)
            chosen = (rows == low).astype(jnp.float32).astype(jnp.bfloat16)
            chosen = jnp.concatenate([chosen, chosen], axis=0)
            picked = jnp.dot(table_ref[...], chosen, preferred_element_type=jnp.float32)
            sums = [jnp.zeros((cols, width), jnp.float32) for _ in range(2)]
            for g in range(groups):
                block = picked[g * cols : (g + 1) * cols]
                sums[g % 2] = jnp.where(high == g, block, sums[g % 2])
            total = sums[0] + sums[1]
            for i, t in enumerate(pair):
                out_ref[t] = total[:, i * samp : (i + 1) * samp]


def gather(first, cols, groups, even, odd, offsets):
    count, samp = offsets.shape
    return pl.pallas_call(
        functools.partial(gather_kernel, first, groups, cols),
        out_shape=jax.ShapeDtypeStruct((count, cols, samp), jnp.float32),
        in_specs=[vmem()] * 3,
        out_specs=vmem(),
        compiler_params=pltpu.CompilerParams(vmem_limit_bytes=VMEM_LIMIT),
        cost_estimate=pl.CostEstimate(
            flops=4 * groups * cols * LOW * count * samp, bytes_accessed=4 * groups * cols * LOW, transcendentals=0
        ),
        name="gather",
    )(even, odd, offsets)


def per_device(panel, signs, samples):
    cols, rows = panel.shape
    samp = samples.shape[0]
    n_wide = lax.axis_size("wide")
    n_narrow = lax.axis_size("narrow")
    wide_bits = n_wide.bit_length() - 1
    narrow_bits = n_narrow.bit_length() - 1
    n_all = n_wide * n_narrow
    wide_me = lax.axis_index("wide")
    narrow_me = lax.axis_index("narrow")

    def across(values, mask):
        return lax.ppermute(values, AXES, [(i, i ^ mask) for i in range(n_all)])

    asked = samples
    for bit in range(wide_bits):
        asked = jnp.concatenate([asked, across(asked, n_narrow << bit | 1)])
    asked = asked.reshape(n_wide, samp)

    for bit in range(1, narrow_bits):
        if bit == 1:
            panel = panel * signs.astype(jnp.float32)[None, :]
            signs = jnp.ones_like(signs)
        upper = narrow_me >> bit & 1 == 1
        partner = across(panel, 1 << bit)
        panel = jnp.where(upper, partner - panel, panel + partner)
    even, odd = transform(panel, across(panel, 1), signs, across(signs, 1))

    groups = rows // LOW
    half = n_wide // 2
    near = gather(0, cols, groups, even, odd, asked[:half])
    far = gather(half, cols, groups, even, odd, asked[half:])
    for bit in reversed(range(wide_bits)):
        sign = (1 - 2 * (wide_me >> bit & 1)).astype(jnp.float32)
        total = across(far, n_narrow << bit | 1) + sign * near
        near, far = total[: 1 << bit >> 1], total[1 << bit >> 1 :]
    return total[0] * jnp.float32(1.0 / math.sqrt(samp * n_all))


def solution(mesh):
    in_specs = (P(None, AXES), P(AXES), P(AXES))
    return jax.shard_map(per_device, mesh=mesh, in_specs=in_specs, out_specs=P(None, AXES), check_vma=False)
```

time: 91.3 us -> 34.3 us (0.38)
  waiting for transfers between devices: 50.2 us -> 10.9 us
  local copies, waits for them, and re-layouts: 17.7 us -> 2.85 us
  Pallas kernels: 0 us -> 5.55 us
  matrix products: 4.08 us -> 0 us
  other arithmetic: 4.01 us -> 0.63 us
    all_to_all x2 -> x0, waiting for transfers between devices: 47.9 us -> none  [the longest x1 24.6 us: wide_section(): lax.all_to_all(arranged, 'wide', split_axis=1, concat_axis=1, tiled=True)]
    all_to_all x2 -> x0, starting transfers between devices: 14.3 us -> none  [the longest x1 8.23 us: wide_section(): lax.all_to_all(arranged, 'wide', split_axis=1, concat_axis=1, tiled=True)]
    ppermute x1 -> x10, starting transfers between devices: 0.53 us -> 14.2 us  [across(): return lax.ppermute(values, AXES, [(i, i ^ mask) for i in range(n_all)])]
    ppermute x1 -> x10, waiting for transfers between devices: 2.29 us -> 10.9 us  [across(): return lax.ppermute(values, AXES, [(i, i ^ mask) for i in range(n_all)])]
    all_to_all x1 -> x0, local copies, waits for them, and re-layouts: 8.47 us -> none  [per_device(): lax.all_to_all(mixed, 'wide', split_axis=1, concat_axis=1, tiled=True)]
    gather x1 -> x0, local copies, waits for them, and re-layouts: 6.41 us -> none  [per_device(): chosen = jnp.take(returned, offsets, axis=1)]
    pallas_call x0 -> x3, Pallas kernels: none -> 5.55 us  [the longest x1 2.98 us: transform(): pl.pallas_call(functools.partial(transform_kernel, outer, inner), out_sha...]
    dot_general x3 -> x0, matrix products: 4.08 us -> none  [the longest x1 1.62 us: wide_section(): jnp.einsum('ij,cjp->cip', sylvester(n_wide), received, precision=lax.Prec...]
  transfers between devices with their start and end apart: 3 -> 10, of which waited for: 3 -> 7; matrix products, arithmetic and copies ran while one was open for 0% -> 0% of each run, Pallas kernels for 0% -> 12%
where the time goes in v1:
time: 34.3 us; the launch traced here: 34.1 us
  starting transfers between devices  14.2 us (41%)
  waiting for transfers between devices  10.9 us (32%)
  Pallas kernels  5.55 us (16%)
  local copies, waits for them, and re-layouts  2.85 us (8%)
  other arithmetic  0.63 us (2%)
    ppermute x10, starting transfers between devices, across(): return lax.ppermute(values, AXES, [(i, i ^ mask) for i in range(n_all)])  14.2 us
    ppermute x10, waiting for transfers between devices, across(): return lax.ppermute(values, AXES, [(i, i ^ mask) for i in range(n_all)])  10.9 us
    pallas_call x1, Pallas kernels, transform(): pl.pallas_call(functools.partial(transform_kernel, outer, inner), out_sha...  2.98 us
    unnamed x9, local copies, waits for them, and re-layouts  2.83 us
    pallas_call x2, Pallas kernels, gather(): pl.pallas_call(functools.partial(gather_kernel, first, groups, cols), out...  2.57 us
  transfers between devices with their start and end apart: 10, of which 7 were waited for; matrix products, arithmetic and copies ran while one was open for 0% of the time, Pallas kernels for 12%

profile of v1, /device:TPU:0, one launch (start us, length us, event | category | flops | bytes accessed | tf_op | source)
XLA Modules:
  0.0 34.1 jit_solution(6068500549404764851)
XLA Ops:
  0.0 0.5 %collective-permute-start = (f32[8,32768]{1,0:T(8,128)}, f32[8,32768]{1,0:T(8,128)S(1)}, u32[]{:S(2)}, u32[]{:S(2)}) collective-permute-start(f32[8,32768]{1,0:T(8,128)} %mine_ref.1), channel_id=1, source_target_pairs={{0,1},{1,0},{2,3},{3,2},{4,5},{5,4},{6,7},{7,6},{8,9},{9,8},{10,11... | collective-permute-start | bytes 3145736 | tf_op jit(solution)/shard_map/ppermute | solution.py:165
  0.5 0.1 collective-permute-start.1
  0.5 2.5 %collective-permute-start.2 = (s32[128]{0:T(128)}, s32[128]{0:T(128)S(1)}, u32[]{:S(2)}, u32[]{:S(2)}) collective-permute-start(s32[128]{0:T(128)} %param.5), channel_id=1, source_target_pairs={{0,3},{1,2},{2,1},{3,0},{4,7},{5,6},{6,5},{7,4},{8,11},{9,10},{10,... | collective-permute-start | bytes 1544 | tf_op jit(solution)/shard_map/ppermute | solution.py:165
  3.1 0.0 copy-start.2
  3.1 0.7 %copy-done.2 = s32[128]{0:T(128)S(1)} copy-done((s32[128]{0:T(128)S(1)}, s32[128]{0:T(128)}, u32[]{:S(2)}) %copy-start.2) | copy-done | bytes 536
  3.8 0.7 %collective-permute-done.2 = s32[128]{0:T(128)S(1)} collective-permute-done((s32[128]{0:T(128)}, s32[128]{0:T(128)S(1)}, u32[]{:S(2)}, u32[]{:S(2)}) %collective-permute-start.2) | collective-permute-done | bytes 544 | tf_op jit(solution)/shard_map/ppermute | solution.py:165
  4.5 1.7 %collective-permute-start.3 = (s32[256]{0:T(256)S(1)}, s32[256]{0:T(256)S(1)}, u32[]{:S(2)}, u32[]{:S(2)}) collective-permute-start(s32[256]{0:T(256)S(1)} %pad_add_fusion.1), channel_id=1, source_target_pairs={{0,5},{1,4},{2,7},{3,6},{4,1},{5,0},{6,3},{7,2},{8,13},{9,12},{10,... | collective-permute-start | bytes 3080 | tf_op jit(solution)/shard_map/ppermute | solution.py:165
  6.2 1.3 %collective-permute-done.3 = s32[256]{0:T(256)S(1)} collective-permute-done((s32[256]{0:T(256)S(1)}, s32[256]{0:T(256)S(1)}, u32[]{:S(2)}, u32[]{:S(2)}) %collective-permute-start.3) | collective-permute-done | bytes 1056 | tf_op jit(solution)/shard_map/ppermute | solution.py:165
  7.5 1.9 %collective-permute-start.4 = (s32[512]{0:T(512)S(1)}, s32[512]{0:T(512)S(1)}, u32[]{:S(2)}, u32[]{:S(2)}) collective-permute-start(s32[512]{0:T(512)S(1)} %pad_add_fusion), channel_id=1, source_target_pairs={{0,9},{1,8},{2,11},{3,10},{4,13},{5,12},{6,15},{7,14},{8,1},{9,0},... | collective-permute-start | bytes 6152 | tf_op jit(solution)/shard_map/ppermute | solution.py:165
  9.4 1.3 %collective-permute-done.4 = s32[512]{0:T(512)S(1)} collective-permute-done((s32[512]{0:T(512)S(1)}, s32[512]{0:T(512)S(1)}, u32[]{:S(2)}, u32[]{:S(2)}) %collective-permute-start.4) | collective-permute-done | bytes 2080 | tf_op jit(solution)/shard_map/ppermute | solution.py:165
  10.7 2.7 %collective-permute-start.5 = (s32[1024]{0:T(1024)S(1)}, s32[1024]{0:T(1024)S(1)}, u32[]{:S(2)}, u32[]{:S(2)}) collective-permute-start(s32[1024]{0:T(1024)S(1)} %constant_dynamic-update-slice_fusion), channel_id=1, source_target_pairs={{0,17},{1,16},{2,19},{3,18},{4,21},{5,20},{6,23},{7,22},{8,25},{9,... | collective-permute-start | bytes 12296 | tf_op jit(solution)/shard_map/ppermute | solution.py:165
  13.4 0.0 collective-permute-done.1
  13.4 0.0 collective-permute-done.other_ref
  13.4 0.0 copy-start
  13.4 1.2 %copy-done = f32[8,32768]{1,0:T(8,128)S(1)} copy-done((f32[8,32768]{1,0:T(8,128)S(1)}, f32[8,32768]{1,0:T(8,128)}, u32[]{:S(2)}) %copy-start) | copy-done | bytes 1048600
  14.6 0.0 copy-start.1
  14.6 0.9 %copy-done.1 = s32[32768]{0:T(1024)S(1)} copy-done((s32[32768]{0:T(1024)S(1)}, s32[32768]{0:T(1024)}, u32[]{:S(2)}) %copy-start.1) | copy-done | bytes 131096
  15.5 3.0 %transform.1 = (bf16[1024,512]{1,0:T(8,128)(2,1)S(1)}, bf16[1024,512]{1,0:T(8,128)(2,1)S(1)}) custom-call(f32[8,32768]{1,0:T(8,128)S(1)} %copy-done, f32[8,32768]{1,0:T(8,128)S(1)} %collective-permute-done.other_ref, s32[256,128]{1,0:T(8,128)S(1)} %bitcast.6, s32[256,128]{1,0:T(8,128)S(1)} %bitcast.7), custom_call_target="tpu_custom_call" | custom-call | flops 536870912 | bytes 5242880 | tf_op jit(solution)/shard_map/transform/pallas_call | solution.py:101
  18.5 0.0 collective-permute-done.5
  18.5 1.3 %gather.2 = f32[8,8,128]{2,1,0:T(8,128)S(1)} custom-call(bf16[1024,512]{1,0:T(8,128)(2,1)S(1)} %get-tuple-element.7.even_ref, bf16[1024,512]{1,0:T(8,128)(2,1)S(1)} %get-tuple-element.8.odd_ref, s32[8,128]{1,0:T(8,128)S(1)} %bitcast.8), custom_call_target="tpu_custom_call" | custom-call | flops 1073741824 | bytes 1048576 | tf_op jit(solution)/shard_map/gather/pallas_call | solution.py:140
  19.8 0.1 collective-permute-start.6
  19.9 1.3 %gather.3 = f32[8,8,128]{2,1,0:T(8,128)S(1)} custom-call(bf16[1024,512]{1,0:T(8,128)(2,1)S(1)} %get-tuple-element.7.even_ref, bf16[1024,512]{1,0:T(8,128)(2,1)S(1)} %get-tuple-element.8.odd_ref, s32[8,128]{1,0:T(8,128)S(1)} %bitcast.9), custom_call_target="tpu_custom_call" | custom-call | flops 1073741824 | bytes 1048576 | tf_op jit(solution)/shard_map/gather/pallas_call | solution.py:140
  21.2 2.9 %collective-permute-done.6 = f32[8,8,128]{2,1,0:T(8,128)S(1)} collective-permute-done((f32[8,8,128]{2,1,0:T(8,128)S(1)}, f32[8,8,128]{2,1,0:T(8,128)S(1)}, u32[]{:S(2)}, u32[]{:S(2)}) %collective-permute-start.6) | collective-permute-done | bytes 32800 | tf_op jit(solution)/shard_map/ppermute | solution.py:165
  24.1 1.6 %collective-permute-start.7 = (f32[4,8,128]{2,1,0:T(8,128)S(1)}, f32[4,8,128]{2,1,0:T(8,128)S(1)}, u32[]{:S(2)}, u32[]{:S(2)}) collective-permute-start(f32[4,8,128]{2,1,0:T(8,128)S(1)} %slice.39), channel_id=1, source_target_pairs={{0,9},{1,8},{2,11},{3,10},{4,13},{5,12},{6,15},{7,14},{8,1},{9,0},... | collective-permute-start | bytes 49160 | tf_op jit(solution)/shard_map/ppermute | solution.py:165
  25.8 1.6 %collective-permute-done.7 = f32[4,8,128]{2,1,0:T(8,128)S(1)} collective-permute-done((f32[4,8,128]{2,1,0:T(8,128)S(1)}, f32[4,8,128]{2,1,0:T(8,128)S(1)}, u32[]{:S(2)}, u32[]{:S(2)}) %collective-permute-start.7) | collective-permute-done | bytes 16416 | tf_op jit(solution)/shard_map/ppermute | solution.py:165
  27.4 1.6 %collective-permute-start.8 = (f32[2,8,128]{2,1,0:T(8,128)S(1)}, f32[2,8,128]{2,1,0:T(8,128)S(1)}, u32[]{:S(2)}, u32[]{:S(2)}) collective-permute-start(f32[2,8,128]{2,1,0:T(8,128)S(1)} %slice.41), channel_id=1, source_target_pairs={{0,5},{1,4},{2,7},{3,6},{4,1},{5,0},{6,3},{7,2},{8,13},{9,12},{10,... | collective-permute-start | bytes 24584 | tf_op jit(solution)/shard_map/ppermute | solution.py:165
  28.9 1.5 %collective-permute-done.8 = f32[2,8,128]{2,1,0:T(8,128)S(1)} collective-permute-done((f32[2,8,128]{2,1,0:T(8,128)S(1)}, f32[2,8,128]{2,1,0:T(8,128)S(1)}, u32[]{:S(2)}, u32[]{:S(2)}) %collective-permute-start.8) | collective-permute-done | bytes 8224 | tf_op jit(solution)/shard_map/ppermute | solution.py:165
  30.5 1.5 %collective-permute-start.9 = (f32[1,8,128]{2,1,0:T(8,128)S(1)}, f32[1,8,128]{2,1,0:T(8,128)S(1)}, u32[]{:S(2)}, u32[]{:S(2)}) collective-permute-start(f32[1,8,128]{2,1,0:T(8,128)S(1)} %slice.43), channel_id=1, source_target_pairs={{0,3},{1,2},{2,1},{3,0},{4,7},{5,6},{6,5},{7,4},{8,11},{9,10},{10,... | collective-permute-start | bytes 12296 | tf_op jit(solution)/shard_map/ppermute | solution.py:165
  32.0 1.5 %collective-permute-done.9 = f32[1,8,128]{2,1,0:T(8,128)S(1)} collective-permute-done((f32[1,8,128]{2,1,0:T(8,128)S(1)}, f32[1,8,128]{2,1,0:T(8,128)S(1)}, u32[]{:S(2)}, u32[]{:S(2)}) %collective-permute-start.9) | collective-permute-done | bytes 4128 | tf_op jit(solution)/shard_map/ppermute | solution.py:165
  33.5 0.6 %fusion.4 = f32[8,128]{1,0:T(8,128)} fusion(f32[1,8,128]{2,1,0:T(8,128)S(1)} %collective-permute-done.9, f32[2,8,128]{2,1,0:T(8,128)S(1)} %fusion.1, f32[]{:T(128)S(6)} %convert_element_type.15), kind=kLoop, calls=%fused_computation.8 | loop fusion | flops 3072 | bytes 12292 | tf_op jit(solution)/shard_map/mul | solution.py:189
  (13 shorter events, 0.1 us)
Async XLA Ops:
  0.0 13.4 %collective-permute-start = (f32[8,32768]{1,0:T(8,128)}, f32[8,32768]{1,0:T(8,128)S(1)}, u32[]{:S(2)}, u32[]{:S(2)}) collective-permute-start(f32[8,32768]{1,0:T(8,128)} %mine_ref.1), channel_id=1, source_target_pairs={{0,1},{1,0},{2,3},{3,2},{4,5},{5,4},{6,7},{7,6},{8,9},{9,8},{10,11... | collective-permute-start | bytes 3145736 | tf_op jit(solution)/shard_map/ppermute | solution.py:165
  0.5 12.9 %collective-permute-start.1 = (s32[32768]{0:T(1024)}, s32[32768]{0:T(1024)S(1)}, u32[]{:S(2)}, u32[]{:S(2)}) collective-permute-start(s32[32768]{0:T(1024)} %param.4), channel_id=1, source_target_pairs={{0,1},{1,0},{2,3},{3,2},{4,5},{5,4},{6,7},{7,6},{8,9},{9,8},{10,11... | collective-permute-start | bytes 393224 | tf_op jit(solution)/shard_map/ppermute | solution.py:165
  0.5 4.0 %collective-permute-start.2 = (s32[128]{0:T(128)}, s32[128]{0:T(128)S(1)}, u32[]{:S(2)}, u32[]{:S(2)}) collective-permute-start(s32[128]{0:T(128)} %param.5), channel_id=1, source_target_pairs={{0,3},{1,2},{2,1},{3,0},{4,7},{5,6},{6,5},{7,4},{8,11},{9,10},{10,... | collective-permute-start | bytes 1544 | tf_op jit(solution)/shard_map/ppermute | solution.py:165
  3.1 0.7 %copy-start.2 = (s32[128]{0:T(128)S(1)}, s32[128]{0:T(128)}, u32[]{:S(2)}) copy-start(s32[128]{0:T(128)} %param.5) | copy-start | bytes 1540
  4.5 3.0 %collective-permute-start.3 = (s32[256]{0:T(256)S(1)}, s32[256]{0:T(256)S(1)}, u32[]{:S(2)}, u32[]{:S(2)}) collective-permute-start(s32[256]{0:T(256)S(1)} %pad_add_fusion.1), channel_id=1, source_target_pairs={{0,5},{1,4},{2,7},{3,6},{4,1},{5,0},{6,3},{7,2},{8,13},{9,12},{10,... | collective-permute-start | bytes 3080 | tf_op jit(solution)/shard_map/ppermute | solution.py:165
  7.5 3.2 %collective-permute-start.4 = (s32[512]{0:T(512)S(1)}, s32[512]{0:T(512)S(1)}, u32[]{:S(2)}, u32[]{:S(2)}) collective-permute-start(s32[512]{0:T(512)S(1)} %pad_add_fusion), channel_id=1, source_target_pairs={{0,9},{1,8},{2,11},{3,10},{4,13},{5,12},{6,15},{7,14},{8,1},{9,0},... | collective-permute-start | bytes 6152 | tf_op jit(solution)/shard_map/ppermute | solution.py:165
  10.7 7.8 %collective-permute-start.5 = (s32[1024]{0:T(1024)S(1)}, s32[1024]{0:T(1024)S(1)}, u32[]{:S(2)}, u32[]{:S(2)}) collective-permute-start(s32[1024]{0:T(1024)S(1)} %constant_dynamic-update-slice_fusion), channel_id=1, source_target_pairs={{0,17},{1,16},{2,19},{3,18},{4,21},{5,20},{6,23},{7,22},{8,25},{9,... | collective-permute-start | bytes 12296 | tf_op jit(solution)/shard_map/ppermute | solution.py:165
  13.4 1.2 %copy-start = (f32[8,32768]{1,0:T(8,128)S(1)}, f32[8,32768]{1,0:T(8,128)}, u32[]{:S(2)}) copy-start(f32[8,32768]{1,0:T(8,128)} %mine_ref.1) | copy-start | bytes 3145732
  14.6 0.9 %copy-start.1 = (s32[32768]{0:T(1024)S(1)}, s32[32768]{0:T(1024)}, u32[]{:S(2)}) copy-start(s32[32768]{0:T(1024)} %param.4) | copy-start | bytes 393220
  19.8 4.3 %collective-permute-start.6 = (f32[8,8,128]{2,1,0:T(8,128)S(1)}, f32[8,8,128]{2,1,0:T(8,128)S(1)}, u32[]{:S(2)}, u32[]{:S(2)}) collective-permute-start(f32[8,8,128]{2,1,0:T(8,128)S(1)} %gather.2), channel_id=1, source_target_pairs={{0,17},{1,16},{2,19},{3,18},{4,21},{5,20},{6,23},{7,22},{8,25},{9,... | collective-permute-start | bytes 98312 | tf_op jit(solution)/shard_map/ppermute | solution.py:165
  24.1 3.2 %collective-permute-start.7 = (f32[4,8,128]{2,1,0:T(8,128)S(1)}, f32[4,8,128]{2,1,0:T(8,128)S(1)}, u32[]{:S(2)}, u32[]{:S(2)}) collective-permute-start(f32[4,8,128]{2,1,0:T(8,128)S(1)} %slice.39), channel_id=1, source_target_pairs={{0,9},{1,8},{2,11},{3,10},{4,13},{5,12},{6,15},{7,14},{8,1},{9,0},... | collective-permute-start | bytes 49160 | tf_op jit(solution)/shard_map/ppermute | solution.py:165
  27.4 3.1 %collective-permute-start.8 = (f32[2,8,128]{2,1,0:T(8,128)S(1)}, f32[2,8,128]{2,1,0:T(8,128)S(1)}, u32[]{:S(2)}, u32[]{:S(2)}) collective-permute-start(f32[2,8,128]{2,1,0:T(8,128)S(1)} %slice.41), channel_id=1, source_target_pairs={{0,5},{1,4},{2,7},{3,6},{4,1},{5,0},{6,3},{7,2},{8,13},{9,12},{10,... | collective-permute-start | bytes 24584 | tf_op jit(solution)/shard_map/ppermute | solution.py:165
  30.5 3.0 %collective-permute-start.9 = (f32[1,8,128]{2,1,0:T(8,128)S(1)}, f32[1,8,128]{2,1,0:T(8,128)S(1)}, u32[]{:S(2)}, u32[]{:S(2)}) collective-permute-start(f32[1,8,128]{2,1,0:T(8,128)S(1)} %slice.43), channel_id=1, source_target_pairs={{0,3},{1,2},{2,1},{3,0},{4,7},{5,6},{6,5},{7,4},{8,11},{9,10},{10,... | collective-permute-start | bytes 12296 | tf_op jit(solution)/shard_map/ppermute | solution.py:165

commit v2 on v1

--- a/solution.py
+++ b/solution.py
@@ -52,62 +52,122 @@
     return values
 
 
-def transform_kernel(outer, inner, mine_ref, other_ref, mine_signs_ref, other_signs_ref, even_ref, odd_ref, even_mid, odd_mid):
+def first_pass(outer, inner, values_ref, signs_ref, mid, a):
+    cols = values_ref.shape[0]
+    tiles = LOW // LANES
+    for tile in range(tiles):
+        values = []
+        for b in range(inner):
+            at = (a * inner + b) * tiles + tile
+            lanes = pl.ds(pl.multiple_of(at * LANES, LANES), LANES)
+            values.append(values_ref[:, lanes] * signs_ref[pl.ds(at, 1), :].astype(jnp.float32))
+        for b, value in enumerate(butterfly(values)):
+            rows = pl.ds(pl.multiple_of((a * inner + b) * cols, cols), cols)
+            mid[rows, tile * LANES : (tile + 1) * LANES] = value
+
+
+def second_pass(outer, inner, cols, mid, parts):
+    def step(b, carry):
+        values = [mid[pl.ds(pl.multiple_of((a * inner + b) * cols, cols), cols), :] for a in range(outer)]
+        block = two_parts(jnp.concatenate(butterfly(values), axis=0))
+        parts[pl.ds(pl.multiple_of(b * outer * cols, outer * cols), outer * cols), :] = block
+        return carry
+
+    lax.fori_loop(0, inner, step, 0)
+
+
+def own_kernel(outer, inner, values_hbm, signs_hbm, samples_ref, out_ref, list_ref, values_ref, signs_ref, mid, parts, sems):
+    cols, rows = values_hbm.shape
+    block = rows // outer
+    signs_copy = pltpu.make_async_copy(signs_hbm, signs_ref, sems.at[outer])
+    copies = [
+        pltpu.make_async_copy(
+            values_hbm.at[:, pl.ds(a * block, block)], values_ref.at[:, pl.ds(a * block, block)], sems.at[a]
+        )
+        for a in range(outer)
+    ]
+    signs_copy.start()
+    for copy in copies:
+        copy.start()
+    list_ref[...] = samples_ref[...]
+    matrix = hadamard_rows(LOW)
+    signs_copy.wait()
+    for a, copy in enumerate(copies):
+        copy.wait()
+        first_pass(outer, inner, values_ref, signs_ref, mid, a)
+    second_pass(outer, inner, cols, mid, parts)
+    out_ref[...] = jnp.dot(parts[...], matrix, preferred_element_type=jnp.float32)
+
+
+def other_kernel(outer, inner, values_ref, signs_ref, mine_ref, even_ref, odd_ref, mid, parts):
+    cols = values_ref.shape[0]
+
+    def step(a, carry):
+        first_pass(outer, inner, values_ref, signs_ref, mid, a)
+        return carry
+
+    lax.fori_loop(0, outer, step, 0)
+    second_pass(outer, inner, cols, mid, parts)
+    other = jnp.dot(parts[...], hadamard_rows(LOW), preferred_element_type=jnp.float32)
     core = lax.axis_index("narrow") & 1
     flip = (1 - 2 * core).astype(jnp.float32)
-    cols = mine_ref.shape[0]
-    tiles = LOW // LANES
-
-    def load(group, tile):
-        at = group * tiles + tile
-        lanes = pl.ds(pl.multiple_of(at * LANES, LANES), LANES)
-        mine_sign = mine_signs_ref[pl.ds(at, 1), :].astype(jnp.float32)
-        other_sign = other_signs_ref[pl.ds(at, 1), :].astype(jnp.float32)
-        mine = mine_ref[:, lanes] * mine_sign
-        other = other_ref[:, lanes] * other_sign
-        return other + flip * mine, mine - flip * other
-
-    def first_pass(b, carry):
-        for tile in range(tiles):
-            pairs = [load(a * inner + b, tile) for a in range(outer)]
-            for mid, values in ((even_mid, [p[0] for p in pairs]), (odd_mid, [p[1] for p in pairs])):
-                for a, value in enumerate(butterfly(values)):
-                    rows = pl.ds(pl.multiple_of((a * inner + b) * cols, cols), cols)
-                    mid[rows, tile * LANES : (tile + 1) * LANES] = value
-        return carry
-
-    lax.fori_loop(0, inner, first_pass, 0)
-    matrix = hadamard_rows(LOW)
-
-    def second_pass(a, carry):
-        rows = pl.ds(pl.multiple_of(a * inner * cols, inner * cols), inner * cols)
-        for mid, out_ref in ((even_mid, even_ref), (odd_mid, odd_ref)):
-            block = mid[rows, :]
-            values = butterfly([block[b * cols : (b + 1) * cols] for b in range(inner)])
-            block = two_parts(jnp.concatenate(values, axis=0))
-            block = jnp.dot(block, matrix, preferred_element_type=jnp.float32)
-            out_ref[rows, :] = two_parts(block)
-        return carry
-
-    lax.fori_loop(0, outer, second_pass, 0)
-
-
-def transform(mine, other, mine_signs, other_signs):
-    cols, rows = mine.shape
+    mine = mine_ref[...]
+    even_ref[...] = two_parts(other + flip * mine)
+    odd_ref[...] = two_parts(mine - flip * other)
+
+
+def split_groups(groups):
+    outer = 1 << (groups.bit_length() - 1) // 2
+    return outer, groups // outer
+
+
+def transform_own(values, signs, samples):
+    cols, rows = values.shape
     groups = rows // LOW
-    outer = 1 << (groups.bit_length() - 1) // 2
-    inner = groups // outer
-    shape = (groups * cols, 2 * LOW)
+    outer, inner = split_groups(groups)
+    hbm = pl.BlockSpec(memory_space=pltpu.HBM)
     return pl.pallas_call(
-        functools.partial(transform_kernel, outer, inner),
-        out_shape=[jax.ShapeDtypeStruct(shape, jnp.bfloat16)] * 2,
-        in_specs=[vmem()] * 4,
+        functools.partial(own_kernel, outer, inner),
+        out_shape=[
+            jax.ShapeDtypeStruct((groups * cols, LOW), jnp.float32),
+            jax.ShapeDtypeStruct(samples.shape, samples.dtype),
+        ],
+        in_specs=[hbm, hbm, vmem()],
         out_specs=[vmem()] * 2,
-        scratch_shapes=[pltpu.VMEM((groups * cols, LOW), jnp.float32)] * 2,
+        scratch_shapes=[
+            pltpu.VMEM(values.shape, jnp.float32),
+            pltpu.VMEM((rows // LANES, LANES), jnp.int32),
+            pltpu.VMEM((groups * cols, LOW), jnp.float32),
+            pltpu.VMEM((groups * cols, 2 * LOW), jnp.bfloat16),
+            pltpu.SemaphoreType.DMA((outer + 1,)),
+        ],
         compiler_params=pltpu.CompilerParams(vmem_limit_bytes=VMEM_LIMIT),
-        cost_estimate=pl.CostEstimate(flops=8 * cols * rows * LOW, bytes_accessed=20 * cols * rows, transcendentals=0),
-        name="transform",
-    )(mine, other, mine_signs.reshape(rows // LANES, LANES), other_signs.reshape(rows // LANES, LANES))
+        cost_estimate=pl.CostEstimate(flops=4 * cols * rows * LOW, bytes_accessed=10 * cols * rows, transcendentals=0),
+        name="transform_own",
+    )(
+        pltpu.with_memory_space_constraint(values, pltpu.HBM),
+        pltpu.with_memory_space_constraint(signs.reshape(rows // LANES, LANES), pltpu.HBM),
+        samples,
+    )
+
+
+def transform_other(values, signs, mine):
+    cols, rows = values.shape
+    groups = rows // LOW
+    outer, inner = split_groups(groups)
+    return pl.pallas_call(
+        functools.partial(other_kernel, outer, inner),
+        out_shape=[jax.ShapeDtypeStruct((groups * cols, 2 * LOW), jnp.bfloat16)] * 2,
+        in_specs=[vmem()] * 3,
+        out_specs=[vmem()] * 2,
+        scratch_shapes=[
+            pltpu.VMEM((groups * cols, LOW), jnp.float32),
+            pltpu.VMEM((groups * cols, 2 * LOW), jnp.bfloat16),
+        ],
+        compiler_params=pltpu.CompilerParams(vmem_limit_bytes=VMEM_LIMIT),
+        cost_estimate=pl.CostEstimate(flops=4 * cols * rows * LOW, bytes_accessed=10 * cols * rows, transcendentals=0),
+        name="transform_other",
+    )(values, signs.reshape(rows // LANES, LANES), mine)
 
 
 def gather_kernel(first, groups, cols, even_ref, odd_ref, offsets_ref, out_ref):
@@ -127,9 +187,10 @@
             chosen = jnp.concatenate([chosen, chosen], axis=0)
             picked = jnp.dot(table_ref[...], chosen, preferred_element_type=jnp.float32)
             sums = [jnp.zeros((cols, width), jnp.float32) for _ in range(2)]
+            outer, inner = split_groups(groups)
             for g in range(groups):
                 block = picked[g * cols : (g + 1) * cols]
-                sums[g % 2] = jnp.where(high == g, block, sums[g % 2])
+                sums[g % 2] = jnp.where(high == g % outer * inner + g // outer, block, sums[g % 2])
             total = sums[0] + sums[1]
             for i, t in enumerate(pair):
                 out_ref[t] = total[:, i * samp : (i + 1) * samp]
@@ -164,11 +225,6 @@
     def across(values, mask):
         return lax.ppermute(values, AXES, [(i, i ^ mask) for i in range(n_all)])
 
-    asked = samples
-    for bit in range(wide_bits):
-        asked = jnp.concatenate([asked, across(asked, n_narrow << bit | 1)])
-    asked = asked.reshape(n_wide, samp)
-
     for bit in range(1, narrow_bits):
         if bit == 1:
             panel = panel * signs.astype(jnp.float32)[None, :]
@@ -176,11 +232,26 @@
         upper = narrow_me >> bit & 1 == 1
         partner = across(panel, 1 << bit)
         panel = jnp.where(upper, partner - panel, panel + partner)
-    even, odd = transform(panel, across(panel, 1), signs, across(signs, 1))
 
     groups = rows // LOW
     half = n_wide // 2
-    near = gather(0, cols, groups, even, odd, asked[:half])
+    arrived = across(samples, n_narrow | 1)
+    other, other_signs = across(panel, 1), across(signs, 1)
+    mine, listed = transform_own(panel, signs, samples)
+    arrived, mine, listed, other, other_signs = lax.optimization_barrier((arrived, mine, listed, other, other_signs))
+    asked = jnp.concatenate([listed, arrived])
+    for bit in range(1, wide_bits):
+        if bit == 2:
+            asked, even, odd = lax.optimization_barrier((asked, even, odd))
+        if bit == wide_bits - 1:
+            near = gather(0, cols, groups, even, odd, asked.reshape(half, samp))
+        arrived = across(asked, n_narrow << bit | 1)
+        if bit == 1:
+            even, odd = transform_other(other, other_signs, mine)
+        asked = jnp.concatenate([asked, arrived])
+    asked, near = lax.optimization_barrier((asked, near))
+    asked = asked.reshape(n_wide, samp)
+
     far = gather(half, cols, groups, even, odd, asked[half:])
     for bit in reversed(range(wide_bits)):
         sign = (1 - 2 * (wide_me >> bit & 1)).astype(jnp.float32)

time: 34.3 us -> 31.4 us (0.915)
  local copies, waits for them, and re-layouts: 2.85 us -> 0.02 us
  waiting for transfers between devices: 10.9 us -> 9.32 us
  Pallas kernels: 5.55 us -> 6.37 us
  starting transfers between devices: 14.2 us -> 14.8 us
    unnamed x9 -> x2, local copies, waits for them, and re-layouts: 2.83 us -> 0.01 us
    ppermute x10, waiting for transfers between devices: 10.9 us -> 9.32 us  [across(): return lax.ppermute(values, AXES, [(i, i ^ mask) for i in range(n_all)])]
    pallas_call x1 -> x2, Pallas kernels: 2.98 us -> 3.8 us  [the longest x1 2.22 us: transform_own(): pl.pallas_call(functools.partial(own_kernel, outer, inner), out_shape=[ja...]
    ppermute x10, starting transfers between devices: 14.2 us -> 14.8 us  [across(): return lax.ppermute(values, AXES, [(i, i ^ mask) for i in range(n_all)])]
  transfers between devices with their start and end apart: 10 -> 10, of which waited for: 7 -> 6; matrix products, arithmetic and copies ran while one was open for 0% -> 0% of each run, Pallas kernels for 12% -> 16%
where the time goes in v2:
time: 31.4 us; the launch traced here: 31.2 us
  starting transfers between devices  14.8 us (47%)
  waiting for transfers between devices  9.32 us (30%)
  Pallas kernels  6.37 us (20%)
  other arithmetic  0.65 us (2%)
    ppermute x10, starting transfers between devices, across(): return lax.ppermute(values, AXES, [(i, i ^ mask) for i in range(n_all)])  14.8 us
    ppermute x10, waiting for transfers between devices, across(): return lax.ppermute(values, AXES, [(i, i ^ mask) for i in range(n_all)])  9.32 us
    pallas_call x2, Pallas kernels, gather(): pl.pallas_call(functools.partial(gather_kernel, first, groups, cols), out...  2.58 us
    pallas_call x1, Pallas kernels, transform_own(): pl.pallas_call(functools.partial(own_kernel, outer, inner), out_shape=[ja...  2.22 us
    pallas_call x1, Pallas kernels, transform_other(): pl.pallas_call(functools.partial(other_kernel, outer, inner), out_shape=[...  1.57 us
  transfers between devices with their start and end apart: 10, of which 6 were waited for; matrix products, arithmetic and copies ran while one was open for 0% of the time, Pallas kernels for 16%

profile of v2, /device:TPU:0, one launch (start us, length us, event | category | flops | bytes accessed | tf_op | source)
XLA Modules:
  0.0 31.2 jit_solution(6457322587562850238)
XLA Ops:
  0.0 0.0 copy-start
  0.0 0.5 %collective-permute-start.1 = (f32[8,32768]{1,0:T(8,128)}, f32[8,32768]{1,0:T(8,128)S(1)}, u32[]{:S(2)}, u32[]{:S(2)}) collective-permute-start(f32[8,32768]{1,0:T(8,128)} %values_hbm.1), channel_id=1, source_target_pairs={{0,1},{1,0},{2,3},{3,2},{4,5},{5,4},{6,7},{7,6},{8,9},{9,8},{10,11... | collective-permute-start | bytes 3145736 | tf_op jit(solution)/shard_map/ppermute | solution.py:226
  0.5 0.1 collective-permute-start.2
  0.5 2.6 %collective-permute-start = (s32[128]{0:T(128)}, s32[128]{0:T(128)S(1)}, u32[]{:S(2)}, u32[]{:S(2)}) collective-permute-start(s32[128]{0:T(128)} %samples_ref.1), channel_id=1, source_target_pairs={{0,3},{1,2},{2,1},{3,0},{4,7},{5,6},{6,5},{7,4},{8,11},{9,10},{10,... | collective-permute-start | bytes 1544 | tf_op jit(solution)/shard_map/ppermute | solution.py:226
  3.1 0.0 copy-done
  3.1 2.2 %transform_own.1 = (f32[1024,256]{1,0:T(8,128)S(1)}, s32[128]{0:T(128)S(1)}) custom-call(f32[8,32768]{1,0:T(8,128)} %values_hbm.1, s32[256,128]{1,0:T(8,128)} %bitcast.9, s32[128]{0:T(128)S(1)} %copy-done), custom_call_target="tpu_custom_call" | custom-call | flops 268435456 | bytes 2621440 | tf_op jit(solution)/shard_map/transform_own/pallas_call | solution.py:129
  5.4 0.0 collective-permute-done
  5.4 0.0 collective-permute-done.2
  5.4 0.0 collective-permute-done.1.values_ref
  5.4 1.6 %collective-permute-start.3 = (s32[256]{0:T(256)S(1)}, s32[256]{0:T(256)S(1)}, u32[]{:S(2)}, u32[]{:S(2)}) collective-permute-start(s32[256]{0:T(256)S(1)} %pad_add_fusion.4), channel_id=1, source_target_pairs={{0,5},{1,4},{2,7},{3,6},{4,1},{5,0},{6,3},{7,2},{8,13},{9,12},{10,... | collective-permute-start | bytes 3080 | tf_op jit(solution)/shard_map/ppermute | solution.py:226
  7.0 1.6 %transform_other.1 = (bf16[1024,512]{1,0:T(8,128)(2,1)S(1)}, bf16[1024,512]{1,0:T(8,128)(2,1)S(1)}) custom-call(f32[8,32768]{1,0:T(8,128)S(1)} %collective-permute-done.1.values_ref, s32[256,128]{1,0:T(8,128)S(1)} %bitcast.8, f32[1024,256]{1,0:T(8,128)S(1)} %get-tuple-element.25.mine_ref), custom_call_target="tpu_custom_call" | custom-call | flops 268435456 | bytes 2621440 | tf_op jit(solution)/shard_map/transform_other/pallas_call | solution.py:158
  8.6 0.0 collective-permute-done.3
  8.6 1.5 %collective-permute-start.4 = (s32[512]{0:T(512)S(1)}, s32[512]{0:T(512)S(1)}, u32[]{:S(2)}, u32[]{:S(2)}) collective-permute-start(s32[512]{0:T(512)S(1)} %pad_add_fusion.3), channel_id=1, source_target_pairs={{0,9},{1,8},{2,11},{3,10},{4,13},{5,12},{6,15},{7,14},{8,1},{9,0},... | collective-permute-start | bytes 6152 | tf_op jit(solution)/shard_map/ppermute | solution.py:226
  10.1 1.6 %collective-permute-done.4 = s32[512]{0:T(512)S(1)} collective-permute-done((s32[512]{0:T(512)S(1)}, s32[512]{0:T(512)S(1)}, u32[]{:S(2)}, u32[]{:S(2)}) %collective-permute-start.4) | collective-permute-done | bytes 2080 | tf_op jit(solution)/shard_map/ppermute | solution.py:226
  11.7 2.4 %collective-permute-start.5 = (s32[1024]{0:T(1024)S(1)}, s32[1024]{0:T(1024)S(1)}, u32[]{:S(2)}, u32[]{:S(2)}) collective-permute-start(s32[1024]{0:T(1024)S(1)} %pad_add_fusion.1), channel_id=1, source_target_pairs={{0,17},{1,16},{2,19},{3,18},{4,21},{5,20},{6,23},{7,22},{8,25},{9,... | collective-permute-start | bytes 12296 | tf_op jit(solution)/shard_map/ppermute | solution.py:226
  14.1 1.3 %gather.2 = f32[8,8,128]{2,1,0:T(8,128)S(1)} custom-call(bf16[1024,512]{1,0:T(8,128)(2,1)S(1)} %get-tuple-element.28.even_ref, bf16[1024,512]{1,0:T(8,128)(2,1)S(1)} %get-tuple-element.29.odd_ref, s32[8,128]{1,0:T(8,128)S(1)} %pad_add_fusion.2.offsets_ref), custom_call_target="tpu_custom_call" | custom-call | flops 1073741824 | bytes 1048576 | tf_op jit(solution)/shard_map/gather/pallas_call | solution.py:201
  15.4 0.2 collective-permute-done.5
  15.7 1.3 %gather.3 = f32[8,8,128]{2,1,0:T(8,128)S(1)} custom-call(bf16[1024,512]{1,0:T(8,128)(2,1)S(1)} %get-tuple-element.28.even_ref, bf16[1024,512]{1,0:T(8,128)(2,1)S(1)} %get-tuple-element.29.odd_ref, s32[8,128]{1,0:T(8,128)S(1)} %slice_bitcast_fusion.offsets_ref), custom_call_target="tpu_custom_call" | custom-call | flops 1073741824 | bytes 1048576 | tf_op jit(solution)/shard_map/gather/pallas_call | solution.py:201
  17.0 2.5 %collective-permute-start.6 = (f32[8,8,128]{2,1,0:T(8,128)S(1)}, f32[8,8,128]{2,1,0:T(8,128)S(1)}, u32[]{:S(2)}, u32[]{:S(2)}) collective-permute-start(f32[8,8,128]{2,1,0:T(8,128)S(1)} %gather.3), channel_id=1, source_target_pairs={{0,17},{1,16},{2,19},{3,18},{4,21},{5,20},{6,23},{7,22},{8,25},{9,... | collective-permute-start | bytes 98312 | tf_op jit(solution)/shard_map/ppermute | solution.py:226
  19.4 1.8 %collective-permute-done.6 = f32[8,8,128]{2,1,0:T(8,128)S(1)} collective-permute-done((f32[8,8,128]{2,1,0:T(8,128)S(1)}, f32[8,8,128]{2,1,0:T(8,128)S(1)}, u32[]{:S(2)}, u32[]{:S(2)}) %collective-permute-start.6) | collective-permute-done | bytes 32800 | tf_op jit(solution)/shard_map/ppermute | solution.py:226
  21.3 1.5 %collective-permute-start.7 = (f32[4,8,128]{2,1,0:T(8,128)S(1)}, f32[4,8,128]{2,1,0:T(8,128)S(1)}, u32[]{:S(2)}, u32[]{:S(2)}) collective-permute-start(f32[4,8,128]{2,1,0:T(8,128)S(1)} %slice.40), channel_id=1, source_target_pairs={{0,9},{1,8},{2,11},{3,10},{4,13},{5,12},{6,15},{7,14},{8,1},{9,0},... | collective-permute-start | bytes 49160 | tf_op jit(solution)/shard_map/ppermute | solution.py:226
  22.7 1.8 %collective-permute-done.7 = f32[4,8,128]{2,1,0:T(8,128)S(1)} collective-permute-done((f32[4,8,128]{2,1,0:T(8,128)S(1)}, f32[4,8,128]{2,1,0:T(8,128)S(1)}, u32[]{:S(2)}, u32[]{:S(2)}) %collective-permute-start.7) | collective-permute-done | bytes 16416 | tf_op jit(solution)/shard_map/ppermute | solution.py:226
  24.5 1.4 %collective-permute-start.8 = (f32[2,8,128]{2,1,0:T(8,128)S(1)}, f32[2,8,128]{2,1,0:T(8,128)S(1)}, u32[]{:S(2)}, u32[]{:S(2)}) collective-permute-start(f32[2,8,128]{2,1,0:T(8,128)S(1)} %slice.42), channel_id=1, source_target_pairs={{0,5},{1,4},{2,7},{3,6},{4,1},{5,0},{6,3},{7,2},{8,13},{9,12},{10,... | collective-permute-start | bytes 24584 | tf_op jit(solution)/shard_map/ppermute | solution.py:226
  25.9 1.7 %collective-permute-done.8 = f32[2,8,128]{2,1,0:T(8,128)S(1)} collective-permute-done((f32[2,8,128]{2,1,0:T(8,128)S(1)}, f32[2,8,128]{2,1,0:T(8,128)S(1)}, u32[]{:S(2)}, u32[]{:S(2)}) %collective-permute-start.8) | collective-permute-done | bytes 8224 | tf_op jit(solution)/shard_map/ppermute | solution.py:226
  27.6 0.8 %collective-permute-start.9 = (f32[1,8,128]{2,1,0:T(8,128)S(1)}, f32[1,8,128]{2,1,0:T(8,128)S(1)}, u32[]{:S(2)}, u32[]{:S(2)}) collective-permute-start(f32[1,8,128]{2,1,0:T(8,128)S(1)} %slice.44), channel_id=1, source_target_pairs={{0,3},{1,2},{2,1},{3,0},{4,7},{5,6},{6,5},{7,4},{8,11},{9,10},{10,... | collective-permute-start | bytes 12296 | tf_op jit(solution)/shard_map/ppermute | solution.py:226
  28.4 2.2 %collective-permute-done.9 = f32[1,8,128]{2,1,0:T(8,128)S(1)} collective-permute-done((f32[1,8,128]{2,1,0:T(8,128)S(1)}, f32[1,8,128]{2,1,0:T(8,128)S(1)}, u32[]{:S(2)}, u32[]{:S(2)}) %collective-permute-start.9) | collective-permute-done | bytes 4128 | tf_op jit(solution)/shard_map/ppermute | solution.py:226
  30.6 0.6 %fusion.4 = f32[8,128]{1,0:T(8,128)} fusion(f32[1,8,128]{2,1,0:T(8,128)S(1)} %collective-permute-done.9, f32[2,8,128]{2,1,0:T(8,128)S(1)} %fusion.1, f32[]{:T(128)S(6)} %convert_element_type.15), kind=kLoop, calls=%fused_computation.9 | loop fusion | flops 3072 | bytes 12292 | tf_op jit(solution)/shard_map/mul | solution.py:260
  (12 shorter events, 0.1 us)
Async XLA Ops:
  0.0 3.1 %copy-start = (s32[128]{0:T(128)S(1)}, s32[128]{0:T(128)}, u32[]{:S(2)}) copy-start(s32[128]{0:T(128)} %samples_ref.1) | copy-start | bytes 1540
  0.0 5.4 %collective-permute-start.1 = (f32[8,32768]{1,0:T(8,128)}, f32[8,32768]{1,0:T(8,128)S(1)}, u32[]{:S(2)}, u32[]{:S(2)}) collective-permute-start(f32[8,32768]{1,0:T(8,128)} %values_hbm.1), channel_id=1, source_target_pairs={{0,1},{1,0},{2,3},{3,2},{4,5},{5,4},{6,7},{7,6},{8,9},{9,8},{10,11... | collective-permute-start | bytes 3145736 | tf_op jit(solution)/shard_map/ppermute | solution.py:226
  0.5 4.9 %collective-permute-start.2 = (s32[32768]{0:T(1024)}, s32[32768]{0:T(1024)S(1)}, u32[]{:S(2)}, u32[]{:S(2)}) collective-permute-start(s32[32768]{0:T(1024)} %param.4), channel_id=1, source_target_pairs={{0,1},{1,0},{2,3},{3,2},{4,5},{5,4},{6,7},{7,6},{8,9},{9,8},{10,11... | collective-permute-start | bytes 393224 | tf_op jit(solution)/shard_map/ppermute | solution.py:226
  0.5 4.8 %collective-permute-start = (s32[128]{0:T(128)}, s32[128]{0:T(128)S(1)}, u32[]{:S(2)}, u32[]{:S(2)}) collective-permute-start(s32[128]{0:T(128)} %samples_ref.1), channel_id=1, source_target_pairs={{0,3},{1,2},{2,1},{3,0},{4,7},{5,6},{6,5},{7,4},{8,11},{9,10},{10,... | collective-permute-start | bytes 1544 | tf_op jit(solution)/shard_map/ppermute | solution.py:226
  5.4 3.2 %collective-permute-start.3 = (s32[256]{0:T(256)S(1)}, s32[256]{0:T(256)S(1)}, u32[]{:S(2)}, u32[]{:S(2)}) collective-permute-start(s32[256]{0:T(256)S(1)} %pad_add_fusion.4), channel_id=1, source_target_pairs={{0,5},{1,4},{2,7},{3,6},{4,1},{5,0},{6,3},{7,2},{8,13},{9,12},{10,... | collective-permute-start | bytes 3080 | tf_op jit(solution)/shard_map/ppermute | solution.py:226
  8.6 3.1 %collective-permute-start.4 = (s32[512]{0:T(512)S(1)}, s32[512]{0:T(512)S(1)}, u32[]{:S(2)}, u32[]{:S(2)}) collective-permute-start(s32[512]{0:T(512)S(1)} %pad_add_fusion.3), channel_id=1, source_target_pairs={{0,9},{1,8},{2,11},{3,10},{4,13},{5,12},{6,15},{7,14},{8,1},{9,0},... | collective-permute-start | bytes 6152 | tf_op jit(solution)/shard_map/ppermute | solution.py:226
  11.7 3.9 %collective-permute-start.5 = (s32[1024]{0:T(1024)S(1)}, s32[1024]{0:T(1024)S(1)}, u32[]{:S(2)}, u32[]{:S(2)}) collective-permute-start(s32[1024]{0:T(1024)S(1)} %pad_add_fusion.1), channel_id=1, source_target_pairs={{0,17},{1,16},{2,19},{3,18},{4,21},{5,20},{6,23},{7,22},{8,25},{9,... | collective-permute-start | bytes 12296 | tf_op jit(solution)/shard_map/ppermute | solution.py:226
  17.0 4.3 %collective-permute-start.6 = (f32[8,8,128]{2,1,0:T(8,128)S(1)}, f32[8,8,128]{2,1,0:T(8,128)S(1)}, u32[]{:S(2)}, u32[]{:S(2)}) collective-permute-start(f32[8,8,128]{2,1,0:T(8,128)S(1)} %gather.3), channel_id=1, source_target_pairs={{0,17},{1,16},{2,19},{3,18},{4,21},{5,20},{6,23},{7,22},{8,25},{9,... | collective-permute-start | bytes 98312 | tf_op jit(solution)/shard_map/ppermute | solution.py:226
  21.3 3.2 %collective-permute-start.7 = (f32[4,8,128]{2,1,0:T(8,128)S(1)}, f32[4,8,128]{2,1,0:T(8,128)S(1)}, u32[]{:S(2)}, u32[]{:S(2)}) collective-permute-start(f32[4,8,128]{2,1,0:T(8,128)S(1)} %slice.40), channel_id=1, source_target_pairs={{0,9},{1,8},{2,11},{3,10},{4,13},{5,12},{6,15},{7,14},{8,1},{9,0},... | collective-permute-start | bytes 49160 | tf_op jit(solution)/shard_map/ppermute | solution.py:226
  24.5 3.1 %collective-permute-start.8 = (f32[2,8,128]{2,1,0:T(8,128)S(1)}, f32[2,8,128]{2,1,0:T(8,128)S(1)}, u32[]{:S(2)}, u32[]{:S(2)}) collective-permute-start(f32[2,8,128]{2,1,0:T(8,128)S(1)} %slice.42), channel_id=1, source_target_pairs={{0,5},{1,4},{2,7},{3,6},{4,1},{5,0},{6,3},{7,2},{8,13},{9,12},{10,... | collective-permute-start | bytes 24584 | tf_op jit(solution)/shard_map/ppermute | solution.py:226
  27.6 3.0 %collective-permute-start.9 = (f32[1,8,128]{2,1,0:T(8,128)S(1)}, f32[1,8,128]{2,1,0:T(8,128)S(1)}, u32[]{:S(2)}, u32[]{:S(2)}) collective-permute-start(f32[1,8,128]{2,1,0:T(8,128)S(1)} %slice.44), channel_id=1, source_target_pairs={{0,3},{1,2},{2,1},{3,0},{4,7},{5,6},{6,5},{7,4},{8,11},{9,10},{10,... | collective-permute-start | bytes 12296 | tf_op jit(solution)/shard_map/ppermute | solution.py:226

commit v3 on v2

v3 whole, which is shorter than its diff:
```python
import functools
import math

import jax
import jax.numpy as jnp
from jax import lax
from jax.experimental import pallas as pl
from jax.experimental.pallas import tpu as pltpu
from jax.sharding import PartitionSpec as P

LANES = 128
LOW = 256
MIX_ROWS = 64
AXES = ("wide", "narrow")
VMEM_LIMIT = 40 << 20


def vmem():
    return pl.BlockSpec(memory_space=pltpu.VMEM)


def parity(value):
    return bin(value).count("1") & 1


def hadamard_rows(order):
    row = lax.broadcasted_iota(jnp.int32, (order, order), 0)
    col = lax.broadcasted_iota(jnp.int32, (order, order), 1)
    bits = row & col
    shift = order.bit_length() // 2
    while shift:
        bits = bits ^ (bits >> shift)
        shift //= 2
    sign = (1 - 2 * (bits & 1)).astype(jnp.float32).astype(jnp.bfloat16)
    return jnp.concatenate([sign, sign], axis=0)


def two_parts(values):
    high = values.astype(jnp.bfloat16)
    low = (values - high.astype(jnp.float32)).astype(jnp.bfloat16)
    return jnp.concatenate([high, low], axis=1)


def butterfly(values):
    values = list(values)
    step = 1
    while step < len(values):
        for at in range(len(values)):
            if not at & step:
                first, second = values[at], values[at | step]
                values[at], values[at | step] = first + second, first - second
        step *= 2
    return values


def first_pass(outer, inner, values_ref, signs_ref, mid, a):
    cols = values_ref.shape[0]
    tiles = LOW // LANES
    for tile in range(tiles):
        values = []
        for b in range(inner):
            at = (a * inner + b) * tiles + tile
            lanes = pl.ds(pl.multiple_of(at * LANES, LANES), LANES)
            values.append(values_ref[:, lanes] * signs_ref[pl.ds(at, 1), :].astype(jnp.float32))
        for b, value in enumerate(butterfly(values)):
            rows = pl.ds(pl.multiple_of((a * inner + b) * cols, cols), cols)
            mid[rows, tile * LANES : (tile + 1) * LANES] = value


def second_pass(outer, inner, cols, mid, parts):
    def step(b, carry):
        values = [mid[pl.ds(pl.multiple_of((a * inner + b) * cols, cols), cols), :] for a in range(outer)]
        block = two_parts(jnp.concatenate(butterfly(values), axis=0))
        parts[pl.ds(pl.multiple_of(b * outer * cols, outer * cols), outer * cols), :] = block
        return carry

    lax.fori_loop(0, inner, step, 0)


def high_kernel(outer, inner, values_hbm, signs_hbm, samples_ref, parts_ref, list_ref, values_ref, signs_ref, mid, sems):
    cols, rows = values_hbm.shape
    block = rows // outer
    signs_copy = pltpu.make_async_copy(signs_hbm, signs_ref, sems.at[outer])
    copies = [
        pltpu.make_async_copy(
            values_hbm.at[:, pl.ds(a * block, block)], values_ref.at[:, pl.ds(a * block, block)], sems.at[a]
        )
        for a in range(outer)
    ]
    signs_copy.start()
    for copy in copies:
        copy.start()
    list_ref[...] = samples_ref[...]
    signs_copy.wait()
    for a, copy in enumerate(copies):
        copy.wait()
        first_pass(outer, inner, values_ref, signs_ref, mid, a)
    second_pass(outer, inner, cols, mid, parts_ref)


def low_kernel(parts_ref, out_ref):
    out_ref[...] = jnp.dot(parts_ref[...], hadamard_rows(LOW), preferred_element_type=jnp.float32)


def mix_kernel(groups, mine_ref, other_ref, offsets_ref, even_ref, odd_ref, out_ref):
    core = lax.axis_index("narrow") & 1
    flip = (1 - 2 * core).astype(jnp.float32)

    def step(at, carry):
        rows = pl.ds(pl.multiple_of(at * MIX_ROWS, MIX_ROWS), MIX_ROWS)
        mine, other = mine_ref[rows, :], other_ref[rows, :]
        even_ref[rows, :] = two_parts(other + flip * mine)
        odd_ref[rows, :] = two_parts(mine - flip * other)
        return carry

    lax.fori_loop(0, mine_ref.shape[0] // MIX_ROWS, step, 0)
    pick(0, groups, mine_ref.shape[0] // groups, (even_ref, odd_ref), offsets_ref[...], out_ref, 0)


def split_groups(groups):
    outer = 1 << (groups.bit_length() - 1) // 2
    return outer, groups // outer


def transform_high(values, signs, samples):
    cols, rows = values.shape
    groups = rows // LOW
    outer, inner = split_groups(groups)
    hbm = pl.BlockSpec(memory_space=pltpu.HBM)
    return pl.pallas_call(
        functools.partial(high_kernel, outer, inner),
        out_shape=[
            jax.ShapeDtypeStruct((groups * cols, 2 * LOW), jnp.bfloat16),
            jax.ShapeDtypeStruct(samples.shape, samples.dtype),
        ],
        in_specs=[hbm, hbm, vmem()],
        out_specs=[vmem()] * 2,
        scratch_shapes=[
            pltpu.VMEM(values.shape, jnp.float32),
            pltpu.VMEM((rows // LANES, LANES), jnp.int32),
            pltpu.VMEM((groups * cols, LOW), jnp.float32),
            pltpu.SemaphoreType.DMA((outer + 1,)),
        ],
        compiler_params=pltpu.CompilerParams(vmem_limit_bytes=VMEM_LIMIT),
        cost_estimate=pl.CostEstimate(flops=4 * cols * rows * LOW, bytes_accessed=10 * cols * rows, transcendentals=0),
        name="transform_high",
    )(
        pltpu.with_memory_space_constraint(values, pltpu.HBM),
        pltpu.with_memory_space_constraint(signs.reshape(rows // LANES, LANES), pltpu.HBM),
        samples,
    )


def transform_low(parts):
    rows, width = parts.shape
    return pl.pallas_call(
        low_kernel,
        out_shape=jax.ShapeDtypeStruct((rows, width // 2), jnp.float32),
        in_specs=[vmem()],
        out_specs=vmem(),
        compiler_params=pltpu.CompilerParams(vmem_limit_bytes=VMEM_LIMIT),
        cost_estimate=pl.CostEstimate(flops=rows * width * width, bytes_accessed=4 * rows * width, transcendentals=0),
        name="transform_low",
    )(parts)


def mix(mine, other, groups, offsets):
    rows, low = mine.shape
    count, samp = offsets.shape
    return pl.pallas_call(
        functools.partial(mix_kernel, groups),
        out_shape=[
            jax.ShapeDtypeStruct((rows, 2 * low), jnp.bfloat16),
            jax.ShapeDtypeStruct((rows, 2 * low), jnp.bfloat16),
            jax.ShapeDtypeStruct((count, rows // groups, samp), jnp.float32),
        ],
        in_specs=[vmem()] * 3,
        out_specs=[vmem()] * 3,
        compiler_params=pltpu.CompilerParams(vmem_limit_bytes=VMEM_LIMIT),
        cost_estimate=pl.CostEstimate(
            flops=4 * rows * low * count * samp, bytes_accessed=16 * rows * low, transcendentals=0
        ),
        name="mix",
    )(mine, other, offsets)


def pick(first, groups, cols, tables, offsets, out_ref, at_row):
    count, samp = offsets.shape
    outer, inner = split_groups(groups)
    by_parity = [[t for t in range(count) if parity(first + t) == p] for p in range(2)]
    for table_ref, targets in zip(tables, by_parity):
        for at in range(0, len(targets), 2):
            pair = targets[at : at + 2]
            offset = jnp.concatenate([offsets[t : t + 1] for t in pair], axis=1)
            width = offset.shape[1]
            low = offset & (LOW - 1)
            high = jnp.broadcast_to(offset // LOW & (groups - 1), (cols, width))
            rows = lax.broadcasted_iota(jnp.int32, (LOW, width), 0)
            chosen = (rows == low).astype(jnp.float32).astype(jnp.bfloat16)
            chosen = jnp.concatenate([chosen, chosen], axis=0)
            picked = jnp.dot(table_ref[...], chosen, preferred_element_type=jnp.float32)
            sums = [jnp.zeros((cols, width), jnp.float32) for _ in range(2)]
            for g in range(groups):
                block = picked[g * cols : (g + 1) * cols]
                sums[g % 2] = jnp.where(high == g % outer * inner + g // outer, block, sums[g % 2])
            total = sums[0] + sums[1]
            for i, t in enumerate(pair):
                out_ref[at_row + t] = total[:, i * samp : (i + 1) * samp]


def gather_kernel(first, groups, even_ref, odd_ref, offsets_ref, known_ref, out_ref):
    kept, cols, _ = known_ref.shape
    out_ref[:kept] = known_ref[...]
    pick(first, groups, cols, (even_ref, odd_ref), offsets_ref[...], out_ref, kept)


def gather(first, groups, even, odd, offsets, known):
    count, samp = offsets.shape
    kept, cols, _ = known.shape
    return pl.pallas_call(
        functools.partial(gather_kernel, first, groups),
        out_shape=jax.ShapeDtypeStruct((kept + count, cols, samp), jnp.float32),
        in_specs=[vmem()] * 4,
        out_specs=vmem(),
        compiler_params=pltpu.CompilerParams(vmem_limit_bytes=VMEM_LIMIT),
        cost_estimate=pl.CostEstimate(
            flops=4 * groups * cols * LOW * count * samp, bytes_accessed=4 * groups * cols * LOW, transcendentals=0
        ),
        name="gather",
    )(even, odd, offsets, known)


def per_device(panel, signs, samples):
    cols, rows = panel.shape
    samp = samples.shape[0]
    n_wide = lax.axis_size("wide")
    n_narrow = lax.axis_size("narrow")
    wide_bits = n_wide.bit_length() - 1
    narrow_bits = n_narrow.bit_length() - 1
    n_all = n_wide * n_narrow
    wide_me = lax.axis_index("wide")
    narrow_me = lax.axis_index("narrow")

    def across(values, mask):
        return lax.ppermute(values, AXES, [(i, i ^ mask) for i in range(n_all)])

    for bit in range(1, narrow_bits):
        if bit == 1:
            panel = panel * signs.astype(jnp.float32)[None, :]
            signs = jnp.ones_like(signs)
        upper = narrow_me >> bit & 1 == 1
        partner = across(panel, 1 << bit)
        panel = jnp.where(upper, partner - panel, panel + partner)

    groups = rows // LOW
    half, quarter = n_wide // 2, n_wide // 4
    ladder = list(reversed(range(wide_bits)))

    def exchange(values, i):
        return across(values, n_narrow << ladder[i] | 1)

    arrived = exchange(samples, 0)
    parts, listed = transform_high(panel, signs, samples)
    arrived, parts, listed = lax.optimization_barrier((arrived, parts, listed))
    asked = jnp.concatenate([listed, arrived])
    for i in range(1, wide_bits):
        if i == 2:
            asked, mine = lax.optimization_barrier((asked, mine))
            other = across(mine, 1)
        if i == wide_bits - 1:
            asked, other = lax.optimization_barrier((asked, other))
            even, odd, early = mix(mine, other, groups, asked.reshape(half, samp))
        arrived = exchange(asked, i)
        if i == 1:
            mine = transform_low(parts)
        asked = jnp.concatenate([asked, arrived])
    arrived, early = lax.optimization_barrier((arrived, early))
    late = arrived.reshape(half, samp)

    far = gather(half + quarter, groups, even, odd, late[quarter:], early[quarter:])
    near = gather(half, groups, even, odd, late[:quarter], early[:quarter])
    for i in [wide_bits - 2, wide_bits - 1, *reversed(range(wide_bits - 2))]:
        sign = (1 - 2 * (wide_me >> ladder[i] & 1)).astype(jnp.float32)
        total = exchange(far, i) + sign * near
        middle = total.shape[0] // 2
        near, far = total[:middle], total[middle:]
    return total[0] * jnp.float32(1.0 / math.sqrt(samp * n_all))


def solution(mesh):
    in_specs = (P(None, AXES), P(AXES), P(AXES))
    return jax.shard_map(per_device, mesh=mesh, in_specs=in_specs, out_specs=P(None, AXES), check_vma=False)
```

time: 31.4 us -> 30.4 us (0.968)
  Pallas kernels: 6.37 us -> 5.54 us
    pallas_call x4 -> x5, Pallas kernels: 6.37 us -> 5.54 us  [the longest x1 1.8 us: transform_high(): pl.pallas_call(functools.partial(high_kernel, outer, inner), out_shape=[j...]
    ppermute x10 -> x9, waiting for transfers between devices: 9.32 us -> 9.05 us  [across(): return lax.ppermute(values, AXES, [(i, i ^ mask) for i in range(n_all)])]
    ppermute x10 -> x9, starting transfers between devices: 14.8 us -> 14.9 us  [across(): return lax.ppermute(values, AXES, [(i, i ^ mask) for i in range(n_all)])]
  transfers between devices with their start and end apart: 10 -> 9, of which waited for: 6 -> 7; matrix products, arithmetic and copies ran while one was open for 0% -> 0% of each run, Pallas kernels for 16% -> 16%
where the time goes in v3:
time: 30.4 us; the launch traced here: 30.2 us
  starting transfers between devices  14.9 us (49%)
  waiting for transfers between devices  9.05 us (30%)
  Pallas kernels  5.54 us (18%)
  other arithmetic  0.63 us (2%)
    ppermute x9, starting transfers between devices, across(): return lax.ppermute(values, AXES, [(i, i ^ mask) for i in range(n_all)])  14.9 us
    ppermute x9, waiting for transfers between devices, across(): return lax.ppermute(values, AXES, [(i, i ^ mask) for i in range(n_all)])  9.05 us
    pallas_call x1, Pallas kernels, transform_high(): pl.pallas_call(functools.partial(high_kernel, outer, inner), out_shape=[j...  1.8 us
    pallas_call x1, Pallas kernels, mix(): pl.pallas_call(functools.partial(mix_kernel, groups), out_shape=[jax.Shap...  1.76 us
    pallas_call x2, Pallas kernels, gather(): pl.pallas_call(functools.partial(gather_kernel, first, groups), out_shape...  1.48 us
  transfers between devices with their start and end apart: 9, of which 7 were waited for; matrix products, arithmetic and copies ran while one was open for 0% of the time, Pallas kernels for 16%

profile of v3, /device:TPU:0, one launch (start us, length us, event | category | flops | bytes accessed | tf_op | source)
XLA Modules:
  0.0 30.2 jit_solution(1674717807197643909)
XLA Ops:
  0.0 0.0 copy-start
  0.0 3.5 %collective-permute-start = (s32[128]{0:T(128)}, s32[128]{0:T(128)S(1)}, u32[]{:S(2)}, u32[]{:S(2)}) collective-permute-start(s32[128]{0:T(128)} %samples_ref.1), channel_id=1, source_target_pairs={{0,17},{1,16},{2,19},{3,18},{4,21},{5,20},{6,23},{7,22},{8,25},{9,... | collective-permute-start | bytes 1544 | tf_op jit(solution)/shard_map/ppermute | solution.py:245
  3.5 0.0 copy-done
  3.5 1.8 %transform_high.1 = (bf16[1024,512]{1,0:T(8,128)(2,1)S(1)}, s32[128]{0:T(128)S(1)}) custom-call(f32[8,32768]{1,0:T(8,128)} %values_hbm.1, s32[256,128]{1,0:T(8,128)} %bitcast.9, s32[128]{0:T(128)S(1)} %copy-done), custom_call_target="tpu_custom_call" | custom-call | flops 268435456 | bytes 2621440 | tf_op jit(solution)/shard_map/transform_high/pallas_call | solution.py:130
  5.3 0.0 collective-permute-done
  5.3 1.9 %collective-permute-start.1 = (s32[256]{0:T(256)S(1)}, s32[256]{0:T(256)S(1)}, u32[]{:S(2)}, u32[]{:S(2)}) collective-permute-start(s32[256]{0:T(256)S(1)} %pad_add_fusion.2), channel_id=1, source_target_pairs={{0,9},{1,8},{2,11},{3,10},{4,13},{5,12},{6,15},{7,14},{8,1},{9,0},... | collective-permute-start | bytes 3080 | tf_op jit(solution)/shard_map/ppermute | solution.py:245
  7.2 0.5 %transform_low.1.mine_ref = f32[1024,256]{1,0:T(8,128)S(1)} custom-call(bf16[1024,512]{1,0:T(8,128)(2,1)S(1)} %get-tuple-element.23.parts_ref), custom_call_target="tpu_custom_call" | custom-call | flops 268435456 | bytes 2097152 | tf_op jit(solution)/shard_map/transform_low/pallas_call | solution.py:156
  7.7 0.8 %collective-permute-done.1 = s32[256]{0:T(256)S(1)} collective-permute-done((s32[256]{0:T(256)S(1)}, s32[256]{0:T(256)S(1)}, u32[]{:S(2)}, u32[]{:S(2)}) %collective-permute-start.1) | collective-permute-done | bytes 1056 | tf_op jit(solution)/shard_map/ppermute | solution.py:245
  8.5 0.5 %collective-permute-start.3 = (f32[1024,256]{1,0:T(8,128)S(1)}, f32[1024,256]{1,0:T(8,128)S(1)}, u32[]{:S(2)}, u32[]{:S(2)}) collective-permute-start(f32[1024,256]{1,0:T(8,128)S(1)} %transform_low.1.mine_ref), channel_id=1, source_target_pairs={{0,1},{1,0},{2,3},{3,2},{4,5},{5,4},{6,7},{7,6},{8,9},{9,8},{10,11... | collective-permute-start | bytes 3145736 | tf_op jit(solution)/shard_map/ppermute | solution.py:245
  9.1 1.2 %collective-permute-start.2 = (s32[512]{0:T(512)S(1)}, s32[512]{0:T(512)S(1)}, u32[]{:S(2)}, u32[]{:S(2)}) collective-permute-start(s32[512]{0:T(512)S(1)} %pad_add_fusion.1), channel_id=1, source_target_pairs={{0,5},{1,4},{2,7},{3,6},{4,1},{5,0},{6,3},{7,2},{8,13},{9,12},{10,... | collective-permute-start | bytes 6152 | tf_op jit(solution)/shard_map/ppermute | solution.py:245
  10.3 1.8 %collective-permute-done.2 = s32[512]{0:T(512)S(1)} collective-permute-done((s32[512]{0:T(512)S(1)}, s32[512]{0:T(512)S(1)}, u32[]{:S(2)}, u32[]{:S(2)}) %collective-permute-start.2) | collective-permute-done | bytes 2080 | tf_op jit(solution)/shard_map/ppermute | solution.py:245
  12.1 0.0 collective-permute-done.3.other_ref
  12.1 1.3 %collective-permute-start.4 = (s32[1024]{0:T(1024)S(1)}, s32[1024]{0:T(1024)S(1)}, u32[]{:S(2)}, u32[]{:S(2)}) collective-permute-start(s32[1024]{0:T(1024)S(1)} %pad_add_fusion), channel_id=1, source_target_pairs={{0,3},{1,2},{2,1},{3,0},{4,7},{5,6},{6,5},{7,4},{8,11},{9,10},{10,... | collective-permute-start | bytes 12296 | tf_op jit(solution)/shard_map/ppermute | solution.py:245
  13.4 1.8 %mix.1 = (bf16[1024,512]{1,0:T(8,128)(2,1)S(1)}, bf16[1024,512]{1,0:T(8,128)(2,1)S(1)}, f32[8,8,128]{2,1,0:T(8,128)S(1)}) custom-call(f32[1024,256]{1,0:T(8,128)S(1)} %transform_low.1.mine_ref, f32[1024,256]{1,0:T(8,128)S(1)} %collective-permute-done.3.other_ref, s32[8,128]{1,0:T(8,128)S(1)} %bitcast.8), custom_call_target="tpu_custom_call" | custom-call | flops 1073741824 | bytes 4194304 | tf_op jit(solution)/shard_map/mix/pallas_call | solution.py:170
  15.1 0.1 collective-permute-done.4
  15.2 0.7 %gather.2 = f32[8,8,128]{2,1,0:T(8,128)S(1)} custom-call(bf16[1024,512]{1,0:T(8,128)(2,1)S(1)} %get-tuple-element.28.even_ref, bf16[1024,512]{1,0:T(8,128)(2,1)S(1)} %get-tuple-element.29.odd_ref, s32[4,128]{1,0:T(4,128)S(1)} %get-tuple-element.36.offsets_ref, f32[4,8,128]{2,1,0:T(8,128)S(1)} %get-tuple-element.34.known_ref), custom_call_target="tpu_custom_call" | custom-call | flops 536870912 | bytes 1048576 | tf_op jit(solution)/shard_map/gather/pallas_call | solution.py:220
  15.9 1.6 %collective-permute-start.5 = (f32[8,8,128]{2,1,0:T(8,128)S(1)}, f32[8,8,128]{2,1,0:T(8,128)S(1)}, u32[]{:S(2)}, u32[]{:S(2)}) collective-permute-start(f32[8,8,128]{2,1,0:T(8,128)S(1)} %gather.2), channel_id=1, source_target_pairs={{0,5},{1,4},{2,7},{3,6},{4,1},{5,0},{6,3},{7,2},{8,13},{9,12},{10,... | collective-permute-start | bytes 98312 | tf_op jit(solution)/shard_map/ppermute | solution.py:245
  17.5 0.7 %gather.3 = f32[8,8,128]{2,1,0:T(8,128)S(1)} custom-call(bf16[1024,512]{1,0:T(8,128)(2,1)S(1)} %get-tuple-element.28.even_ref, bf16[1024,512]{1,0:T(8,128)(2,1)S(1)} %get-tuple-element.29.odd_ref, s32[4,128]{1,0:T(4,128)S(1)} %get-tuple-element.35.offsets_ref, f32[4,8,128]{2,1,0:T(8,128)S(1)} %get-tuple-element.33.known_ref), custom_call_target="tpu_custom_call" | custom-call | flops 536870912 | bytes 1048576 | tf_op jit(solution)/shard_map/gather/pallas_call | solution.py:220
  18.2 1.1 %collective-permute-done.5 = f32[8,8,128]{2,1,0:T(8,128)S(1)} collective-permute-done((f32[8,8,128]{2,1,0:T(8,128)S(1)}, f32[8,8,128]{2,1,0:T(8,128)S(1)}, u32[]{:S(2)}, u32[]{:S(2)}) %collective-permute-start.5) | collective-permute-done | bytes 32800 | tf_op jit(solution)/shard_map/ppermute | solution.py:245
  19.4 1.3 %collective-permute-start.6 = (f32[4,8,128]{2,1,0:T(8,128)S(1)}, f32[4,8,128]{2,1,0:T(8,128)S(1)}, u32[]{:S(2)}, u32[]{:S(2)}) collective-permute-start(f32[4,8,128]{2,1,0:T(8,128)S(1)} %slice.64), channel_id=1, source_target_pairs={{0,3},{1,2},{2,1},{3,0},{4,7},{5,6},{6,5},{7,4},{8,11},{9,10},{10,... | collective-permute-start | bytes 49160 | tf_op jit(solution)/shard_map/ppermute | solution.py:245
  20.7 1.9 %collective-permute-done.6 = f32[4,8,128]{2,1,0:T(8,128)S(1)} collective-permute-done((f32[4,8,128]{2,1,0:T(8,128)S(1)}, f32[4,8,128]{2,1,0:T(8,128)S(1)}, u32[]{:S(2)}, u32[]{:S(2)}) %collective-permute-start.6) | collective-permute-done | bytes 16416 | tf_op jit(solution)/shard_map/ppermute | solution.py:245
  22.6 1.5 %collective-permute-start.7 = (f32[2,8,128]{2,1,0:T(8,128)S(1)}, f32[2,8,128]{2,1,0:T(8,128)S(1)}, u32[]{:S(2)}, u32[]{:S(2)}) collective-permute-start(f32[2,8,128]{2,1,0:T(8,128)S(1)} %slice.66), channel_id=1, source_target_pairs={{0,9},{1,8},{2,11},{3,10},{4,13},{5,12},{6,15},{7,14},{8,1},{9,0},... | collective-permute-start | bytes 24584 | tf_op jit(solution)/shard_map/ppermute | solution.py:245
  24.1 1.5 %collective-permute-done.7 = f32[2,8,128]{2,1,0:T(8,128)S(1)} collective-permute-done((f32[2,8,128]{2,1,0:T(8,128)S(1)}, f32[2,8,128]{2,1,0:T(8,128)S(1)}, u32[]{:S(2)}, u32[]{:S(2)}) %collective-permute-start.7) | collective-permute-done | bytes 8224 | tf_op jit(solution)/shard_map/ppermute | solution.py:245
  25.7 2.1 %collective-permute-start.8 = (f32[1,8,128]{2,1,0:T(8,128)S(1)}, f32[1,8,128]{2,1,0:T(8,128)S(1)}, u32[]{:S(2)}, u32[]{:S(2)}) collective-permute-start(f32[1,8,128]{2,1,0:T(8,128)S(1)} %slice.68), channel_id=1, source_target_pairs={{0,17},{1,16},{2,19},{3,18},{4,21},{5,20},{6,23},{7,22},{8,25},{9,... | collective-permute-start | bytes 12296 | tf_op jit(solution)/shard_map/ppermute | solution.py:245
  27.8 1.8 %collective-permute-done.8 = f32[1,8,128]{2,1,0:T(8,128)S(1)} collective-permute-done((f32[1,8,128]{2,1,0:T(8,128)S(1)}, f32[1,8,128]{2,1,0:T(8,128)S(1)}, u32[]{:S(2)}, u32[]{:S(2)}) %collective-permute-start.8) | collective-permute-done | bytes 4128 | tf_op jit(solution)/shard_map/ppermute | solution.py:245
  29.6 0.6 %fusion.4 = f32[8,128]{1,0:T(8,128)} fusion(f32[1,8,128]{2,1,0:T(8,128)S(1)} %collective-permute-done.8, f32[2,8,128]{2,1,0:T(8,128)S(1)} %fusion.1, f32[]{:T(128)S(6)} %convert_element_type.15), kind=kLoop, calls=%fused_computation.8 | loop fusion | flops 3072 | bytes 12292 | tf_op jit(solution)/shard_map/mul | solution.py:287
  (11 shorter events, 0.1 us)
Async XLA Ops:
  0.0 3.5 %copy-start = (s32[128]{0:T(128)S(1)}, s32[128]{0:T(128)}, u32[]{:S(2)}) copy-start(s32[128]{0:T(128)} %samples_ref.1) | copy-start | bytes 1540
  0.0 5.3 %collective-permute-start = (s32[128]{0:T(128)}, s32[128]{0:T(128)S(1)}, u32[]{:S(2)}, u32[]{:S(2)}) collective-permute-start(s32[128]{0:T(128)} %samples_ref.1), channel_id=1, source_target_pairs={{0,17},{1,16},{2,19},{3,18},{4,21},{5,20},{6,23},{7,22},{8,25},{9,... | collective-permute-start | bytes 1544 | tf_op jit(solution)/shard_map/ppermute | solution.py:245
  5.3 3.2 %collective-permute-start.1 = (s32[256]{0:T(256)S(1)}, s32[256]{0:T(256)S(1)}, u32[]{:S(2)}, u32[]{:S(2)}) collective-permute-start(s32[256]{0:T(256)S(1)} %pad_add_fusion.2), channel_id=1, source_target_pairs={{0,9},{1,8},{2,11},{3,10},{4,13},{5,12},{6,15},{7,14},{8,1},{9,0},... | collective-permute-start | bytes 3080 | tf_op jit(solution)/shard_map/ppermute | solution.py:245
  8.5 3.5 %collective-permute-start.3 = (f32[1024,256]{1,0:T(8,128)S(1)}, f32[1024,256]{1,0:T(8,128)S(1)}, u32[]{:S(2)}, u32[]{:S(2)}) collective-permute-start(f32[1024,256]{1,0:T(8,128)S(1)} %transform_low.1.mine_ref), channel_id=1, source_target_pairs={{0,1},{1,0},{2,3},{3,2},{4,5},{5,4},{6,7},{7,6},{8,9},{9,8},{10,11... | collective-permute-start | bytes 3145736 | tf_op jit(solution)/shard_map/ppermute | solution.py:245
  9.1 3.0 %collective-permute-start.2 = (s32[512]{0:T(512)S(1)}, s32[512]{0:T(512)S(1)}, u32[]{:S(2)}, u32[]{:S(2)}) collective-permute-start(s32[512]{0:T(512)S(1)} %pad_add_fusion.1), channel_id=1, source_target_pairs={{0,5},{1,4},{2,7},{3,6},{4,1},{5,0},{6,3},{7,2},{8,13},{9,12},{10,... | collective-permute-start | bytes 6152 | tf_op jit(solution)/shard_map/ppermute | solution.py:245
  12.1 3.1 %collective-permute-start.4 = (s32[1024]{0:T(1024)S(1)}, s32[1024]{0:T(1024)S(1)}, u32[]{:S(2)}, u32[]{:S(2)}) collective-permute-start(s32[1024]{0:T(1024)S(1)} %pad_add_fusion), channel_id=1, source_target_pairs={{0,3},{1,2},{2,1},{3,0},{4,7},{5,6},{6,5},{7,4},{8,11},{9,10},{10,... | collective-permute-start | bytes 12296 | tf_op jit(solution)/shard_map/ppermute | solution.py:245
  15.9 3.4 %collective-permute-start.5 = (f32[8,8,128]{2,1,0:T(8,128)S(1)}, f32[8,8,128]{2,1,0:T(8,128)S(1)}, u32[]{:S(2)}, u32[]{:S(2)}) collective-permute-start(f32[8,8,128]{2,1,0:T(8,128)S(1)} %gather.2), channel_id=1, source_target_pairs={{0,5},{1,4},{2,7},{3,6},{4,1},{5,0},{6,3},{7,2},{8,13},{9,12},{10,... | collective-permute-start | bytes 98312 | tf_op jit(solution)/shard_map/ppermute | solution.py:245
  19.4 3.2 %collective-permute-start.6 = (f32[4,8,128]{2,1,0:T(8,128)S(1)}, f32[4,8,128]{2,1,0:T(8,128)S(1)}, u32[]{:S(2)}, u32[]{:S(2)}) collective-permute-start(f32[4,8,128]{2,1,0:T(8,128)S(1)} %slice.64), channel_id=1, source_target_pairs={{0,3},{1,2},{2,1},{3,0},{4,7},{5,6},{6,5},{7,4},{8,11},{9,10},{10,... | collective-permute-start | bytes 49160 | tf_op jit(solution)/shard_map/ppermute | solution.py:245
  22.6 3.1 %collective-permute-start.7 = (f32[2,8,128]{2,1,0:T(8,128)S(1)}, f32[2,8,128]{2,1,0:T(8,128)S(1)}, u32[]{:S(2)}, u32[]{:S(2)}) collective-permute-start(f32[2,8,128]{2,1,0:T(8,128)S(1)} %slice.66), channel_id=1, source_target_pairs={{0,9},{1,8},{2,11},{3,10},{4,13},{5,12},{6,15},{7,14},{8,1},{9,0},... | collective-permute-start | bytes 24584 | tf_op jit(solution)/shard_map/ppermute | solution.py:245
  25.7 3.9 %collective-permute-start.8 = (f32[1,8,128]{2,1,0:T(8,128)S(1)}, f32[1,8,128]{2,1,0:T(8,128)S(1)}, u32[]{:S(2)}, u32[]{:S(2)}) collective-permute-start(f32[1,8,128]{2,1,0:T(8,128)S(1)} %slice.68), channel_id=1, source_target_pairs={{0,17},{1,16},{2,19},{3,18},{4,21},{5,20},{6,23},{7,22},{8,25},{9,... | collective-permute-start | bytes 12296 | tf_op jit(solution)/shard_map/ppermute | solution.py:245

commit v4 on v3

--- a/solution.py
+++ b/solution.py
@@ -21,6 +21,10 @@
 
 def parity(value):
     return bin(value).count("1") & 1
+
+
+def ladder_place(place, bits):
+    return sum((place >> i & 1) << (bits - 1 - i) for i in range(bits))
 
 
 def hadamard_rows(order):
@@ -208,20 +212,34 @@
                 out_ref[at_row + t] = total[:, i * samp : (i + 1) * samp]
 
 
-def gather_kernel(first, groups, even_ref, odd_ref, offsets_ref, known_ref, out_ref):
+def gather_kernel(first, groups, bits, turn, scale, even_ref, odd_ref, offsets_ref, known_ref, out_ref, late_ref):
     kept, cols, _ = known_ref.shape
-    out_ref[:kept] = known_ref[...]
-    pick(first, groups, cols, (even_ref, odd_ref), offsets_ref[...], out_ref, kept)
-
-
-def gather(first, groups, even, odd, offsets, known):
+    me = lax.axis_index("wide")
+
+    def place(place_of, value):
+        target = me ^ place_of
+        common = target & me
+        odd = common & 1
+        for bit in range(1, bits):
+            odd = odd ^ (common >> bit & 1)
+        out_ref[target ^ turn] = value * ((1 - 2 * odd).astype(jnp.float32) * scale)
+
+    pick(first, groups, cols, (even_ref, odd_ref), offsets_ref[...], late_ref, 0)
+    for t in range(kept):
+        place(ladder_place(t, bits), known_ref[t])
+    for t in range(late_ref.shape[0]):
+        place(ladder_place(first + t, bits), late_ref[t])
+
+
+def gather(first, groups, bits, turn, scale, even, odd, offsets, known):
     count, samp = offsets.shape
     kept, cols, _ = known.shape
     return pl.pallas_call(
-        functools.partial(gather_kernel, first, groups),
+        functools.partial(gather_kernel, first, groups, bits, turn, scale),
         out_shape=jax.ShapeDtypeStruct((kept + count, cols, samp), jnp.float32),
         in_specs=[vmem()] * 4,
         out_specs=vmem(),
+        scratch_shapes=[pltpu.VMEM((count, cols, samp), jnp.float32)],
         compiler_params=pltpu.CompilerParams(vmem_limit_bytes=VMEM_LIMIT),
         cost_estimate=pl.CostEstimate(
             flops=4 * groups * cols * LOW * count * samp, bytes_accessed=4 * groups * cols * LOW, transcendentals=0
@@ -238,7 +256,6 @@
     wide_bits = n_wide.bit_length() - 1
     narrow_bits = n_narrow.bit_length() - 1
     n_all = n_wide * n_narrow
-    wide_me = lax.axis_index("wide")
     narrow_me = lax.axis_index("narrow")
 
     def across(values, mask):
@@ -253,7 +270,7 @@
         panel = jnp.where(upper, partner - panel, panel + partner)
 
     groups = rows // LOW
-    half, quarter = n_wide // 2, n_wide // 4
+    half = n_wide // 2
     ladder = list(reversed(range(wide_bits)))
 
     def exchange(values, i):
@@ -277,14 +294,12 @@
     arrived, early = lax.optimization_barrier((arrived, early))
     late = arrived.reshape(half, samp)
 
-    far = gather(half + quarter, groups, even, odd, late[quarter:], early[quarter:])
-    near = gather(half, groups, even, odd, late[:quarter], early[:quarter])
-    for i in [wide_bits - 2, wide_bits - 1, *reversed(range(wide_bits - 2))]:
-        sign = (1 - 2 * (wide_me >> ladder[i] & 1)).astype(jnp.float32)
-        total = exchange(far, i) + sign * near
-        middle = total.shape[0] // 2
-        near, far = total[:middle], total[middle:]
-    return total[0] * jnp.float32(1.0 / math.sqrt(samp * n_all))
+    scale = 1.0 / math.sqrt(samp * n_all)
+    turn = n_wide - 1
+    pieces = gather(half, groups, wide_bits, turn, scale, even, odd, late, early)
+    teams = [[w * n_narrow + (n ^ parity(w)) for w in reversed(range(n_wide))] for n in range(n_narrow)]
+    pieces = lax.all_to_all(pieces, AXES, 0, 0, axis_index_groups=teams, tiled=True)
+    return jnp.sum(pieces, axis=0)
 
 
 def solution(mesh):

time: 30.4 us -> 27.8 us (0.914)
  blocking collectives: 0 us -> 10.5 us
  starting transfers between devices: 14.9 us -> 8.38 us
  waiting for transfers between devices: 9.05 us -> 2.67 us
    all_to_all x0 -> x1, blocking collectives: none -> 10.5 us  [per_device(): lax.all_to_all(pieces, AXES, 0, 0, axis_index_groups=teams, tiled=True)]
    ppermute x9 -> x5, starting transfers between devices: 14.9 us -> 8.38 us  [across(): return lax.ppermute(values, AXES, [(i, i ^ mask) for i in range(n_all)])]
    ppermute x9 -> x5, waiting for transfers between devices: 9.05 us -> 2.67 us  [across(): return lax.ppermute(values, AXES, [(i, i ^ mask) for i in range(n_all)])]
    reduce_sum x0 -> x1, other arithmetic: none -> 0.61 us  [per_device(): return jnp.sum(pieces, axis=0)]
    mul x1 -> x0, other arithmetic: 0.6 us -> none  [per_device(): return total[0] * jnp.float32(1.0 / math.sqrt(samp * n_all))]
    pallas_call x2 -> x1, Pallas kernels: 1.48 us -> 1.28 us  [gather(): pl.pallas_call(functools.partial(gather_kernel, first, groups, bits, turn...]
  transfers between devices with their start and end apart: 9 -> 5, of which waited for: 7 -> 3; matrix products, arithmetic and copies ran while one was open for 0% -> 0% of each run, Pallas kernels for 16% -> 15%
where the time goes in v4:
time: 27.8 us; the launch traced here: 27.6 us
  blocking collectives  10.5 us (38%)
  starting transfers between devices  8.38 us (30%)
  Pallas kernels  5.34 us (19%)
  waiting for transfers between devices  2.67 us (10%)
  other arithmetic  0.63 us (2%)
    all_to_all x1, blocking collectives, per_device(): lax.all_to_all(pieces, AXES, 0, 0, axis_index_groups=teams, tiled=True)  10.5 us
    ppermute x5, starting transfers between devices, across(): return lax.ppermute(values, AXES, [(i, i ^ mask) for i in range(n_all)])  8.38 us
    ppermute x5, waiting for transfers between devices, across(): return lax.ppermute(values, AXES, [(i, i ^ mask) for i in range(n_all)])  2.67 us
    pallas_call x1, Pallas kernels, transform_high(): pl.pallas_call(functools.partial(high_kernel, outer, inner), out_shape=[j...  1.8 us
    pallas_call x1, Pallas kernels, mix(): pl.pallas_call(functools.partial(mix_kernel, groups), out_shape=[jax.Shap...  1.76 us
    pallas_call x1, Pallas kernels, gather(): pl.pallas_call(functools.partial(gather_kernel, first, groups, bits, turn...  1.28 us
    reduce_sum x1, other arithmetic, per_device(): return jnp.sum(pieces, axis=0)  0.61 us
  transfers between devices with their start and end apart: 5, of which 3 were waited for; matrix products, arithmetic and copies ran while one was open for 0% of the time, Pallas kernels for 15%

profile of v4, /device:TPU:0, one launch (start us, length us, event | category | flops | bytes accessed | tf_op | source)
XLA Modules:
  0.0 27.6 jit_solution(11018877372863072572)
XLA Ops:
  0.0 0.0 copy-start
  0.0 3.5 %collective-permute-start = (s32[128]{0:T(128)}, s32[128]{0:T(128)S(1)}, u32[]{:S(2)}, u32[]{:S(2)}) collective-permute-start(s32[128]{0:T(128)} %samples_ref.1), channel_id=1, source_target_pairs={{0,17},{1,16},{2,19},{3,18},{4,21},{5,20},{6,23},{7,22},{8,25},{9,... | collective-permute-start | bytes 1544 | tf_op jit(solution)/shard_map/ppermute | solution.py:262
  3.5 0.0 copy-done
  3.5 1.8 %transform_high.1 = (bf16[1024,512]{1,0:T(8,128)(2,1)S(1)}, s32[128]{0:T(128)S(1)}) custom-call(f32[8,32768]{1,0:T(8,128)} %values_hbm.1, s32[256,128]{1,0:T(8,128)} %bitcast.5, s32[128]{0:T(128)S(1)} %copy-done), custom_call_target="tpu_custom_call" | custom-call | flops 268435456 | bytes 2621440 | tf_op jit(solution)/shard_map/transform_high/pallas_call | solution.py:134
  5.3 0.0 collective-permute-done
  5.3 1.9 %collective-permute-start.1 = (s32[256]{0:T(256)S(1)}, s32[256]{0:T(256)S(1)}, u32[]{:S(2)}, u32[]{:S(2)}) collective-permute-start(s32[256]{0:T(256)S(1)} %pad_add_fusion.2), channel_id=1, source_target_pairs={{0,9},{1,8},{2,11},{3,10},{4,13},{5,12},{6,15},{7,14},{8,1},{9,0},... | collective-permute-start | bytes 3080 | tf_op jit(solution)/shard_map/ppermute | solution.py:262
  7.2 0.5 %transform_low.1.mine_ref = f32[1024,256]{1,0:T(8,128)S(1)} custom-call(bf16[1024,512]{1,0:T(8,128)(2,1)S(1)} %get-tuple-element.23.parts_ref), custom_call_target="tpu_custom_call" | custom-call | flops 268435456 | bytes 2097152 | tf_op jit(solution)/shard_map/transform_low/pallas_call | solution.py:160
  7.7 0.8 %collective-permute-done.1 = s32[256]{0:T(256)S(1)} collective-permute-done((s32[256]{0:T(256)S(1)}, s32[256]{0:T(256)S(1)}, u32[]{:S(2)}, u32[]{:S(2)}) %collective-permute-start.1) | collective-permute-done | bytes 1056 | tf_op jit(solution)/shard_map/ppermute | solution.py:262
  8.5 0.5 %collective-permute-start.3 = (f32[1024,256]{1,0:T(8,128)S(1)}, f32[1024,256]{1,0:T(8,128)S(1)}, u32[]{:S(2)}, u32[]{:S(2)}) collective-permute-start(f32[1024,256]{1,0:T(8,128)S(1)} %transform_low.1.mine_ref), channel_id=1, source_target_pairs={{0,1},{1,0},{2,3},{3,2},{4,5},{5,4},{6,7},{7,6},{8,9},{9,8},{10,11... | collective-permute-start | bytes 3145736 | tf_op jit(solution)/shard_map/ppermute | solution.py:262
  9.1 1.2 %collective-permute-start.2 = (s32[512]{0:T(512)S(1)}, s32[512]{0:T(512)S(1)}, u32[]{:S(2)}, u32[]{:S(2)}) collective-permute-start(s32[512]{0:T(512)S(1)} %pad_add_fusion.1), channel_id=1, source_target_pairs={{0,5},{1,4},{2,7},{3,6},{4,1},{5,0},{6,3},{7,2},{8,13},{9,12},{10,... | collective-permute-start | bytes 6152 | tf_op jit(solution)/shard_map/ppermute | solution.py:262
  10.3 1.8 %collective-permute-done.2 = s32[512]{0:T(512)S(1)} collective-permute-done((s32[512]{0:T(512)S(1)}, s32[512]{0:T(512)S(1)}, u32[]{:S(2)}, u32[]{:S(2)}) %collective-permute-start.2) | collective-permute-done | bytes 2080 | tf_op jit(solution)/shard_map/ppermute | solution.py:262
  12.1 0.0 collective-permute-done.3.other_ref
  12.1 1.3 %collective-permute-start.4 = (s32[1024]{0:T(1024)S(1)}, s32[1024]{0:T(1024)S(1)}, u32[]{:S(2)}, u32[]{:S(2)}) collective-permute-start(s32[1024]{0:T(1024)S(1)} %pad_add_fusion), channel_id=1, source_target_pairs={{0,3},{1,2},{2,1},{3,0},{4,7},{5,6},{6,5},{7,4},{8,11},{9,10},{10,... | collective-permute-start | bytes 12296 | tf_op jit(solution)/shard_map/ppermute | solution.py:262
  13.4 1.8 %mix.1 = (bf16[1024,512]{1,0:T(8,128)(2,1)S(1)}, bf16[1024,512]{1,0:T(8,128)(2,1)S(1)}, f32[8,8,128]{2,1,0:T(8,128)S(1)}) custom-call(f32[1024,256]{1,0:T(8,128)S(1)} %transform_low.1.mine_ref, f32[1024,256]{1,0:T(8,128)S(1)} %collective-permute-done.3.other_ref, s32[8,128]{1,0:T(8,128)S(1)} %bitcast.3), custom_call_target="tpu_custom_call" | custom-call | flops 1073741824 | bytes 4194304 | tf_op jit(solution)/shard_map/mix/pallas_call | solution.py:174
  15.1 0.1 collective-permute-done.4
  15.2 1.3 %gather.1 = f32[16,8,128]{2,1,0:T(8,128)S(1)} custom-call(bf16[1024,512]{1,0:T(8,128)(2,1)S(1)} %get-tuple-element.28.even_ref, bf16[1024,512]{1,0:T(8,128)(2,1)S(1)} %get-tuple-element.29.odd_ref, s32[8,128]{1,0:T(8,128)S(1)} %bitcast.4, f32[8,8,128]{2,1,0:T(8,128)S(1)} %get-tuple-element.32.known_ref), custom_call_target="tpu_custom_call" | custom-call | flops 1073741824 | bytes 1048576 | tf_op jit(solution)/shard_map/gather/pallas_call | solution.py:237
  16.5 10.5 %all_to_all.5 = f32[16,8,128]{2,1,0:T(8,128)S(1)} all-to-all(f32[16,8,128]{2,1,0:T(8,128)S(1)} %gather.1), channel_id=1, replica_groups={{30,29,27,24,23,20,18,17,15,12,10,9,6,5,3,0},{31,28,26,25,22,21,19,16,1..., dimensions={0} | all-to-all | bytes 131072 | tf_op jit(solution)/shard_map/all_to_all | solution.py:301
  27.0 0.6 %reduce_sum.9 = f32[8,128]{1,0:T(8,128)} reduce(f32[16,8,128]{2,1,0:T(8,128)S(1)} %all_to_all.5, f32[]{:T(128)} %constant.0.clone.1), dimensions={0}, to_apply=%region_0.0 | reduce | flops 15360 | bytes 69636 | tf_op jit(solution)/shard_map/reduce_sum | solution.py:302
  (3 shorter events, 0.0 us)
Async XLA Ops:
  0.0 3.5 %copy-start = (s32[128]{0:T(128)S(1)}, s32[128]{0:T(128)}, u32[]{:S(2)}) copy-start(s32[128]{0:T(128)} %samples_ref.1) | copy-start | bytes 1540
  0.0 5.3 %collective-permute-start = (s32[128]{0:T(128)}, s32[128]{0:T(128)S(1)}, u32[]{:S(2)}, u32[]{:S(2)}) collective-permute-start(s32[128]{0:T(128)} %samples_ref.1), channel_id=1, source_target_pairs={{0,17},{1,16},{2,19},{3,18},{4,21},{5,20},{6,23},{7,22},{8,25},{9,... | collective-permute-start | bytes 1544 | tf_op jit(solution)/shard_map/ppermute | solution.py:262
  5.3 3.2 %collective-permute-start.1 = (s32[256]{0:T(256)S(1)}, s32[256]{0:T(256)S(1)}, u32[]{:S(2)}, u32[]{:S(2)}) collective-permute-start(s32[256]{0:T(256)S(1)} %pad_add_fusion.2), channel_id=1, source_target_pairs={{0,9},{1,8},{2,11},{3,10},{4,13},{5,12},{6,15},{7,14},{8,1},{9,0},... | collective-permute-start | bytes 3080 | tf_op jit(solution)/shard_map/ppermute | solution.py:262
  8.5 3.5 %collective-permute-start.3 = (f32[1024,256]{1,0:T(8,128)S(1)}, f32[1024,256]{1,0:T(8,128)S(1)}, u32[]{:S(2)}, u32[]{:S(2)}) collective-permute-start(f32[1024,256]{1,0:T(8,128)S(1)} %transform_low.1.mine_ref), channel_id=1, source_target_pairs={{0,1},{1,0},{2,3},{3,2},{4,5},{5,4},{6,7},{7,6},{8,9},{9,8},{10,11... | collective-permute-start | bytes 3145736 | tf_op jit(solution)/shard_map/ppermute | solution.py:262
  9.1 3.0 %collective-permute-start.2 = (s32[512]{0:T(512)S(1)}, s32[512]{0:T(512)S(1)}, u32[]{:S(2)}, u32[]{:S(2)}) collective-permute-start(s32[512]{0:T(512)S(1)} %pad_add_fusion.1), channel_id=1, source_target_pairs={{0,5},{1,4},{2,7},{3,6},{4,1},{5,0},{6,3},{7,2},{8,13},{9,12},{10,... | collective-permute-start | bytes 6152 | tf_op jit(solution)/shard_map/ppermute | solution.py:262
  12.1 3.1 %collective-permute-start.4 = (s32[1024]{0:T(1024)S(1)}, s32[1024]{0:T(1024)S(1)}, u32[]{:S(2)}, u32[]{:S(2)}) collective-permute-start(s32[1024]{0:T(1024)S(1)} %pad_add_fusion), channel_id=1, source_target_pairs={{0,3},{1,2},{2,1},{3,0},{4,7},{5,6},{6,5},{7,4},{8,11},{9,10},{10,... | collective-permute-start | bytes 12296 | tf_op jit(solution)/shard_map/ppermute | solution.py:262

commit v5 on v4

--- a/solution.py
+++ b/solution.py
@@ -81,7 +81,7 @@
     lax.fori_loop(0, inner, step, 0)
 
 
-def high_kernel(outer, inner, values_hbm, signs_hbm, samples_ref, parts_ref, list_ref, values_ref, signs_ref, mid, sems):
+def transform_kernel(outer, inner, values_hbm, signs_hbm, samples_ref, out_ref, list_ref, values_ref, signs_ref, mid, parts, sems):
     cols, rows = values_hbm.shape
     block = rows // outer
     signs_copy = pltpu.make_async_copy(signs_hbm, signs_ref, sems.at[outer])
@@ -95,18 +95,17 @@
     for copy in copies:
         copy.start()
     list_ref[...] = samples_ref[...]
+    matrix = hadamard_rows(LOW)
     signs_copy.wait()
     for a, copy in enumerate(copies):
         copy.wait()
         first_pass(outer, inner, values_ref, signs_ref, mid, a)
-    second_pass(outer, inner, cols, mid, parts_ref)
-
-
-def low_kernel(parts_ref, out_ref):
-    out_ref[...] = jnp.dot(parts_ref[...], hadamard_rows(LOW), preferred_element_type=jnp.float32)
-
-
-def mix_kernel(groups, mine_ref, other_ref, offsets_ref, even_ref, odd_ref, out_ref):
+    second_pass(outer, inner, cols, mid, parts)
+    out_ref[...] = jnp.dot(parts[...], matrix, preferred_element_type=jnp.float32)
+
+
+def mix_kernel(firsts, groups, mine_ref, other_ref, *refs):
+    *offset_refs, even_ref, odd_ref, out_ref = refs
     core = lax.axis_index("narrow") & 1
     flip = (1 - 2 * core).astype(jnp.float32)
 
@@ -118,7 +117,10 @@
         return carry
 
     lax.fori_loop(0, mine_ref.shape[0] // MIX_ROWS, step, 0)
-    pick(0, groups, mine_ref.shape[0] // groups, (even_ref, odd_ref), offsets_ref[...], out_ref, 0)
+    at_row = 0
+    for first, offsets_ref in zip(firsts, offset_refs):
+        pick(first, groups, mine_ref.shape[0] // groups, (even_ref, odd_ref), offsets_ref[...], out_ref, at_row)
+        at_row += offsets_ref.shape[0]
 
 
 def split_groups(groups):
@@ -126,15 +128,15 @@
     return outer, groups // outer
 
 
-def transform_high(values, signs, samples):
+def transform(values, signs, samples):
     cols, rows = values.shape
     groups = rows // LOW
     outer, inner = split_groups(groups)
     hbm = pl.BlockSpec(memory_space=pltpu.HBM)
     return pl.pallas_call(
-        functools.partial(high_kernel, outer, inner),
+        functools.partial(transform_kernel, outer, inner),
         out_shape=[
-            jax.ShapeDtypeStruct((groups * cols, 2 * LOW), jnp.bfloat16),
+            jax.ShapeDtypeStruct((groups * cols, LOW), jnp.float32),
             jax.ShapeDtypeStruct(samples.shape, samples.dtype),
         ],
         in_specs=[hbm, hbm, vmem()],
@@ -143,11 +145,12 @@
             pltpu.VMEM(values.shape, jnp.float32),
             pltpu.VMEM((rows // LANES, LANES), jnp.int32),
             pltpu.VMEM((groups * cols, LOW), jnp.float32),
+            pltpu.VMEM((groups * cols, 2 * LOW), jnp.bfloat16),
             pltpu.SemaphoreType.DMA((outer + 1,)),
         ],
         compiler_params=pltpu.CompilerParams(vmem_limit_bytes=VMEM_LIMIT),
         cost_estimate=pl.CostEstimate(flops=4 * cols * rows * LOW, bytes_accessed=10 * cols * rows, transcendentals=0),
-        name="transform_high",
+        name="transform",
     )(
         pltpu.with_memory_space_constraint(values, pltpu.HBM),
         pltpu.with_memory_space_constraint(signs.reshape(rows // LANES, LANES), pltpu.HBM),
@@ -155,37 +158,28 @@
     )
 
 
-def transform_low(parts):
-    rows, width = parts.shape
+def gather_cost(groups, cols, count, samp):
+    return pl.CostEstimate(
+        flops=4 * groups * cols * LOW * count * samp, bytes_accessed=4 * groups * cols * LOW, transcendentals=0
+    )
+
+
+def mix(firsts, groups, mine, other, lists):
+    rows, low = mine.shape
+    count, samp = sum(offsets.shape[0] for offsets in lists), lists[0].shape[1]
     return pl.pallas_call(
-        low_kernel,
-        out_shape=jax.ShapeDtypeStruct((rows, width // 2), jnp.float32),
-        in_specs=[vmem()],
-        out_specs=vmem(),
-        compiler_params=pltpu.CompilerParams(vmem_limit_bytes=VMEM_LIMIT),
-        cost_estimate=pl.CostEstimate(flops=rows * width * width, bytes_accessed=4 * rows * width, transcendentals=0),
-        name="transform_low",
-    )(parts)
-
-
-def mix(mine, other, groups, offsets):
-    rows, low = mine.shape
-    count, samp = offsets.shape
-    return pl.pallas_call(
-        functools.partial(mix_kernel, groups),
+        functools.partial(mix_kernel, firsts, groups),
         out_shape=[
             jax.ShapeDtypeStruct((rows, 2 * low), jnp.bfloat16),
             jax.ShapeDtypeStruct((rows, 2 * low), jnp.bfloat16),
             jax.ShapeDtypeStruct((count, rows // groups, samp), jnp.float32),
         ],
-        in_specs=[vmem()] * 3,
+        in_specs=[vmem()] * (2 + len(lists)),
         out_specs=[vmem()] * 3,
         compiler_params=pltpu.CompilerParams(vmem_limit_bytes=VMEM_LIMIT),
-        cost_estimate=pl.CostEstimate(
-            flops=4 * rows * low * count * samp, bytes_accessed=16 * rows * low, transcendentals=0
-        ),
+        cost_estimate=gather_cost(groups, rows // groups, count, samp),
         name="mix",
-    )(mine, other, offsets)
+    )(mine, other, *lists)
 
 
 def pick(first, groups, cols, tables, offsets, out_ref, at_row):
@@ -212,8 +206,17 @@
                 out_ref[at_row + t] = total[:, i * samp : (i + 1) * samp]
 
 
-def gather_kernel(first, groups, bits, turn, scale, even_ref, odd_ref, offsets_ref, known_ref, out_ref, late_ref):
-    kept, cols, _ = known_ref.shape
+def early_kernel(firsts, groups, even_ref, odd_ref, *refs):
+    *offset_refs, out_ref = refs
+    at_row = 0
+    for first, offsets_ref in zip(firsts, offset_refs):
+        pick(first, groups, out_ref.shape[1], (even_ref, odd_ref), offsets_ref[...], out_ref, at_row)
+        at_row += offsets_ref.shape[0]
+
+
+def gather_kernel(first, groups, bits, first_piece, scale, even_ref, odd_ref, offsets_ref, *refs):
+    *known_refs, out_ref, late_ref = refs
+    cols = out_ref.shape[1]
     me = lax.axis_index("wide")
 
     def place(place_of, value):
@@ -222,30 +225,43 @@
         odd = common & 1
         for bit in range(1, bits):
             odd = odd ^ (common >> bit & 1)
-        out_ref[target ^ turn] = value * ((1 - 2 * odd).astype(jnp.float32) * scale)
+        out_ref[target - first_piece & (1 << bits) - 1] = value * ((1 - 2 * odd).astype(jnp.float32) * scale)
 
     pick(first, groups, cols, (even_ref, odd_ref), offsets_ref[...], late_ref, 0)
-    for t in range(kept):
-        place(ladder_place(t, bits), known_ref[t])
-    for t in range(late_ref.shape[0]):
-        place(ladder_place(first + t, bits), late_ref[t])
-
-
-def gather(first, groups, bits, turn, scale, even, odd, offsets, known):
+    at_place = 0
+    for ref in (*known_refs, late_ref):
+        for t in range(ref.shape[0]):
+            place(ladder_place(at_place, bits), ref[t])
+            at_place += 1
+
+
+def gather_early(firsts, groups, even, odd, lists):
+    count, samp = sum(offsets.shape[0] for offsets in lists), lists[0].shape[1]
+    cols = even.shape[0] // groups
+    return pl.pallas_call(
+        functools.partial(early_kernel, firsts, groups),
+        out_shape=jax.ShapeDtypeStruct((count, cols, samp), jnp.float32),
+        in_specs=[vmem()] * (2 + len(lists)),
+        out_specs=vmem(),
+        compiler_params=pltpu.CompilerParams(vmem_limit_bytes=VMEM_LIMIT),
+        cost_estimate=gather_cost(groups, cols, count, samp),
+        name="gather_early",
+    )(even, odd, *lists)
+
+
+def gather(first, groups, bits, first_piece, scale, even, odd, offsets, known):
     count, samp = offsets.shape
-    kept, cols, _ = known.shape
+    cols = even.shape[0] // groups
     return pl.pallas_call(
-        functools.partial(gather_kernel, first, groups, bits, turn, scale),
-        out_shape=jax.ShapeDtypeStruct((kept + count, cols, samp), jnp.float32),
-        in_specs=[vmem()] * 4,
+        functools.partial(gather_kernel, first, groups, bits, first_piece, scale),
+        out_shape=jax.ShapeDtypeStruct((first + count, cols, samp), jnp.float32),
+        in_specs=[vmem()] * (3 + len(known)),
         out_specs=vmem(),
         scratch_shapes=[pltpu.VMEM((count, cols, samp), jnp.float32)],
         compiler_params=pltpu.CompilerParams(vmem_limit_bytes=VMEM_LIMIT),
-        cost_estimate=pl.CostEstimate(
-            flops=4 * groups * cols * LOW * count * samp, bytes_accessed=4 * groups * cols * LOW, transcendentals=0
-        ),
+        cost_estimate=gather_cost(groups, cols, count, samp),
         name="gather",
-    )(even, odd, offsets, known)
+    )(even, odd, offsets, *known)
 
 
 def per_device(panel, signs, samples):
@@ -270,34 +286,33 @@
         panel = jnp.where(upper, partner - panel, panel + partner)
 
     groups = rows // LOW
-    half = n_wide // 2
+    half, quarter = n_wide // 2, n_wide // 4
     ladder = list(reversed(range(wide_bits)))
+    last = wide_bits - 1
 
     def exchange(values, i):
         return across(values, n_narrow << ladder[i] | 1)
 
     arrived = exchange(samples, 0)
-    parts, listed = transform_high(panel, signs, samples)
-    arrived, parts, listed = lax.optimization_barrier((arrived, parts, listed))
+    mine, listed = transform(panel, signs, samples)
+    arrived, mine, listed = lax.optimization_barrier((arrived, mine, listed))
+    other = across(mine, 1)
     asked = jnp.concatenate([listed, arrived])
-    for i in range(1, wide_bits):
-        if i == 2:
-            asked, mine = lax.optimization_barrier((asked, mine))
-            other = across(mine, 1)
-        if i == wide_bits - 1:
-            asked, other = lax.optimization_barrier((asked, other))
-            even, odd, early = mix(mine, other, groups, asked.reshape(half, samp))
-        arrived = exchange(asked, i)
-        if i == 1:
-            mine = transform_low(parts)
-        asked = jnp.concatenate([asked, arrived])
-    arrived, early = lax.optimization_barrier((arrived, early))
-    late = arrived.reshape(half, samp)
+    for i in range(1, last - 1):
+        asked = jnp.concatenate([asked, exchange(asked, i)])
+    arrived = exchange(asked, last - 1)
+    even, odd, early = mix((0,), groups, mine, other, [asked.reshape(quarter, samp)])
+    asked, arrived, even, odd, early = lax.optimization_barrier((asked, arrived, even, odd, early))
+    late = exchange(jnp.concatenate([asked, arrived]), last)
+    early = [early, gather_early((quarter,), groups, even, odd, [arrived.reshape(quarter, samp)])]
+    late, *early = lax.optimization_barrier((late, *early))
+    late = late.reshape(half, samp)
 
     scale = 1.0 / math.sqrt(samp * n_all)
-    turn = n_wide - 1
-    pieces = gather(half, groups, wide_bits, turn, scale, even, odd, late, early)
-    teams = [[w * n_narrow + (n ^ parity(w)) for w in reversed(range(n_wide))] for n in range(n_narrow)]
+    first_piece = n_wide * 11 // 16
+    pieces = gather(half, groups, wide_bits, first_piece, scale, even, odd, late, early)
+    order = [(p + first_piece) % n_wide for p in range(n_wide)]
+    teams = [[w * n_narrow + (n ^ parity(w)) for w in order] for n in range(n_narrow)]
     pieces = lax.all_to_all(pieces, AXES, 0, 0, axis_index_groups=teams, tiled=True)
     return jnp.sum(pieces, axis=0)
 

time: 27.8 us -> 27.3 us (0.982)
  blocking collectives: 10.5 us -> 9.64 us
  waiting for transfers between devices: 2.67 us -> 3.32 us
  starting transfers between devices: 8.38 us -> 7.94 us
    all_to_all x1, blocking collectives: 10.5 us -> 9.64 us  [per_device(): lax.all_to_all(pieces, AXES, 0, 0, axis_index_groups=teams, tiled=True)]
    ppermute x5, waiting for transfers between devices: 2.67 us -> 3.32 us  [across(): return lax.ppermute(values, AXES, [(i, i ^ mask) for i in range(n_all)])]
    ppermute x5, starting transfers between devices: 8.38 us -> 7.94 us  [across(): return lax.ppermute(values, AXES, [(i, i ^ mask) for i in range(n_all)])]
where the time goes in v5:
time: 27.3 us; the launch traced here: 27.1 us
  blocking collectives  9.64 us (35%)
  starting transfers between devices  7.94 us (29%)
  Pallas kernels  5.47 us (20%)
  waiting for transfers between devices  3.32 us (12%)
  other arithmetic  0.62 us (2%)
    all_to_all x1, blocking collectives, per_device(): lax.all_to_all(pieces, AXES, 0, 0, axis_index_groups=teams, tiled=True)  9.64 us
    ppermute x5, starting transfers between devices, across(): return lax.ppermute(values, AXES, [(i, i ^ mask) for i in range(n_all)])  7.94 us
    ppermute x5, waiting for transfers between devices, across(): return lax.ppermute(values, AXES, [(i, i ^ mask) for i in range(n_all)])  3.32 us
    pallas_call x1, Pallas kernels, transform(): pl.pallas_call(functools.partial(transform_kernel, outer, inner), out_sha...  2.23 us
    pallas_call x1, Pallas kernels, gather(): pl.pallas_call(functools.partial(gather_kernel, first, groups, bits, firs...  1.28 us
    pallas_call x1, Pallas kernels, mix(): pl.pallas_call(functools.partial(mix_kernel, firsts, groups), out_shape=[...  1.21 us
    pallas_call x1, Pallas kernels, gather_early(): pl.pallas_call(functools.partial(early_kernel, firsts, groups), out_shape...  0.74 us
    reduce_sum x1, other arithmetic, per_device(): return jnp.sum(pieces, axis=0)  0.61 us
  transfers between devices with their start and end apart: 5, of which 3 were waited for; matrix products, arithmetic and copies ran while one was open for 0% of the time, Pallas kernels for 15%

profile of v5, /device:TPU:0, one launch (start us, length us, event | category | flops | bytes accessed | tf_op | source)
XLA Modules:
  0.0 27.1 jit_solution(5376280859421327123)
XLA Ops:
  0.0 0.0 copy-start
  0.0 3.5 %collective-permute-start = (s32[128]{0:T(128)}, s32[128]{0:T(128)S(1)}, u32[]{:S(2)}, u32[]{:S(2)}) collective-permute-start(s32[128]{0:T(128)} %samples_ref.1), channel_id=1, source_target_pairs={{0,17},{1,16},{2,19},{3,18},{4,21},{5,20},{6,23},{7,22},{8,25},{9,... | collective-permute-start | bytes 1544 | tf_op jit(solution)/shard_map/ppermute | solution.py:278
  3.5 0.0 copy-done
  3.5 2.2 %transform.1 = (f32[1024,256]{1,0:T(8,128)S(1)}, s32[128]{0:T(128)S(1)}) custom-call(f32[8,32768]{1,0:T(8,128)} %values_hbm.1, s32[256,128]{1,0:T(8,128)} %bitcast.7, s32[128]{0:T(128)S(1)} %copy-done), custom_call_target="tpu_custom_call" | custom-call | flops 268435456 | bytes 2621440 | tf_op jit(solution)/shard_map/transform/pallas_call | solution.py:136
  5.7 0.0 collective-permute-done
  5.7 0.7 %collective-permute-start.3 = (f32[1024,256]{1,0:T(8,128)S(1)}, f32[1024,256]{1,0:T(8,128)S(1)}, u32[]{:S(2)}, u32[]{:S(2)}) collective-permute-start(f32[1024,256]{1,0:T(8,128)S(1)} %get-tuple-element.25.mine_ref), channel_id=1, source_target_pairs={{0,1},{1,0},{2,3},{3,2},{4,5},{5,4},{6,7},{7,6},{8,9},{9,8},{10,11... | collective-permute-start | bytes 3145736 | tf_op jit(solution)/shard_map/ppermute | solution.py:278
  6.5 1.3 %collective-permute-start.1 = (s32[256]{0:T(256)S(1)}, s32[256]{0:T(256)S(1)}, u32[]{:S(2)}, u32[]{:S(2)}) collective-permute-start(s32[256]{0:T(256)S(1)} %pad_add_fusion.1), channel_id=1, source_target_pairs={{0,9},{1,8},{2,11},{3,10},{4,13},{5,12},{6,15},{7,14},{8,1},{9,0},... | collective-permute-start | bytes 3080 | tf_op jit(solution)/shard_map/ppermute | solution.py:278
  7.8 1.7 %collective-permute-done.1 = s32[256]{0:T(256)S(1)} collective-permute-done((s32[256]{0:T(256)S(1)}, s32[256]{0:T(256)S(1)}, u32[]{:S(2)}, u32[]{:S(2)}) %collective-permute-start.1) | collective-permute-done | bytes 1056 | tf_op jit(solution)/shard_map/ppermute | solution.py:278
  9.5 1.2 %collective-permute-start.2 = (s32[512]{0:T(512)S(1)}, s32[512]{0:T(512)S(1)}, u32[]{:S(2)}, u32[]{:S(2)}) collective-permute-start(s32[512]{0:T(512)S(1)} %constant_dynamic-update-slice_fusion), channel_id=1, source_target_pairs={{0,5},{1,4},{2,7},{3,6},{4,1},{5,0},{6,3},{7,2},{8,13},{9,12},{10,... | collective-permute-start | bytes 6152 | tf_op jit(solution)/shard_map/ppermute | solution.py:278
  10.7 0.0 collective-permute-done.3.other_ref
  10.7 1.2 %mix.1 = (bf16[1024,512]{1,0:T(8,128)(2,1)S(1)}, bf16[1024,512]{1,0:T(8,128)(2,1)S(1)}, f32[4,8,128]{2,1,0:T(8,128)S(1)}) custom-call(f32[1024,256]{1,0:T(8,128)S(1)} %get-tuple-element.25.mine_ref, f32[1024,256]{1,0:T(8,128)S(1)} %collective-permute-done.3.other_ref, s32[4,128]{1,0:T(4,128)S(1)} %bitcast.5), custom_call_target="tpu_custom_call" | custom-call | flops 536870912 | bytes 1048576 | tf_op jit(solution)/shard_map/mix/pallas_call | solution.py:170
  12.0 0.5 %collective-permute-done.2 = s32[512]{0:T(512)S(1)} collective-permute-done((s32[512]{0:T(512)S(1)}, s32[512]{0:T(512)S(1)}, u32[]{:S(2)}, u32[]{:S(2)}) %collective-permute-start.2) | collective-permute-done | bytes 2080 | tf_op jit(solution)/shard_map/ppermute | solution.py:278
  12.5 1.2 %collective-permute-start.4 = (s32[1024]{0:T(1024)S(1)}, s32[1024]{0:T(1024)S(1)}, u32[]{:S(2)}, u32[]{:S(2)}) collective-permute-start(s32[1024]{0:T(1024)S(1)} %pad_add_fusion), channel_id=1, source_target_pairs={{0,3},{1,2},{2,1},{3,0},{4,7},{5,6},{6,5},{7,4},{8,11},{9,10},{10,... | collective-permute-start | bytes 12296 | tf_op jit(solution)/shard_map/ppermute | solution.py:278
  13.7 0.7 %gather_early.1.refs_1_ = f32[4,8,128]{2,1,0:T(8,128)S(1)} custom-call(bf16[1024,512]{1,0:T(8,128)(2,1)S(1)} %get-tuple-element.29.even_ref, bf16[1024,512]{1,0:T(8,128)(2,1)S(1)} %get-tuple-element.30.odd_ref, s32[4,128]{1,0:T(4,128)S(1)} %bitcast.4), custom_call_target="tpu_custom_call" | custom-call | flops 536870912 | bytes 1048576 | tf_op jit(solution)/shard_map/gather_early/pallas_call | solution.py:241
  14.5 1.1 %collective-permute-done.4 = s32[1024]{0:T(1024)S(1)} collective-permute-done((s32[1024]{0:T(1024)S(1)}, s32[1024]{0:T(1024)S(1)}, u32[]{:S(2)}, u32[]{:S(2)}) %collective-permute-start.4) | collective-permute-done | bytes 4128 | tf_op jit(solution)/shard_map/ppermute | solution.py:278
  15.5 1.3 %gather.1 = f32[16,8,128]{2,1,0:T(8,128)S(1)} custom-call(bf16[1024,512]{1,0:T(8,128)(2,1)S(1)} %get-tuple-element.29.even_ref, bf16[1024,512]{1,0:T(8,128)(2,1)S(1)} %get-tuple-element.30.odd_ref, s32[8,128]{1,0:T(8,128)S(1)} %bitcast.6, f32[4,8,128]{2,1,0:T(8,128)S(1)} %get-tuple-element.35.refs_0_, f32[4,8,128]{2,1,0:T(8,128)S(1)} %gather_early.1.refs_1_), custom_call_target="tpu_custom_call" | custom-call | flops 1073741824 | bytes 1048576 | tf_op jit(solution)/shard_map/gather/pallas_call | solution.py:255
  16.8 9.6 %all_to_all.5 = f32[16,8,128]{2,1,0:T(8,128)S(1)} all-to-all(f32[16,8,128]{2,1,0:T(8,128)S(1)} %gather.1), channel_id=1, replica_groups={{23,24,27,29,30,0,3,5,6,9,10,12,15,17,18,20},{22,25,26,28,31,1,2,4,7,8,..., dimensions={0} | all-to-all | bytes 131072 | tf_op jit(solution)/shard_map/all_to_all | solution.py:316
  26.5 0.6 %reduce_sum.9 = f32[8,128]{1,0:T(8,128)} reduce(f32[16,8,128]{2,1,0:T(8,128)S(1)} %all_to_all.5, f32[]{:T(128)} %constant.0.clone.1), dimensions={0}, to_apply=%region_0.0 | reduce | flops 15360 | bytes 69636 | tf_op jit(solution)/shard_map/reduce_sum | solution.py:317
  (6 shorter events, 0.1 us)
Async XLA Ops:
  0.0 3.5 %copy-start = (s32[128]{0:T(128)S(1)}, s32[128]{0:T(128)}, u32[]{:S(2)}) copy-start(s32[128]{0:T(128)} %samples_ref.1) | copy-start | bytes 1540
  0.0 5.7 %collective-permute-start = (s32[128]{0:T(128)}, s32[128]{0:T(128)S(1)}, u32[]{:S(2)}, u32[]{:S(2)}) collective-permute-start(s32[128]{0:T(128)} %samples_ref.1), channel_id=1, source_target_pairs={{0,17},{1,16},{2,19},{3,18},{4,21},{5,20},{6,23},{7,22},{8,25},{9,... | collective-permute-start | bytes 1544 | tf_op jit(solution)/shard_map/ppermute | solution.py:278
  5.7 5.0 %collective-permute-start.3 = (f32[1024,256]{1,0:T(8,128)S(1)}, f32[1024,256]{1,0:T(8,128)S(1)}, u32[]{:S(2)}, u32[]{:S(2)}) collective-permute-start(f32[1024,256]{1,0:T(8,128)S(1)} %get-tuple-element.25.mine_ref), channel_id=1, source_target_pairs={{0,1},{1,0},{2,3},{3,2},{4,5},{5,4},{6,7},{7,6},{8,9},{9,8},{10,11... | collective-permute-start | bytes 3145736 | tf_op jit(solution)/shard_map/ppermute | solution.py:278
  6.5 3.0 %collective-permute-start.1 = (s32[256]{0:T(256)S(1)}, s32[256]{0:T(256)S(1)}, u32[]{:S(2)}, u32[]{:S(2)}) collective-permute-start(s32[256]{0:T(256)S(1)} %pad_add_fusion.1), channel_id=1, source_target_pairs={{0,9},{1,8},{2,11},{3,10},{4,13},{5,12},{6,15},{7,14},{8,1},{9,0},... | collective-permute-start | bytes 3080 | tf_op jit(solution)/shard_map/ppermute | solution.py:278
  9.5 3.0 %collective-permute-start.2 = (s32[512]{0:T(512)S(1)}, s32[512]{0:T(512)S(1)}, u32[]{:S(2)}, u32[]{:S(2)}) collective-permute-start(s32[512]{0:T(512)S(1)} %constant_dynamic-update-slice_fusion), channel_id=1, source_target_pairs={{0,5},{1,4},{2,7},{3,6},{4,1},{5,0},{6,3},{7,2},{8,13},{9,12},{10,... | collective-permute-start | bytes 6152 | tf_op jit(solution)/shard_map/ppermute | solution.py:278
  12.5 3.0 %collective-permute-start.4 = (s32[1024]{0:T(1024)S(1)}, s32[1024]{0:T(1024)S(1)}, u32[]{:S(2)}, u32[]{:S(2)}) collective-permute-start(s32[1024]{0:T(1024)S(1)} %pad_add_fusion), channel_id=1, source_target_pairs={{0,3},{1,2},{2,1},{3,0},{4,7},{5,6},{6,5},{7,4},{8,11},{9,10},{10,... | collective-permute-start | bytes 12296 | tf_op jit(solution)/shard_map/ppermute | solution.py:278

commit v6 on v5

--- a/solution.py
+++ b/solution.py
@@ -104,8 +104,7 @@
     out_ref[...] = jnp.dot(parts[...], matrix, preferred_element_type=jnp.float32)
 
 
-def mix_kernel(firsts, groups, mine_ref, other_ref, *refs):
-    *offset_refs, even_ref, odd_ref, out_ref = refs
+def mix_kernel(mine_ref, other_ref, even_ref, odd_ref):
     core = lax.axis_index("narrow") & 1
     flip = (1 - 2 * core).astype(jnp.float32)
 
@@ -117,10 +116,6 @@
         return carry
 
     lax.fori_loop(0, mine_ref.shape[0] // MIX_ROWS, step, 0)
-    at_row = 0
-    for first, offsets_ref in zip(firsts, offset_refs):
-        pick(first, groups, mine_ref.shape[0] // groups, (even_ref, odd_ref), offsets_ref[...], out_ref, at_row)
-        at_row += offsets_ref.shape[0]
 
 
 def split_groups(groups):
@@ -164,22 +159,17 @@
     )
 
 
-def mix(firsts, groups, mine, other, lists):
+def mix(mine, other):
     rows, low = mine.shape
-    count, samp = sum(offsets.shape[0] for offsets in lists), lists[0].shape[1]
     return pl.pallas_call(
-        functools.partial(mix_kernel, firsts, groups),
-        out_shape=[
-            jax.ShapeDtypeStruct((rows, 2 * low), jnp.bfloat16),
-            jax.ShapeDtypeStruct((rows, 2 * low), jnp.bfloat16),
-            jax.ShapeDtypeStruct((count, rows // groups, samp), jnp.float32),
-        ],
-        in_specs=[vmem()] * (2 + len(lists)),
-        out_specs=[vmem()] * 3,
+        mix_kernel,
+        out_shape=[jax.ShapeDtypeStruct((rows, 2 * low), jnp.bfloat16)] * 2,
+        in_specs=[vmem()] * 2,
+        out_specs=[vmem()] * 2,
         compiler_params=pltpu.CompilerParams(vmem_limit_bytes=VMEM_LIMIT),
-        cost_estimate=gather_cost(groups, rows // groups, count, samp),
+        cost_estimate=pl.CostEstimate(flops=8 * rows * low, bytes_accessed=16 * rows * low, transcendentals=0),
         name="mix",
-    )(mine, other, *lists)
+    )(mine, other)
 
 
 def pick(first, groups, cols, tables, offsets, out_ref, at_row):
@@ -299,18 +289,22 @@
     other = across(mine, 1)
     asked = jnp.concatenate([listed, arrived])
     for i in range(1, last - 1):
-        asked = jnp.concatenate([asked, exchange(asked, i)])
+        arrived = exchange(asked, i)
+        if i == last - 2:
+            even, odd = mix(mine, other)
+            asked, arrived, even, odd = lax.optimization_barrier((asked, arrived, even, odd))
+        asked = jnp.concatenate([asked, arrived])
     arrived = exchange(asked, last - 1)
-    even, odd, early = mix((0,), groups, mine, other, [asked.reshape(quarter, samp)])
-    asked, arrived, even, odd, early = lax.optimization_barrier((asked, arrived, even, odd, early))
-    late = exchange(jnp.concatenate([asked, arrived]), last)
-    early = [early, gather_early((quarter,), groups, even, odd, [arrived.reshape(quarter, samp)])]
+    ahead = exchange(asked, last)
+    late = exchange(arrived, last)
+    lists = [asked.reshape(quarter, samp), arrived.reshape(quarter, samp), ahead.reshape(quarter, samp)]
+    early = [gather_early((0, quarter, half), groups, even, odd, lists)]
     late, *early = lax.optimization_barrier((late, *early))
-    late = late.reshape(half, samp)
+    late = late.reshape(quarter, samp)
 
     scale = 1.0 / math.sqrt(samp * n_all)
     first_piece = n_wide * 11 // 16
-    pieces = gather(half, groups, wide_bits, first_piece, scale, even, odd, late, early)
+    pieces = gather(half + quarter, groups, wide_bits, first_piece, scale, even, odd, late, early)
     order = [(p + first_piece) % n_wide for p in range(n_wide)]
     teams = [[w * n_narrow + (n ^ parity(w)) for w in order] for n in range(n_narrow)]
     pieces = lax.all_to_all(pieces, AXES, 0, 0, axis_index_groups=teams, tiled=True)

time: 27.3 us -> 27.1 us (level)
  waiting for transfers between devices: 3.32 us -> 1.58 us
  starting transfers between devices: 7.94 us -> 9.49 us
    ppermute x5 -> x6, waiting for transfers between devices: 3.32 us -> 1.58 us  [across(): return lax.ppermute(values, AXES, [(i, i ^ mask) for i in range(n_all)])]
    ppermute x5 -> x6, starting transfers between devices: 7.94 us -> 9.49 us  [across(): return lax.ppermute(values, AXES, [(i, i ^ mask) for i in range(n_all)])]
    pallas_call x1, Pallas kernels: 0.74 us -> 1.84 us  [gather_early(): pl.pallas_call(functools.partial(early_kernel, firsts, groups), out_shape...]
    pallas_call x1, Pallas kernels: 1.21 us -> 0.47 us  [mix(): pl.pallas_call(mix_kernel, out_shape=[jax.ShapeDtypeStruct((rows, 2 * low...]
    pallas_call x1, Pallas kernels: 1.28 us -> 0.74 us  [gather(): pl.pallas_call(functools.partial(gather_kernel, first, groups, bits, firs...]
  transfers between devices with their start and end apart: 5 -> 6, of which waited for: 3 -> 3; matrix products, arithmetic and copies ran while one was open for 0% -> 0% of each run, Pallas kernels for 15% -> 17%
where the time goes in v6:
time: 27.1 us; the launch traced here: 27 us
  blocking collectives  9.88 us (36%)
  starting transfers between devices  9.49 us (35%)
  Pallas kernels  5.28 us (19%)
  waiting for transfers between devices  1.58 us (6%)
  other arithmetic  0.62 us (2%)
    all_to_all x1, blocking collectives, per_device(): lax.all_to_all(pieces, AXES, 0, 0, axis_index_groups=teams, tiled=True)  9.88 us
    ppermute x6, starting transfers between devices, across(): return lax.ppermute(values, AXES, [(i, i ^ mask) for i in range(n_all)])  9.49 us
    pallas_call x1, Pallas kernels, transform(): pl.pallas_call(functools.partial(transform_kernel, outer, inner), out_sha...  2.23 us
    pallas_call x1, Pallas kernels, gather_early(): pl.pallas_call(functools.partial(early_kernel, firsts, groups), out_shape...  1.84 us
    ppermute x6, waiting for transfers between devices, across(): return lax.ppermute(values, AXES, [(i, i ^ mask) for i in range(n_all)])  1.58 us
    pallas_call x1, Pallas kernels, gather(): pl.pallas_call(functools.partial(gather_kernel, first, groups, bits, firs...  0.74 us
    reduce_sum x1, other arithmetic, per_device(): return jnp.sum(pieces, axis=0)  0.61 us
  transfers between devices with their start and end apart: 6, of which 3 were waited for; matrix products, arithmetic and copies ran while one was open for 0% of the time, Pallas kernels for 17%

profile of v6, /device:TPU:0, one launch (start us, length us, event | category | flops | bytes accessed | tf_op | source)
XLA Modules:
  0.0 27.0 jit_solution(7219098998173955538)
XLA Ops:
  0.0 0.0 copy-start
  0.0 3.5 %collective-permute-start = (s32[128]{0:T(128)}, s32[128]{0:T(128)S(1)}, u32[]{:S(2)}, u32[]{:S(2)}) collective-permute-start(s32[128]{0:T(128)} %samples_ref.1), channel_id=1, source_target_pairs={{0,17},{1,16},{2,19},{3,18},{4,21},{5,20},{6,23},{7,22},{8,25},{9,... | collective-permute-start | bytes 1544 | tf_op jit(solution)/shard_map/ppermute | solution.py:268
  3.5 0.0 copy-done
  3.5 2.2 %transform.1 = (f32[1024,256]{1,0:T(8,128)S(1)}, s32[128]{0:T(128)S(1)}) custom-call(f32[8,32768]{1,0:T(8,128)} %values_hbm.1, s32[256,128]{1,0:T(8,128)} %bitcast.9, s32[128]{0:T(128)S(1)} %copy-done), custom_call_target="tpu_custom_call" | custom-call | flops 268435456 | bytes 2621440 | tf_op jit(solution)/shard_map/transform/pallas_call | solution.py:131
  5.7 0.0 collective-permute-done
  5.7 0.7 %collective-permute-start.2 = (f32[1024,256]{1,0:T(8,128)S(1)}, f32[1024,256]{1,0:T(8,128)S(1)}, u32[]{:S(2)}, u32[]{:S(2)}) collective-permute-start(f32[1024,256]{1,0:T(8,128)S(1)} %get-tuple-element.22.mine_ref), channel_id=1, source_target_pairs={{0,1},{1,0},{2,3},{3,2},{4,5},{5,4},{6,7},{7,6},{8,9},{9,8},{10,11... | collective-permute-start | bytes 3145736 | tf_op jit(solution)/shard_map/ppermute | solution.py:268
  6.5 1.3 %collective-permute-start.1 = (s32[256]{0:T(256)S(1)}, s32[256]{0:T(256)S(1)}, u32[]{:S(2)}, u32[]{:S(2)}) collective-permute-start(s32[256]{0:T(256)S(1)} %constant_dynamic-update-slice_fusion.2), channel_id=1, source_target_pairs={{0,9},{1,8},{2,11},{3,10},{4,13},{5,12},{6,15},{7,14},{8,1},{9,0},... | collective-permute-start | bytes 3080 | tf_op jit(solution)/shard_map/ppermute | solution.py:268
  7.8 1.0 %collective-permute-done.2.other_ref = f32[1024,256]{1,0:T(8,128)S(1)} collective-permute-done((f32[1024,256]{1,0:T(8,128)S(1)}, f32[1024,256]{1,0:T(8,128)S(1)}, u32[]{:S(2)}, u32[]{:S(2)}) %collective-permute-start.2) | collective-permute-done | bytes 1048608 | tf_op jit(solution)/shard_map/ppermute | solution.py:268
  8.8 0.5 %mix.1 = (bf16[1024,512]{1,0:T(8,128)(2,1)S(1)}, bf16[1024,512]{1,0:T(8,128)(2,1)S(1)}) custom-call(f32[1024,256]{1,0:T(8,128)S(1)} %get-tuple-element.22.mine_ref, f32[1024,256]{1,0:T(8,128)S(1)} %collective-permute-done.2.other_ref), custom_call_target="tpu_custom_call" | custom-call | flops 2097152 | bytes 4194304 | tf_op jit(solution)/shard_map/mix/pallas_call | solution.py:164
  9.2 0.3 %collective-permute-done.1 = s32[256]{0:T(256)S(1)} collective-permute-done((s32[256]{0:T(256)S(1)}, s32[256]{0:T(256)S(1)}, u32[]{:S(2)}, u32[]{:S(2)}) %collective-permute-start.1) | collective-permute-done | bytes 1056 | tf_op jit(solution)/shard_map/ppermute | solution.py:268
  9.6 1.3 %collective-permute-start.3 = (s32[512]{0:T(512)S(1)}, s32[512]{0:T(512)S(1)}, u32[]{:S(2)}, u32[]{:S(2)}) collective-permute-start(s32[512]{0:T(512)S(1)} %constant_dynamic-update-slice_fusion.3), channel_id=1, source_target_pairs={{0,5},{1,4},{2,7},{3,6},{4,1},{5,0},{6,3},{7,2},{8,13},{9,12},{10,... | collective-permute-start | bytes 6152 | tf_op jit(solution)/shard_map/ppermute | solution.py:268
  10.9 1.5 %collective-permute-start.5 = (s32[512]{0:T(512)S(1)}, s32[512]{0:T(512)S(1)}, u32[]{:S(2)}, u32[]{:S(2)}) collective-permute-start(s32[512]{0:T(512)S(1)} %constant_dynamic-update-slice_fusion.3), channel_id=1, source_target_pairs={{0,3},{1,2},{2,1},{3,0},{4,7},{5,6},{6,5},{7,4},{8,11},{9,10},{10,... | collective-permute-start | bytes 6152 | tf_op jit(solution)/shard_map/ppermute | solution.py:268
  12.4 0.2 collective-permute-done.3
  12.6 1.2 %collective-permute-start.4 = (s32[512]{0:T(512)S(1)}, s32[512]{0:T(512)S(1)}, u32[]{:S(2)}, u32[]{:S(2)}) collective-permute-start(s32[512]{0:T(512)S(1)} %collective-permute-done.3), channel_id=1, source_target_pairs={{0,3},{1,2},{2,1},{3,0},{4,7},{5,6},{6,5},{7,4},{8,11},{9,10},{10,... | collective-permute-start | bytes 6152 | tf_op jit(solution)/shard_map/ppermute | solution.py:268
  13.8 0.0 collective-permute-done.5
  13.9 1.8 %gather_early.1.refs_0_ = f32[12,8,128]{2,1,0:T(8,128)S(1)} custom-call(bf16[1024,512]{1,0:T(8,128)(2,1)S(1)} %get-tuple-element.25.even_ref, bf16[1024,512]{1,0:T(8,128)(2,1)S(1)} %get-tuple-element.26.odd_ref, s32[4,128]{1,0:T(4,128)S(1)} %pad_add_fusion.refs_0_, s32[4,128]{1,0:T(4,128)S(1)} %bitcast.7, s32[4,128]{1,0:T(4,128)S(1)} %bitcast.8), custom_call_target="tpu_custom_call" | custom-call | flops 1610612736 | bytes 1048576 | tf_op jit(solution)/shard_map/gather_early/pallas_call | solution.py:231
  15.7 0.0 collective-permute-done.4
  15.7 0.7 %gather.1 = f32[16,8,128]{2,1,0:T(8,128)S(1)} custom-call(bf16[1024,512]{1,0:T(8,128)(2,1)S(1)} %get-tuple-element.25.even_ref, bf16[1024,512]{1,0:T(8,128)(2,1)S(1)} %get-tuple-element.26.odd_ref, s32[4,128]{1,0:T(4,128)S(1)} %bitcast.6, f32[12,8,128]{2,1,0:T(8,128)S(1)} %gather_early.1.refs_0_), custom_call_target="tpu_custom_call" | custom-call | flops 536870912 | bytes 1048576 | tf_op jit(solution)/shard_map/gather/pallas_call | solution.py:245
  16.5 9.9 %all_to_all.5 = f32[16,8,128]{2,1,0:T(8,128)S(1)} all-to-all(f32[16,8,128]{2,1,0:T(8,128)S(1)} %gather.1), channel_id=1, replica_groups={{23,24,27,29,30,0,3,5,6,9,10,12,15,17,18,20},{22,25,26,28,31,1,2,4,7,8,..., dimensions={0} | all-to-all | bytes 131072 | tf_op jit(solution)/shard_map/all_to_all | solution.py:310
  26.4 0.6 %reduce_sum.9 = f32[8,128]{1,0:T(8,128)} reduce(f32[16,8,128]{2,1,0:T(8,128)S(1)} %all_to_all.5, f32[]{:T(128)} %constant.0.clone.1), dimensions={0}, to_apply=%region_0.0 | reduce | flops 15360 | bytes 69636 | tf_op jit(solution)/shard_map/reduce_sum | solution.py:311
  (7 shorter events, 0.1 us)
Async XLA Ops:
  0.0 3.5 %copy-start = (s32[128]{0:T(128)S(1)}, s32[128]{0:T(128)}, u32[]{:S(2)}) copy-start(s32[128]{0:T(128)} %samples_ref.1) | copy-start | bytes 1540
  0.0 5.7 %collective-permute-start = (s32[128]{0:T(128)}, s32[128]{0:T(128)S(1)}, u32[]{:S(2)}, u32[]{:S(2)}) collective-permute-start(s32[128]{0:T(128)} %samples_ref.1), channel_id=1, source_target_pairs={{0,17},{1,16},{2,19},{3,18},{4,21},{5,20},{6,23},{7,22},{8,25},{9,... | collective-permute-start | bytes 1544 | tf_op jit(solution)/shard_map/ppermute | solution.py:268
  5.7 3.0 %collective-permute-start.2 = (f32[1024,256]{1,0:T(8,128)S(1)}, f32[1024,256]{1,0:T(8,128)S(1)}, u32[]{:S(2)}, u32[]{:S(2)}) collective-permute-start(f32[1024,256]{1,0:T(8,128)S(1)} %get-tuple-element.22.mine_ref), channel_id=1, source_target_pairs={{0,1},{1,0},{2,3},{3,2},{4,5},{5,4},{6,7},{7,6},{8,9},{9,8},{10,11... | collective-permute-start | bytes 3145736 | tf_op jit(solution)/shard_map/ppermute | solution.py:268
  6.5 3.0 %collective-permute-start.1 = (s32[256]{0:T(256)S(1)}, s32[256]{0:T(256)S(1)}, u32[]{:S(2)}, u32[]{:S(2)}) collective-permute-start(s32[256]{0:T(256)S(1)} %constant_dynamic-update-slice_fusion.2), channel_id=1, source_target_pairs={{0,9},{1,8},{2,11},{3,10},{4,13},{5,12},{6,15},{7,14},{8,1},{9,0},... | collective-permute-start | bytes 3080 | tf_op jit(solution)/shard_map/ppermute | solution.py:268
  9.6 3.1 %collective-permute-start.3 = (s32[512]{0:T(512)S(1)}, s32[512]{0:T(512)S(1)}, u32[]{:S(2)}, u32[]{:S(2)}) collective-permute-start(s32[512]{0:T(512)S(1)} %constant_dynamic-update-slice_fusion.3), channel_id=1, source_target_pairs={{0,5},{1,4},{2,7},{3,6},{4,1},{5,0},{6,3},{7,2},{8,13},{9,12},{10,... | collective-permute-start | bytes 6152 | tf_op jit(solution)/shard_map/ppermute | solution.py:268
  10.9 3.0 %collective-permute-start.5 = (s32[512]{0:T(512)S(1)}, s32[512]{0:T(512)S(1)}, u32[]{:S(2)}, u32[]{:S(2)}) collective-permute-start(s32[512]{0:T(512)S(1)} %constant_dynamic-update-slice_fusion.3), channel_id=1, source_target_pairs={{0,3},{1,2},{2,1},{3,0},{4,7},{5,6},{6,5},{7,4},{8,11},{9,10},{10,... | collective-permute-start | bytes 6152 | tf_op jit(solution)/shard_map/ppermute | solution.py:268
  12.6 3.1 %collective-permute-start.4 = (s32[512]{0:T(512)S(1)}, s32[512]{0:T(512)S(1)}, u32[]{:S(2)}, u32[]{:S(2)}) collective-permute-start(s32[512]{0:T(512)S(1)} %collective-permute-done.3), channel_id=1, source_target_pairs={{0,3},{1,2},{2,1},{3,0},{4,7},{5,6},{6,5},{7,4},{8,11},{9,10},{10,... | collective-permute-start | bytes 6152 | tf_op jit(solution)/shard_map/ppermute | solution.py:268

commit v7 on v6

--- a/solution.py
+++ b/solution.py
@@ -196,62 +196,52 @@
                 out_ref[at_row + t] = total[:, i * samp : (i + 1) * samp]
 
 
-def early_kernel(firsts, groups, even_ref, odd_ref, *refs):
-    *offset_refs, out_ref = refs
-    at_row = 0
-    for first, offsets_ref in zip(firsts, offset_refs):
-        pick(first, groups, out_ref.shape[1], (even_ref, odd_ref), offsets_ref[...], out_ref, at_row)
-        at_row += offsets_ref.shape[0]
-
-
-def gather_kernel(first, groups, bits, first_piece, scale, even_ref, odd_ref, offsets_ref, *refs):
-    *known_refs, out_ref, late_ref = refs
-    cols = out_ref.shape[1]
+def place(values_ref, first, start, bits, first_piece, scale, out_ref):
     me = lax.axis_index("wide")
-
-    def place(place_of, value):
-        target = me ^ place_of
+    for t in range(values_ref.shape[0] if start is None else start[1]):
+        at = t if start is None else start[0] + t
+        target = me ^ ladder_place(first + t, bits)
         common = target & me
         odd = common & 1
         for bit in range(1, bits):
             odd = odd ^ (common >> bit & 1)
-        out_ref[target - first_piece & (1 << bits) - 1] = value * ((1 - 2 * odd).astype(jnp.float32) * scale)
-
-    pick(first, groups, cols, (even_ref, odd_ref), offsets_ref[...], late_ref, 0)
-    at_place = 0
-    for ref in (*known_refs, late_ref):
-        for t in range(ref.shape[0]):
-            place(ladder_place(at_place, bits), ref[t])
-            at_place += 1
-
-
-def gather_early(firsts, groups, even, odd, lists):
+        sign = (1 - 2 * odd).astype(jnp.float32) * scale
+        out_ref[target - first_piece & (1 << bits) - 1] = values_ref[at] * sign
+
+
+def early_kernel(firsts, groups, bits, first_piece, scale, even_ref, odd_ref, *refs):
+    *offset_refs, out_ref, picked_ref = refs
+    at_row = 0
+    for first, offsets_ref in zip(firsts, offset_refs):
+        count = offsets_ref.shape[0]
+        pick(first, groups, out_ref.shape[1], (even_ref, odd_ref), offsets_ref[...], picked_ref, at_row)
+        place(picked_ref, first, (at_row, count), bits, first_piece, scale, out_ref)
+        at_row += count
+
+
+def late_kernel(first, groups, bits, first_piece, scale, even_ref, odd_ref, offsets_ref, known_ref, out_ref, picked_ref):
+    pick(first, groups, out_ref.shape[1], (even_ref, odd_ref), offsets_ref[...], picked_ref, 0)
+    place(picked_ref, first, None, bits, first_piece, scale, out_ref)
+
+
+def gather(firsts, groups, bits, first_piece, scale, even, odd, lists, known=None):
     count, samp = sum(offsets.shape[0] for offsets in lists), lists[0].shape[1]
     cols = even.shape[0] // groups
+    if known is None:
+        kernel, extra, aliases = functools.partial(early_kernel, firsts), (), {}
+    else:
+        kernel, extra, aliases = functools.partial(late_kernel, *firsts), (known,), {3: 0}
     return pl.pallas_call(
-        functools.partial(early_kernel, firsts, groups),
-        out_shape=jax.ShapeDtypeStruct((count, cols, samp), jnp.float32),
-        in_specs=[vmem()] * (2 + len(lists)),
-        out_specs=vmem(),
-        compiler_params=pltpu.CompilerParams(vmem_limit_bytes=VMEM_LIMIT),
-        cost_estimate=gather_cost(groups, cols, count, samp),
-        name="gather_early",
-    )(even, odd, *lists)
-
-
-def gather(first, groups, bits, first_piece, scale, even, odd, offsets, known):
-    count, samp = offsets.shape
-    cols = even.shape[0] // groups
-    return pl.pallas_call(
-        functools.partial(gather_kernel, first, groups, bits, first_piece, scale),
-        out_shape=jax.ShapeDtypeStruct((first + count, cols, samp), jnp.float32),
-        in_specs=[vmem()] * (3 + len(known)),
+        functools.partial(kernel, groups, bits, first_piece, scale),
+        out_shape=jax.ShapeDtypeStruct((1 << bits, cols, samp), jnp.float32),
+        in_specs=[vmem()] * (2 + len(lists) + len(extra)),
         out_specs=vmem(),
         scratch_shapes=[pltpu.VMEM((count, cols, samp), jnp.float32)],
+        input_output_aliases=aliases,
         compiler_params=pltpu.CompilerParams(vmem_limit_bytes=VMEM_LIMIT),
         cost_estimate=gather_cost(groups, cols, count, samp),
         name="gather",
-    )(even, odd, offsets, *known)
+    )(even, odd, *lists, *extra)
 
 
 def per_device(panel, signs, samples):
@@ -279,6 +269,9 @@
     half, quarter = n_wide // 2, n_wide // 4
     ladder = list(reversed(range(wide_bits)))
     last = wide_bits - 1
+    scale = 1.0 / math.sqrt(samp * n_all)
+    first_piece = n_wide * 11 // 16
+    plan = (groups, wide_bits, first_piece, scale)
 
     def exchange(values, i):
         return across(values, n_narrow << ladder[i] | 1)
@@ -298,13 +291,11 @@
     ahead = exchange(asked, last)
     late = exchange(arrived, last)
     lists = [asked.reshape(quarter, samp), arrived.reshape(quarter, samp), ahead.reshape(quarter, samp)]
-    early = [gather_early((0, quarter, half), groups, even, odd, lists)]
-    late, *early = lax.optimization_barrier((late, *early))
+    early = gather((0, quarter, half), *plan, even, odd, lists)
+    late, early = lax.optimization_barrier((late, early))
     late = late.reshape(quarter, samp)
 
-    scale = 1.0 / math.sqrt(samp * n_all)
-    first_piece = n_wide * 11 // 16
-    pieces = gather(half + quarter, groups, wide_bits, first_piece, scale, even, odd, late, early)
+    pieces = gather((half + quarter,), *plan, even, odd, [late], early)
     order = [(p + first_piece) % n_wide for p in range(n_wide)]
     teams = [[w * n_narrow + (n ^ parity(w)) for w in order] for n in range(n_narrow)]
     pieces = lax.all_to_all(pieces, AXES, 0, 0, axis_index_groups=teams, tiled=True)

time: 27.1 us -> 27.1 us (level)
  no operation moved by 1% of the time
where the time goes in v7:
time: 27.1 us; the launch traced here: 27 us
  blocking collectives  9.88 us (36%)
  starting transfers between devices  9.49 us (35%)
  Pallas kernels  5.28 us (19%)
  waiting for transfers between devices  1.58 us (6%)
  other arithmetic  0.62 us (2%)
    all_to_all x1, blocking collectives, per_device(): lax.all_to_all(pieces, AXES, 0, 0, axis_index_groups=teams, tiled=True)  9.88 us
    ppermute x6, starting transfers between devices, across(): return lax.ppermute(values, AXES, [(i, i ^ mask) for i in range(n_all)])  9.49 us
    pallas_call x2, Pallas kernels, gather(): pl.pallas_call(functools.partial(kernel, groups, bits, first_piece, scale...  2.58 us
    pallas_call x1, Pallas kernels, transform(): pl.pallas_call(functools.partial(transform_kernel, outer, inner), out_sha...  2.23 us
    ppermute x6, waiting for transfers between devices, across(): return lax.ppermute(values, AXES, [(i, i ^ mask) for i in range(n_all)])  1.58 us
    reduce_sum x1, other arithmetic, per_device(): return jnp.sum(pieces, axis=0)  0.61 us
  transfers between devices with their start and end apart: 6, of which 3 were waited for; matrix products, arithmetic and copies ran while one was open for 0% of the time, Pallas kernels for 17%

profile of v7, /device:TPU:0, one launch (start us, length us, event | category | flops | bytes accessed | tf_op | source)
XLA Modules:
  0.0 27.0 jit_solution(9536272288409918204)
XLA Ops:
  0.0 0.0 copy-start
  0.0 3.5 %collective-permute-start = (s32[128]{0:T(128)}, s32[128]{0:T(128)S(1)}, u32[]{:S(2)}, u32[]{:S(2)}) collective-permute-start(s32[128]{0:T(128)} %samples_ref.1), channel_id=1, source_target_pairs={{0,17},{1,16},{2,19},{3,18},{4,21},{5,20},{6,23},{7,22},{8,25},{9,... | collective-permute-start | bytes 1544 | tf_op jit(solution)/shard_map/ppermute | solution.py:258
  3.5 0.0 copy-done
  3.5 2.2 %transform.1 = (f32[1024,256]{1,0:T(8,128)S(1)}, s32[128]{0:T(128)S(1)}) custom-call(f32[8,32768]{1,0:T(8,128)} %values_hbm.1, s32[256,128]{1,0:T(8,128)} %bitcast.9, s32[128]{0:T(128)S(1)} %copy-done), custom_call_target="tpu_custom_call" | custom-call | flops 268435456 | bytes 2621440 | tf_op jit(solution)/shard_map/transform/pallas_call | solution.py:131
  5.7 0.0 collective-permute-done
  5.7 0.7 %collective-permute-start.2 = (f32[1024,256]{1,0:T(8,128)S(1)}, f32[1024,256]{1,0:T(8,128)S(1)}, u32[]{:S(2)}, u32[]{:S(2)}) collective-permute-start(f32[1024,256]{1,0:T(8,128)S(1)} %get-tuple-element.22.mine_ref), channel_id=1, source_target_pairs={{0,1},{1,0},{2,3},{3,2},{4,5},{5,4},{6,7},{7,6},{8,9},{9,8},{10,11... | collective-permute-start | bytes 3145736 | tf_op jit(solution)/shard_map/ppermute | solution.py:258
  6.5 1.3 %collective-permute-start.1 = (s32[256]{0:T(256)S(1)}, s32[256]{0:T(256)S(1)}, u32[]{:S(2)}, u32[]{:S(2)}) collective-permute-start(s32[256]{0:T(256)S(1)} %constant_dynamic-update-slice_fusion.2), channel_id=1, source_target_pairs={{0,9},{1,8},{2,11},{3,10},{4,13},{5,12},{6,15},{7,14},{8,1},{9,0},... | collective-permute-start | bytes 3080 | tf_op jit(solution)/shard_map/ppermute | solution.py:258
  7.8 1.0 %collective-permute-done.2.other_ref = f32[1024,256]{1,0:T(8,128)S(1)} collective-permute-done((f32[1024,256]{1,0:T(8,128)S(1)}, f32[1024,256]{1,0:T(8,128)S(1)}, u32[]{:S(2)}, u32[]{:S(2)}) %collective-permute-start.2) | collective-permute-done | bytes 1048608 | tf_op jit(solution)/shard_map/ppermute | solution.py:258
  8.8 0.5 %mix.1 = (bf16[1024,512]{1,0:T(8,128)(2,1)S(1)}, bf16[1024,512]{1,0:T(8,128)(2,1)S(1)}) custom-call(f32[1024,256]{1,0:T(8,128)S(1)} %get-tuple-element.22.mine_ref, f32[1024,256]{1,0:T(8,128)S(1)} %collective-permute-done.2.other_ref), custom_call_target="tpu_custom_call" | custom-call | flops 2097152 | bytes 4194304 | tf_op jit(solution)/shard_map/mix/pallas_call | solution.py:164
  9.2 0.3 %collective-permute-done.1 = s32[256]{0:T(256)S(1)} collective-permute-done((s32[256]{0:T(256)S(1)}, s32[256]{0:T(256)S(1)}, u32[]{:S(2)}, u32[]{:S(2)}) %collective-permute-start.1) | collective-permute-done | bytes 1056 | tf_op jit(solution)/shard_map/ppermute | solution.py:258
  9.6 1.3 %collective-permute-start.3 = (s32[512]{0:T(512)S(1)}, s32[512]{0:T(512)S(1)}, u32[]{:S(2)}, u32[]{:S(2)}) collective-permute-start(s32[512]{0:T(512)S(1)} %constant_dynamic-update-slice_fusion.3), channel_id=1, source_target_pairs={{0,5},{1,4},{2,7},{3,6},{4,1},{5,0},{6,3},{7,2},{8,13},{9,12},{10,... | collective-permute-start | bytes 6152 | tf_op jit(solution)/shard_map/ppermute | solution.py:258
  10.9 1.5 %collective-permute-start.5 = (s32[512]{0:T(512)S(1)}, s32[512]{0:T(512)S(1)}, u32[]{:S(2)}, u32[]{:S(2)}) collective-permute-start(s32[512]{0:T(512)S(1)} %constant_dynamic-update-slice_fusion.3), channel_id=1, source_target_pairs={{0,3},{1,2},{2,1},{3,0},{4,7},{5,6},{6,5},{7,4},{8,11},{9,10},{10,... | collective-permute-start | bytes 6152 | tf_op jit(solution)/shard_map/ppermute | solution.py:258
  12.4 0.2 collective-permute-done.3
  12.6 1.2 %collective-permute-start.4 = (s32[512]{0:T(512)S(1)}, s32[512]{0:T(512)S(1)}, u32[]{:S(2)}, u32[]{:S(2)}) collective-permute-start(s32[512]{0:T(512)S(1)} %collective-permute-done.3), channel_id=1, source_target_pairs={{0,3},{1,2},{2,1},{3,0},{4,7},{5,6},{6,5},{7,4},{8,11},{9,10},{10,... | collective-permute-start | bytes 6152 | tf_op jit(solution)/shard_map/ppermute | solution.py:258
  13.8 0.0 collective-permute-done.5
  13.9 1.8 %gather.2.known_ref = f32[16,8,128]{2,1,0:T(8,128)S(1)} custom-call(bf16[1024,512]{1,0:T(8,128)(2,1)S(1)} %get-tuple-element.25.even_ref, bf16[1024,512]{1,0:T(8,128)(2,1)S(1)} %get-tuple-element.26.odd_ref, s32[4,128]{1,0:T(4,128)S(1)} %pad_add_fusion.refs_0_, s32[4,128]{1,0:T(4,128)S(1)} %bitcast.7, s32[4,128]{1,0:T(4,128)S(1)} %bitcast.8), custom_call_target="tpu_custom_call" | custom-call | flops 1610612736 | bytes 1048576 | tf_op jit(solution)/shard_map/gather/pallas_call | solution.py:234
  15.7 0.0 collective-permute-done.4
  15.7 0.7 %gather.3 = f32[16,8,128]{2,1,0:T(8,128)S(1)} custom-call(bf16[1024,512]{1,0:T(8,128)(2,1)S(1)} %get-tuple-element.25.even_ref, bf16[1024,512]{1,0:T(8,128)(2,1)S(1)} %get-tuple-element.26.odd_ref, s32[4,128]{1,0:T(4,128)S(1)} %bitcast.6, f32[16,8,128]{2,1,0:T(8,128)S(1)} %gather.2.known_ref), custom_call_target="tpu_custom_call", output_to_operand_aliasing={{}: (3, {})} | custom-call | flops 536870912 | bytes 1048576 | tf_op jit(solution)/shard_map/gather/pallas_call | solution.py:234
  16.5 9.9 %all_to_all.5 = f32[16,8,128]{2,1,0:T(8,128)S(1)} all-to-all(f32[16,8,128]{2,1,0:T(8,128)S(1)} %gather.3), channel_id=1, replica_groups={{23,24,27,29,30,0,3,5,6,9,10,12,15,17,18,20},{22,25,26,28,31,1,2,4,7,8,..., dimensions={0} | all-to-all | bytes 131072 | tf_op jit(solution)/shard_map/all_to_all | solution.py:301
  26.4 0.6 %reduce_sum.9 = f32[8,128]{1,0:T(8,128)} reduce(f32[16,8,128]{2,1,0:T(8,128)S(1)} %all_to_all.5, f32[]{:T(128)} %constant.0.clone.1), dimensions={0}, to_apply=%region_0.0 | reduce | flops 15360 | bytes 69636 | tf_op jit(solution)/shard_map/reduce_sum | solution.py:302
  (7 shorter events, 0.1 us)
Async XLA Ops:
  0.0 3.5 %copy-start = (s32[128]{0:T(128)S(1)}, s32[128]{0:T(128)}, u32[]{:S(2)}) copy-start(s32[128]{0:T(128)} %samples_ref.1) | copy-start | bytes 1540
  0.0 5.7 %collective-permute-start = (s32[128]{0:T(128)}, s32[128]{0:T(128)S(1)}, u32[]{:S(2)}, u32[]{:S(2)}) collective-permute-start(s32[128]{0:T(128)} %samples_ref.1), channel_id=1, source_target_pairs={{0,17},{1,16},{2,19},{3,18},{4,21},{5,20},{6,23},{7,22},{8,25},{9,... | collective-permute-start | bytes 1544 | tf_op jit(solution)/shard_map/ppermute | solution.py:258
  5.7 3.0 %collective-permute-start.2 = (f32[1024,256]{1,0:T(8,128)S(1)}, f32[1024,256]{1,0:T(8,128)S(1)}, u32[]{:S(2)}, u32[]{:S(2)}) collective-permute-start(f32[1024,256]{1,0:T(8,128)S(1)} %get-tuple-element.22.mine_ref), channel_id=1, source_target_pairs={{0,1},{1,0},{2,3},{3,2},{4,5},{5,4},{6,7},{7,6},{8,9},{9,8},{10,11... | collective-permute-start | bytes 3145736 | tf_op jit(solution)/shard_map/ppermute | solution.py:258
  6.5 3.0 %collective-permute-start.1 = (s32[256]{0:T(256)S(1)}, s32[256]{0:T(256)S(1)}, u32[]{:S(2)}, u32[]{:S(2)}) collective-permute-start(s32[256]{0:T(256)S(1)} %constant_dynamic-update-slice_fusion.2), channel_id=1, source_target_pairs={{0,9},{1,8},{2,11},{3,10},{4,13},{5,12},{6,15},{7,14},{8,1},{9,0},... | collective-permute-start | bytes 3080 | tf_op jit(solution)/shard_map/ppermute | solution.py:258
  9.6 3.1 %collective-permute-start.3 = (s32[512]{0:T(512)S(1)}, s32[512]{0:T(512)S(1)}, u32[]{:S(2)}, u32[]{:S(2)}) collective-permute-start(s32[512]{0:T(512)S(1)} %constant_dynamic-update-slice_fusion.3), channel_id=1, source_target_pairs={{0,5},{1,4},{2,7},{3,6},{4,1},{5,0},{6,3},{7,2},{8,13},{9,12},{10,... | collective-permute-start | bytes 6152 | tf_op jit(solution)/shard_map/ppermute | solution.py:258
  10.9 3.0 %collective-permute-start.5 = (s32[512]{0:T(512)S(1)}, s32[512]{0:T(512)S(1)}, u32[]{:S(2)}, u32[]{:S(2)}) collective-permute-start(s32[512]{0:T(512)S(1)} %constant_dynamic-update-slice_fusion.3), channel_id=1, source_target_pairs={{0,3},{1,2},{2,1},{3,0},{4,7},{5,6},{6,5},{7,4},{8,11},{9,10},{10,... | collective-permute-start | bytes 6152 | tf_op jit(solution)/shard_map/ppermute | solution.py:258
  12.6 3.1 %collective-permute-start.4 = (s32[512]{0:T(512)S(1)}, s32[512]{0:T(512)S(1)}, u32[]{:S(2)}, u32[]{:S(2)}) collective-permute-start(s32[512]{0:T(512)S(1)} %collective-permute-done.3), channel_id=1, source_target_pairs={{0,3},{1,2},{2,1},{3,0},{4,7},{5,6},{6,5},{7,4},{8,11},{9,10},{10,... | collective-permute-start | bytes 6152 | tf_op jit(solution)/shard_map/ppermute | solution.py:258

commit v8 on v6

--- a/solution.py
+++ b/solution.py
@@ -209,13 +209,18 @@
     cols = out_ref.shape[1]
     me = lax.axis_index("wide")
 
+    team = lax.axis_index("narrow") & 1
+    for bit in range(bits):
+        team = team ^ (me >> bit & 1)
+    first_of_team = jnp.where(team == 0, first_piece, (1 << bits) - 1)
+
     def place(place_of, value):
         target = me ^ place_of
         common = target & me
         odd = common & 1
         for bit in range(1, bits):
             odd = odd ^ (common >> bit & 1)
-        out_ref[target - first_piece & (1 << bits) - 1] = value * ((1 - 2 * odd).astype(jnp.float32) * scale)
+        out_ref[target - first_of_team & (1 << bits) - 1] = value * ((1 - 2 * odd).astype(jnp.float32) * scale)
 
     pick(first, groups, cols, (even_ref, odd_ref), offsets_ref[...], late_ref, 0)
     at_place = 0
@@ -305,8 +310,11 @@
     scale = 1.0 / math.sqrt(samp * n_all)
     first_piece = n_wide * 11 // 16
     pieces = gather(half + quarter, groups, wide_bits, first_piece, scale, even, odd, late, early)
-    order = [(p + first_piece) % n_wide for p in range(n_wide)]
-    teams = [[w * n_narrow + (n ^ parity(w)) for w in order] for n in range(n_narrow)]
+    firsts = (first_piece, n_wide - 1)
+    teams = [
+        [w * n_narrow + (n ^ parity(w)) for w in ((p + firsts[n & 1]) % n_wide for p in range(n_wide))]
+        for n in range(n_narrow)
+    ]
     pieces = lax.all_to_all(pieces, AXES, 0, 0, axis_index_groups=teams, tiled=True)
     return jnp.sum(pieces, axis=0)
 

time: 27.1 us -> 27 us (level)
  no operation moved by 1% of the time
where the time goes in v8:
time: 27 us; the launch traced here: 26.8 us
  blocking collectives  9.75 us (36%)
  starting transfers between devices  9.49 us (35%)
  Pallas kernels  5.28 us (20%)
  waiting for transfers between devices  1.58 us (6%)
  other arithmetic  0.62 us (2%)
    all_to_all x1, blocking collectives, per_device(): lax.all_to_all(pieces, AXES, 0, 0, axis_index_groups=teams, tiled=True)  9.75 us
    ppermute x6, starting transfers between devices, across(): return lax.ppermute(values, AXES, [(i, i ^ mask) for i in range(n_all)])  9.49 us
    pallas_call x1, Pallas kernels, transform(): pl.pallas_call(functools.partial(transform_kernel, outer, inner), out_sha...  2.23 us
    pallas_call x1, Pallas kernels, gather_early(): pl.pallas_call(functools.partial(early_kernel, firsts, groups), out_shape...  1.84 us
    ppermute x6, waiting for transfers between devices, across(): return lax.ppermute(values, AXES, [(i, i ^ mask) for i in range(n_all)])  1.58 us
    pallas_call x1, Pallas kernels, gather(): pl.pallas_call(functools.partial(gather_kernel, first, groups, bits, firs...  0.74 us
    reduce_sum x1, other arithmetic, per_device(): return jnp.sum(pieces, axis=0)  0.61 us
  transfers between devices with their start and end apart: 6, of which 3 were waited for; matrix products, arithmetic and copies ran while one was open for 0% of the time, Pallas kernels for 17%

profile of v8, /device:TPU:0, one launch (start us, length us, event | category | flops | bytes accessed | tf_op | source)
XLA Modules:
  0.0 26.8 jit_solution(11270847170747957868)
XLA Ops:
  0.0 0.0 copy-start
  0.0 3.5 %collective-permute-start = (s32[128]{0:T(128)}, s32[128]{0:T(128)S(1)}, u32[]{:S(2)}, u32[]{:S(2)}) collective-permute-start(s32[128]{0:T(128)} %samples_ref.1), channel_id=1, source_target_pairs={{0,17},{1,16},{2,19},{3,18},{4,21},{5,20},{6,23},{7,22},{8,25},{9,... | collective-permute-start | bytes 1544 | tf_op jit(solution)/shard_map/ppermute | solution.py:273
  3.5 0.0 copy-done
  3.5 2.2 %transform.1 = (f32[1024,256]{1,0:T(8,128)S(1)}, s32[128]{0:T(128)S(1)}) custom-call(f32[8,32768]{1,0:T(8,128)} %values_hbm.1, s32[256,128]{1,0:T(8,128)} %bitcast.9, s32[128]{0:T(128)S(1)} %copy-done), custom_call_target="tpu_custom_call" | custom-call | flops 268435456 | bytes 2621440 | tf_op jit(solution)/shard_map/transform/pallas_call | solution.py:131
  5.7 0.0 collective-permute-done
  5.7 0.7 %collective-permute-start.2 = (f32[1024,256]{1,0:T(8,128)S(1)}, f32[1024,256]{1,0:T(8,128)S(1)}, u32[]{:S(2)}, u32[]{:S(2)}) collective-permute-start(f32[1024,256]{1,0:T(8,128)S(1)} %get-tuple-element.22.mine_ref), channel_id=1, source_target_pairs={{0,1},{1,0},{2,3},{3,2},{4,5},{5,4},{6,7},{7,6},{8,9},{9,8},{10,11... | collective-permute-start | bytes 3145736 | tf_op jit(solution)/shard_map/ppermute | solution.py:273
  6.5 1.3 %collective-permute-start.1 = (s32[256]{0:T(256)S(1)}, s32[256]{0:T(256)S(1)}, u32[]{:S(2)}, u32[]{:S(2)}) collective-permute-start(s32[256]{0:T(256)S(1)} %constant_dynamic-update-slice_fusion.2), channel_id=1, source_target_pairs={{0,9},{1,8},{2,11},{3,10},{4,13},{5,12},{6,15},{7,14},{8,1},{9,0},... | collective-permute-start | bytes 3080 | tf_op jit(solution)/shard_map/ppermute | solution.py:273
  7.8 1.0 %collective-permute-done.2.other_ref = f32[1024,256]{1,0:T(8,128)S(1)} collective-permute-done((f32[1024,256]{1,0:T(8,128)S(1)}, f32[1024,256]{1,0:T(8,128)S(1)}, u32[]{:S(2)}, u32[]{:S(2)}) %collective-permute-start.2) | collective-permute-done | bytes 1048608 | tf_op jit(solution)/shard_map/ppermute | solution.py:273
  8.8 0.5 %mix.1 = (bf16[1024,512]{1,0:T(8,128)(2,1)S(1)}, bf16[1024,512]{1,0:T(8,128)(2,1)S(1)}) custom-call(f32[1024,256]{1,0:T(8,128)S(1)} %get-tuple-element.22.mine_ref, f32[1024,256]{1,0:T(8,128)S(1)} %collective-permute-done.2.other_ref), custom_call_target="tpu_custom_call" | custom-call | flops 2097152 | bytes 4194304 | tf_op jit(solution)/shard_map/mix/pallas_call | solution.py:164
  9.2 0.3 %collective-permute-done.1 = s32[256]{0:T(256)S(1)} collective-permute-done((s32[256]{0:T(256)S(1)}, s32[256]{0:T(256)S(1)}, u32[]{:S(2)}, u32[]{:S(2)}) %collective-permute-start.1) | collective-permute-done | bytes 1056 | tf_op jit(solution)/shard_map/ppermute | solution.py:273
  9.6 1.3 %collective-permute-start.3 = (s32[512]{0:T(512)S(1)}, s32[512]{0:T(512)S(1)}, u32[]{:S(2)}, u32[]{:S(2)}) collective-permute-start(s32[512]{0:T(512)S(1)} %constant_dynamic-update-slice_fusion.3), channel_id=1, source_target_pairs={{0,5},{1,4},{2,7},{3,6},{4,1},{5,0},{6,3},{7,2},{8,13},{9,12},{10,... | collective-permute-start | bytes 6152 | tf_op jit(solution)/shard_map/ppermute | solution.py:273
  10.9 1.5 %collective-permute-start.5 = (s32[512]{0:T(512)S(1)}, s32[512]{0:T(512)S(1)}, u32[]{:S(2)}, u32[]{:S(2)}) collective-permute-start(s32[512]{0:T(512)S(1)} %constant_dynamic-update-slice_fusion.3), channel_id=1, source_target_pairs={{0,3},{1,2},{2,1},{3,0},{4,7},{5,6},{6,5},{7,4},{8,11},{9,10},{10,... | collective-permute-start | bytes 6152 | tf_op jit(solution)/shard_map/ppermute | solution.py:273
  12.4 0.2 collective-permute-done.3
  12.6 1.2 %collective-permute-start.4 = (s32[512]{0:T(512)S(1)}, s32[512]{0:T(512)S(1)}, u32[]{:S(2)}, u32[]{:S(2)}) collective-permute-start(s32[512]{0:T(512)S(1)} %collective-permute-done.3), channel_id=1, source_target_pairs={{0,3},{1,2},{2,1},{3,0},{4,7},{5,6},{6,5},{7,4},{8,11},{9,10},{10,... | collective-permute-start | bytes 6152 | tf_op jit(solution)/shard_map/ppermute | solution.py:273
  13.8 0.0 collective-permute-done.5
  13.9 1.8 %gather_early.1.refs_0_ = f32[12,8,128]{2,1,0:T(8,128)S(1)} custom-call(bf16[1024,512]{1,0:T(8,128)(2,1)S(1)} %get-tuple-element.25.even_ref, bf16[1024,512]{1,0:T(8,128)(2,1)S(1)} %get-tuple-element.26.odd_ref, s32[4,128]{1,0:T(4,128)S(1)} %pad_add_fusion.refs_0_, s32[4,128]{1,0:T(4,128)S(1)} %bitcast.7, s32[4,128]{1,0:T(4,128)S(1)} %bitcast.8), custom_call_target="tpu_custom_call" | custom-call | flops 1610612736 | bytes 1048576 | tf_op jit(solution)/shard_map/gather_early/pallas_call | solution.py:236
  15.7 0.0 collective-permute-done.4
  15.7 0.7 %gather.1 = f32[16,8,128]{2,1,0:T(8,128)S(1)} custom-call(bf16[1024,512]{1,0:T(8,128)(2,1)S(1)} %get-tuple-element.25.even_ref, bf16[1024,512]{1,0:T(8,128)(2,1)S(1)} %get-tuple-element.26.odd_ref, s32[4,128]{1,0:T(4,128)S(1)} %bitcast.6, f32[12,8,128]{2,1,0:T(8,128)S(1)} %gather_early.1.refs_0_), custom_call_target="tpu_custom_call" | custom-call | flops 536870912 | bytes 1048576 | tf_op jit(solution)/shard_map/gather/pallas_call | solution.py:250
  16.5 9.7 %all_to_all.5 = f32[16,8,128]{2,1,0:T(8,128)S(1)} all-to-all(f32[16,8,128]{2,1,0:T(8,128)S(1)} %gather.1), channel_id=1, replica_groups={{23,24,27,29,30,0,3,5,6,9,10,12,15,17,18,20},{31,1,2,4,7,8,11,13,14,16,..., dimensions={0} | all-to-all | bytes 131072 | tf_op jit(solution)/shard_map/all_to_all | solution.py:318
  26.2 0.6 %reduce_sum.9 = f32[8,128]{1,0:T(8,128)} reduce(f32[16,8,128]{2,1,0:T(8,128)S(1)} %all_to_all.5, f32[]{:T(128)} %constant.0.clone.1), dimensions={0}, to_apply=%region_0.0 | reduce | flops 15360 | bytes 69636 | tf_op jit(solution)/shard_map/reduce_sum | solution.py:319
  (7 shorter events, 0.1 us)
Async XLA Ops:
  0.0 3.5 %copy-start = (s32[128]{0:T(128)S(1)}, s32[128]{0:T(128)}, u32[]{:S(2)}) copy-start(s32[128]{0:T(128)} %samples_ref.1) | copy-start | bytes 1540
  0.0 5.7 %collective-permute-start = (s32[128]{0:T(128)}, s32[128]{0:T(128)S(1)}, u32[]{:S(2)}, u32[]{:S(2)}) collective-permute-start(s32[128]{0:T(128)} %samples_ref.1), channel_id=1, source_target_pairs={{0,17},{1,16},{2,19},{3,18},{4,21},{5,20},{6,23},{7,22},{8,25},{9,... | collective-permute-start | bytes 1544 | tf_op jit(solution)/shard_map/ppermute | solution.py:273
  5.7 3.0 %collective-permute-start.2 = (f32[1024,256]{1,0:T(8,128)S(1)}, f32[1024,256]{1,0:T(8,128)S(1)}, u32[]{:S(2)}, u32[]{:S(2)}) collective-permute-start(f32[1024,256]{1,0:T(8,128)S(1)} %get-tuple-element.22.mine_ref), channel_id=1, source_target_pairs={{0,1},{1,0},{2,3},{3,2},{4,5},{5,4},{6,7},{7,6},{8,9},{9,8},{10,11... | collective-permute-start | bytes 3145736 | tf_op jit(solution)/shard_map/ppermute | solution.py:273
  6.5 3.0 %collective-permute-start.1 = (s32[256]{0:T(256)S(1)}, s32[256]{0:T(256)S(1)}, u32[]{:S(2)}, u32[]{:S(2)}) collective-permute-start(s32[256]{0:T(256)S(1)} %constant_dynamic-update-slice_fusion.2), channel_id=1, source_target_pairs={{0,9},{1,8},{2,11},{3,10},{4,13},{5,12},{6,15},{7,14},{8,1},{9,0},... | collective-permute-start | bytes 3080 | tf_op jit(solution)/shard_map/ppermute | solution.py:273
  9.6 3.1 %collective-permute-start.3 = (s32[512]{0:T(512)S(1)}, s32[512]{0:T(512)S(1)}, u32[]{:S(2)}, u32[]{:S(2)}) collective-permute-start(s32[512]{0:T(512)S(1)} %constant_dynamic-update-slice_fusion.3), channel_id=1, source_target_pairs={{0,5},{1,4},{2,7},{3,6},{4,1},{5,0},{6,3},{7,2},{8,13},{9,12},{10,... | collective-permute-start | bytes 6152 | tf_op jit(solution)/shard_map/ppermute | solution.py:273
  10.9 3.0 %collective-permute-start.5 = (s32[512]{0:T(512)S(1)}, s32[512]{0:T(512)S(1)}, u32[]{:S(2)}, u32[]{:S(2)}) collective-permute-start(s32[512]{0:T(512)S(1)} %constant_dynamic-update-slice_fusion.3), channel_id=1, source_target_pairs={{0,3},{1,2},{2,1},{3,0},{4,7},{5,6},{6,5},{7,4},{8,11},{9,10},{10,... | collective-permute-start | bytes 6152 | tf_op jit(solution)/shard_map/ppermute | solution.py:273
  12.6 3.1 %collective-permute-start.4 = (s32[512]{0:T(512)S(1)}, s32[512]{0:T(512)S(1)}, u32[]{:S(2)}, u32[]{:S(2)}) collective-permute-start(s32[512]{0:T(512)S(1)} %collective-permute-done.3), channel_id=1, source_target_pairs={{0,3},{1,2},{2,1},{3,0},{4,7},{5,6},{6,5},{7,4},{8,11},{9,10},{10,... | collective-permute-start | bytes 6152 | tf_op jit(solution)/shard_map/ppermute | solution.py:273
